TPU v7x, 128 devices: a whole 4x4x4 slice. The times are simulated.
128 devices in a mesh: freq: 8 (over y, x_lo), row: 4 (over z), col: 4 (over x_hi, core).
Axes of the slice: x: 4 (x_hi: 2, x_lo: 2; x = x_hi * 2 + x_lo), y: 4, z: 4, core: 2. Of those that a mesh axis runs over, the one named last changes fastest.
Arguments:
- traces: float32 [512, 1024, 1024], P(('freq', 'row'), None, 'col'), may hold values from -6 to 6
Outputs:
- multiples: float32 [2, 32, 1024, 1024], P(None, 'freq', 'row', 'col')
All inputs are finite; a program needn't handle non-finite values.
Results may differ from a plain program's by a relative error of at most 0.000098.
Values sent between devices are 32-bit elements; how exact they have to be, the bound alone decides.
No kernel may reach another device: no remote copies, remote signals or barrier semaphores. Data moves between devices by JAX's collectives and lax.ppermute only.
A program may use at most 128 MiB of HBM per device.

v0:
```python
import math

import jax
import jax.numpy as jnp
from jax import lax
from jax.sharding import PartitionSpec as P

S = 1024
NT = 512
FG = 4


def local(traces):
    n_freq = lax.axis_size("freq")
    n_row = lax.axis_size("row")
    parts = n_freq * n_row
    width, sources, columns = traces.shape
    block = sources // parts
    ordered = traces.reshape(width, n_row, n_freq, block, columns)
    ordered = jnp.transpose(ordered, (0, 2, 1, 3, 4)).reshape(width, sources, columns)
    device_time_traces = jnp.arange(NT, dtype=jnp.int32)
    shifted_blocks = lax.all_to_all(
        ordered, ("freq", "row"), split_axis=1, concat_axis=0, tiled=True
    )
    band = FG * n_freq
    bins = jnp.arange(band, dtype=jnp.int32) + 1
    phase = device_time_traces[:, None] * bins[None, :] % NT
    angle = phase.astype(jnp.float32) * (2.0 * math.pi / NT)
    scale = 1.0 / math.sqrt(NT)
    cosine_lookup = jnp.cos(angle) * scale
    sine_lookup = -jnp.sin(angle) * scale
    highest_precision = lax.Precision.HIGHEST
    real_part = jnp.einsum(
        "bgd,bw->wgd",
        shifted_blocks,
        cosine_lookup,
        precision=highest_precision,
        preferred_element_type=jnp.float32,
    )
    imag_part = jnp.einsum(
        "bgd,bw->wgd",
        shifted_blocks,
        sine_lookup,
        precision=highest_precision,
        preferred_element_type=jnp.float32,
    )
    spectra = jnp.stack([real_part, imag_part])
    owned = lax.all_to_all(spectra, "freq", split_axis=1, concat_axis=2, tiled=True)
    column_full = lax.all_gather(owned, "row", axis=2, tiled=True)
    panel = lax.all_gather(owned, "col", axis=3, tiled=True)
    ar = panel[0]
    ai = panel[1]
    br = column_full[0]
    bi = column_full[1]
    output_real = jnp.einsum(
        "gik,gkj->gij", ar, br, precision=highest_precision, preferred_element_type=jnp.float32
    ) - jnp.einsum(
        "gik,gkj->gij", ai, bi, precision=highest_precision, preferred_element_type=jnp.float32
    )
    out_im = jnp.einsum(
        "gik,gkj->gij", ar, bi, precision=highest_precision, preferred_element_type=jnp.float32
    ) + jnp.einsum(
        "gik,gkj->gij", ai, br, precision=highest_precision, preferred_element_type=jnp.float32
    )
    product = jnp.stack([output_real, out_im])
    return product * (1.0 / math.sqrt(S))


def solution(mesh):
    in_specs = (P(("freq", "row"), None, "col"),)
    out_specs = P(None, "freq", "row", "col")
    return jax.shard_map(local, mesh=mesh, in_specs=in_specs, out_specs=out_specs, check_vma=False)
```

profile of v0, /device:TPU:1, one launch (start us, length us, event | category | flops | bytes accessed | tf_op | source)
XLA Modules:
  0.0 590.6 jit_solution(6075652367779303252)
XLA Ops:
  6.5 6.6 %copy.8 = f32[16,8,4,32,256]{4,3,2,1,0:T(8,128)S(1)} copy(f32[16,8,4,32,256]{4,3,1,2,0:T(8,128)} %bitcast.65) | data formatting | bytes 33554432 | tf_op jit(solution)/shard_map/transpose | solution.py:20
  13.1 22.8 %copy.9 = f32[16,1024,256]{2,0,1:T(8,128)} copy(f32[16,1024,256]{2,1,0:T(8,128)S(1)} %bitcast.62) | data formatting | bytes 33554432 | tf_op jit(solution)/shard_map/reshape | solution.py:20
  36.0 9.9 %all-to-all-start = ((f32[16,1024,256]{2,0,1:T(8,128)}), f32[16,1024,256]{2,0,1:T(8,128)}, u32[]{:S(2)}, u32[]{:S(2)}) async-start(f32[16,1024,256]{2,0,1:T(8,128)} %copy.9), calls=%async_computation | async-start | bytes 33554432 | tf_op jit(solution)/shard_map/all_to_all | solution.py:22
  45.9 0.0 all-gather.3.cloned.1.call-start
  46.0 293.5 %all-to-all-done = f32[16,1024,256]{2,0,1:T(8,128)} async-done(((f32[16,1024,256]{2,0,1:T(8,128)}), f32[16,1024,256]{2,0,1:T(8,128)}, u32[]{:S(2)}, u32[]{:S(2)}) %all-to-all-start) | async-done | bytes 16777248 | tf_op jit(solution)/shard_map/all_to_all | solution.py:22
  339.5 7.0 %copy.11 = f32[32,16,32,256]{3,1,0,2:T(8,128)S(1)} copy(f32[32,16,32,256]{3,1,2,0:T(8,128)} %bitcast.6) | data formatting | bytes 33554432 | tf_op jit(solution)/shard_map/all_to_all | solution.py:22
  346.5 10.0 %convolution_bitcast_fusion = f32[1,32,32,256]{3,1,2,0:T(8,128)S(1)} fusion(f32[512,32,256]{2,0,1:T(8,128)S(1)} %bitcast.60, s32[32]{0:T(128)S(1)} %iota_add_fusion), kind=kOutput, calls=%fused_computation.14 | convolution fusion | flops 1610874880 | bytes 17825920 | tf_op jit(solution)/shard_map/bgd,bw->wgd/dot_general | solution.py:40
  356.6 10.1 %convolution_bitcast_fusion.1 = f32[1,32,32,256]{3,1,2,0:T(8,128)S(1)} fusion(f32[512,32,256]{2,0,1:T(8,128)S(1)} %bitcast.61, s32[32]{0:T(128)S(1)} %iota_add_fusion), kind=kOutput, calls=%fused_computation.15 | convolution fusion | flops 1610858496 | bytes 17825920 | tf_op jit(solution)/shard_map/bgd,bw->wgd/dot_general | solution.py:33
  366.7 0.2 pad_maximum_fusion
  366.9 1.2 copy.12
  368.2 43.9 %all_to_all.36 = f32[2,32,32,256]{3,2,0,1:T(8,128)S(1)} all-to-all(f32[2,32,32,256]{3,2,0,1:T(8,128)S(1)} %copy.12), channel_id=1, replica_groups=mesh['freq'=8,'row'=4,'col'=4] {'freq'}, dimensions={1} | all-to-all | bytes 4194304 | tf_op jit(solution)/shard_map/all_to_all | solution.py:48
  412.1 1.5 copy.13
  413.5 0.0 all-gather.3.cloned.1.call-update
  413.6 0.0 all-gather.5.cloned.1.call-start
  413.6 0.7 all-gather.5.cloned.1.call-update
  414.3 60.8 %all-gather.3.cloned.1.call-done = f32[2,4,256,1024]{3,2,1,0:T(8,128)} async-done(((f32[2,4,256,256]{3,2,1,0:T(8,128)}), f32[2,4,256,1024]{3,2,1,0:T(8,128)}) %all-gather.3.cloned.1.call-update) | async-done | bytes 8388624 | tf_op jit(solution)/shard_map/all_gather | solution.py:50
  475.1 84.0 %all-gather.5.cloned.1.call-done = f32[2,4,1024,256]{3,2,1,0:T(8,128)} async-done(((f32[2,4,256,256]{3,2,1,0:T(8,128)}), f32[2,4,1024,256]{3,2,1,0:T(8,128)}) %all-gather.5.cloned.1.call-update) | async-done | bytes 8388624 | tf_op jit(solution)/shard_map/all_gather | solution.py:49
  559.2 0.0 copy-start
  559.2 0.0 copy-start.1
  559.2 8.2 %fusion.1 = f32[4,256,256]{2,1,0:T(8,128)S(1)} fusion(f32[2,4,256,1024]{3,2,1,0:T(8,128)} %all-gather.3.cloned.1.call-done, f32[2,4,1024,256]{3,2,1,0:T(8,128)} %all-gather.5.cloned.1.call-done), kind=kOutput, calls=%fused_computation.5 | convolution fusion | flops 3221225472 | bytes 9437184 | tf_op jit(solution)/shard_map/gik,gkj->gij/dot_general | solution.py:55
  567.4 0.0 copy-done
  567.4 6.2 %fusion = f32[4,256,256]{2,1,0:T(8,128)S(1)} fusion(f32[2,4,256,1024]{3,2,1,0:T(8,128)S(1)} %copy-done, f32[2,4,1024,256]{3,2,1,0:T(8,128)} %all-gather.5.cloned.1.call-done), kind=kOutput, calls=%fused_computation.4 | convolution fusion | flops 3221225472 | bytes 9437184 | tf_op jit(solution)/shard_map/gik,gkj->gij/dot_general | solution.py:60
  573.6 0.0 copy-done.1
  573.6 4.1 fusion.7
  577.7 4.1 fusion.6
  581.8 1.5 maximum_multiply_fusion
  (1 shorter events, 0.0 us)
Async XLA Ops:
  36.0 303.5 %all-to-all-start = ((f32[16,1024,256]{2,0,1:T(8,128)}), f32[16,1024,256]{2,0,1:T(8,128)}, u32[]{:S(2)}, u32[]{:S(2)}) async-start(f32[16,1024,256]{2,0,1:T(8,128)} %copy.9), calls=%async_computation | async-start | bytes 33554432 | tf_op jit(solution)/shard_map/all_to_all | solution.py:22
  45.9 429.2 %all-gather.3.cloned.1.call-start = ((), (), s32[]{:S(2)}) async-start(), calls=%async_computation.2 | async-start | bytes 10485760 | tf_op jit(solution)/shard_map/all_gather | solution.py:50
  413.6 145.6 %all-gather.5.cloned.1.call-start = ((), (), s32[]{:S(2)}) async-start(), calls=%async_computation.3 | async-start | bytes 10485760 | tf_op jit(solution)/shard_map/all_gather | solution.py:49
  559.2 8.3 %copy-start = (f32[2,4,256,1024]{3,2,1,0:T(8,128)S(1)}, f32[2,4,256,1024]{3,2,1,0:T(8,128)}, u32[]{:S(2)}) copy-start(f32[2,4,256,1024]{3,2,1,0:T(8,128)} %all-gather.3.cloned.1.call-done) | copy-start | bytes 25165828
  559.2 14.4 %copy-start.1 = (f32[2,4,1024,256]{3,2,1,0:T(8,128)S(1)}, f32[2,4,1024,256]{3,2,1,0:T(8,128)}, u32[]{:S(2)}) copy-start(f32[2,4,1024,256]{3,2,1,0:T(8,128)} %all-gather.5.cloned.1.call-done) | copy-start | bytes 25165828
Sparse Core Ops, SparseCore 0:
  413.7 61.3 all-gather.2
  476.8 82.3 all-gather.4
where the time goes:
time: 596 us; the launch traced here: 591 us
  waiting for transfers between devices  439 us (74%)
  blocking collectives  43.9 us (7%)
  matrix products  42.7 us (7%)
  local copies, waits for them, and re-layouts  39.1 us (7%)
  between operations  14 us (2%)
  starting transfers between devices  10 us (2%)
    all_to_all x1, waiting for transfers between devices, local(): lax.all_to_all(ordered, ('freq', 'row'), split_axis=1, concat_axis=0, til...  294 us
    all_gather x1, waiting for transfers between devices, local(): column_full = lax.all_gather(owned, 'row', axis=2, tiled=True)  84 us
    all_gather x1, waiting for transfers between devices, local(): panel = lax.all_gather(owned, 'col', axis=3, tiled=True)  60.8 us
    all_to_all x1, blocking collectives, local(): lax.all_to_all(spectra, 'freq', split_axis=1, concat_axis=2, tiled=True)  43.9 us
    reshape x1, local copies, waits for them, and re-layouts, local(): jnp.transpose(ordered, (0, 2, 1, 3, 4)).reshape(width, sources, columns)  22.8 us
  transfers between devices with their start and end apart: 3, of which 3 were waited for; matrix products, arithmetic and copies ran while one was open for 0% of the time, Pallas kernels for 0%

commit v1 on v0

v1 whole, which is shorter than its diff:
```python
import functools
import math

import jax
import jax.numpy as jnp
import numpy as np
from jax import lax
from jax.experimental import pallas as pl
from jax.experimental.pallas import tpu as pltpu
from jax.sharding import PartitionSpec as P

S = 1024
NT = 512
NF = 32
C = 256
R1, R2, R3 = 96, 64, 96
VMEM = 50 << 20


def shift(x, axis, by=1):
    if axis == "z":
        return lax.ppermute(x, "row", [(i, (i + by) % 4) for i in range(4)])
    if axis == "y":
        return lax.ppermute(x, "freq", [(i, (i + 2 * by) % 8) for i in range(8)])
    if axis == "x_lo":
        return lax.ppermute(x, "freq", [(i, i ^ 1) for i in range(8)])
    if axis == "x_hi":
        return lax.ppermute(x, "col", [(i, i ^ 2) for i in range(4)])
    return lax.ppermute(x, "col", [(i, i ^ 1) for i in range(4)])


def together(*values):
    return lax.optimization_barrier(values)


def tables():
    k = np.arange(NF) + 1
    phase = np.outer(k, np.arange(NT)) % NT * (2.0 * math.pi / NT)
    scale = 1.0 / math.sqrt(NT * math.sqrt(S))
    full = np.stack([np.cos(phase), -np.sin(phase)]) * scale
    full = full.reshape(2, 8, 4, NT).transpose(1, 0, 2, 3).reshape(8, 8, NT).astype(np.float32)
    one, two, three = [], [], []
    u = np.arange(16)
    for f in range(8):
        y, x_lo = f // 2, f % 2
        owner = np.array([[2 * ((y + ry) % 4) + (x_lo + q) % 2 for q in range(2)] for ry in range(4)])
        by_y = full[owner.reshape(-1)].reshape(64, NT)
        by_q = full[owner.T.reshape(-1)].reshape(64, NT)
        near, far = 64 * f + np.arange(64), 64 * (f ^ 1) + np.arange(64)
        one.append(by_y[:, near])
        three.append(by_y[:, np.stack([near.reshape(4, 16), far.reshape(4, 16)], axis=1).reshape(-1)])
        for z in range(4):
            t = [128 * ((y - r) % 4) + 64 * x_lo + 16 * z + u for r in range(4)]
            two.append(by_q[:, np.concatenate(t)])
    return np.stack(one), np.stack(two), np.stack(three)


def cost(us):
    return pl.CostEstimate(flops=0, bytes_accessed=int(us * 3.6e6), transcendentals=0)


def transform(w_ref, samples, store, rows):
    w = w_ref[0]
    wh = w.astype(jnp.bfloat16)
    wl = (w - wh.astype(jnp.float32)).astype(jnp.bfloat16)
    wcat = jnp.concatenate([wh, wh, wl], axis=1)
    for s in range(rows):
        x = samples(s)
        xh = x.astype(jnp.bfloat16)
        xl = (x - xh.astype(jnp.float32)).astype(jnp.bfloat16)
        xcat = jnp.concatenate([xh, xl, xh], axis=0)
        store(s, jnp.dot(wcat, xcat, preferred_element_type=jnp.float32))


def dft_owner_kernel(rows, _, w_ref, x_ref, *outs):
    def samples(s):
        return jnp.concatenate([x_ref[j, :, s, :] for j in range(x_ref.shape[0])], axis=0)

    def store(s, res):
        for i in range(8):
            outs[i][:, s, :] = res[8 * i : 8 * i + 8]

    transform(w_ref, samples, store, rows)


def dft_by_owner(index, w, x, block):
    n, _, rows, _ = x.shape
    k = w.shape[2]
    flat = pl.pallas_call(
        functools.partial(dft_owner_kernel, block),
        grid_spec=pltpu.PrefetchScalarGridSpec(
            num_scalar_prefetch=1,
            grid=(rows // block,),
            in_specs=[
                pl.BlockSpec((1, 64, k), lambda g, i: (i[0], 0, 0)),
                pl.BlockSpec((n, 16, block, C), lambda g, i: (0, 0, g, 0)),
            ],
            out_specs=[pl.BlockSpec((8, block, C), lambda g, i: (0, g, 0))] * 8,
        ),
        out_shape=[jax.ShapeDtypeStruct((8, rows, C), jnp.float32)] * 8,
        compiler_params=pltpu.CompilerParams(vmem_limit_bytes=VMEM),
        cost_estimate=cost(12),
    )(index, w, x)
    return [flat[2 * r : 2 * r + 2] for r in range(4)]


def dft_row_kernel(rows, _, w_ref, *refs):
    pieces, outs = refs[:4], refs[4:]

    def samples(s):
        return jnp.concatenate([p[:, 0, s, :] for p in pieces], axis=0)

    def store(s, res):
        for q in range(2):
            outs[q][0, :, s, :] = res[32 * q : 32 * q + 32]

    transform(w_ref, samples, store, rows)


def dft_by_row(index, w, pieces):
    rows = pieces[0].shape[2]
    return pl.pallas_call(
        functools.partial(dft_row_kernel, rows),
        grid_spec=pltpu.PrefetchScalarGridSpec(
            num_scalar_prefetch=1,
            grid=(4,),
            in_specs=[pl.BlockSpec((1, 64, 64), lambda g, i: (i[0], 0, 0))]
            + [pl.BlockSpec((16, 1, rows, C), lambda g, i: (0, g, 0, 0))] * 4,
            out_specs=[pl.BlockSpec((1, 32, rows, C), lambda g, i: (g, 0, 0, 0))] * 2,
        ),
        out_shape=[jax.ShapeDtypeStruct((4, 32, rows, C), jnp.float32)] * 2,
        compiler_params=pltpu.CompilerParams(vmem_limit_bytes=VMEM),
        cost_estimate=cost(7),
    )(index, w, *pieces)


def reduce_ring(slots, axis):
    up0 = shift(slots[2][0], axis, 1)
    down1 = shift(slots[2][1], axis, -1)
    up1 = shift(slots[1][1], axis, 1)
    down0 = shift(slots[3][0], axis, -1)
    up0 = shift(slots[1][0] + up0, axis, 1)
    down1 = shift(slots[3][1] + down1, axis, -1)
    return [slots[0][0] + up0 + down0, slots[0][1] + up1 + down1]


def product_kernel(starts, sizes, index, *refs):
    n = len(starts)
    left, right = refs[: 8 * n], refs[8 * n : 10 * n]
    out, a_ref, b_ref = refs[10 * n :]
    col = index[0]

    def split(x):
        hi = x.astype(jnp.bfloat16)
        return hi, (x - hi.astype(jnp.float32)).astype(jnp.bfloat16)

    for i in range(n):
        rows = slice(starts[i], starts[i] + sizes[i])
        for part in range(2):
            for e in range(4):
                hi, lo = split(left[8 * i + 2 * e + part][0])
                a_ref[col ^ e, 2 * part, rows] = hi
                a_ref[col ^ e, 2 * part + 1, rows] = lo
            for k in range(4):
                hi, lo = split(right[2 * i + part][k, 0])
                b_ref[k, 2 * part, rows] = hi
                b_ref[k, 2 * part + 1, rows] = lo

    def dot(x, y):
        return jnp.dot(x, y, preferred_element_type=jnp.float32)

    rr = jnp.zeros((256, C), jnp.float32)
    ii, ri, ir = rr, rr, rr
    for k in range(4):
        arh, arl, aih, ail = (a_ref[k, j] for j in range(4))
        brh, brl, bih, bil = (b_ref[k, j] for j in range(4))
        rr += dot(arh, brh) + dot(arh, brl) + dot(arl, brh)
        ii += dot(aih, bih) + dot(aih, bil) + dot(ail, bih)
        ri += dot(arh, bih) + dot(arh, bil) + dot(arl, bih)
        ir += dot(aih, brh) + dot(aih, brl) + dot(ail, brh)
    out[0, 0] = rr - ii
    out[1, 0] = ri + ir


def product(index, left, right, starts, sizes):
    operands, specs = [], []
    for i, part in enumerate(left):
        for block in part:
            operands += [block, block]
            specs += [pl.BlockSpec((1, sizes[i], C), lambda g, _, p=p: (p + g, 0, 0)) for p in (0, 4)]
    for i, part in enumerate(right):
        operands += [part, part]
        specs += [pl.BlockSpec((4, 1, sizes[i], C), lambda g, _, p=p: (0, p + g, 0, 0)) for p in (0, 4)]
    return pl.pallas_call(
        functools.partial(product_kernel, starts, sizes),
        grid_spec=pltpu.PrefetchScalarGridSpec(
            num_scalar_prefetch=1,
            grid=(4,),
            in_specs=specs,
            out_specs=pl.BlockSpec((2, 1, 256, C), lambda g, i: (0, g, 0, 0)),
            scratch_shapes=[
                pltpu.VMEM((4, 4, 256, C), jnp.bfloat16),
                pltpu.VMEM((4, 4, 256, C), jnp.bfloat16),
            ],
        ),
        out_shape=jax.ShapeDtypeStruct((2, 4, 256, C), jnp.float32),
        compiler_params=pltpu.CompilerParams(vmem_limit_bytes=VMEM),
        cost_estimate=cost(13),
    )(index, *operands)


def local(x):
    f = lax.axis_index("freq")
    y, x_lo = f // 2, f % 2
    z = lax.axis_index("row")
    col = lax.axis_index("col")
    one, two, three = tables()
    at_f = jnp.stack([f])
    blocks = x.reshape(16, 4, 256, C)

    def rows(start, size):
        return lax.dynamic_slice_in_dim(blocks, start, size, 2)

    quarter, half = R2 // 4, R3 // 2
    first = jnp.transpose(blocks[:, :, :R1], (1, 0, 2, 3))
    first = lax.all_to_all(first, "row", split_axis=0, concat_axis=0, tiled=True)
    third_own, third_far = rows(R1 + R2 + half * x_lo, half), rows(R1 + R2 + half * (1 - x_lo), half)
    third_far = shift(third_far, "x_lo")
    second = [rows(R1 + quarter * ((y + r) % 4), quarter) for r in range(4)]
    second = [second[0]] + [shift(second[r], "y", r) for r in (1, 2, 3)]
    first, third_own, third_far, second = together(first, third_own, third_far, second)

    third = jnp.transpose(jnp.stack([third_own, third_far]), (2, 0, 1, 3, 4))
    third = lax.all_to_all(third, "row", split_axis=0, concat_axis=0, tiled=True)
    slots = dft_by_owner(at_f, one, first, 16)
    mine2, other2 = dft_by_row(jnp.stack([4 * f + z]), two, second)
    slots, mine2, other2 = together(slots, mine2, other2)
    mine1, other1 = reduce_ring(slots, "y")
    own2 = mine2 + shift(other2, "x_lo")
    mine1, other1, own2, third = together(mine1, other1, own2, third)

    slots = dft_by_owner(at_f, three, third.reshape(8, 16, half, C), 16)
    own1 = mine1 + shift(other1, "x_lo")
    own2 = lax.psum_scatter(own2, "row", scatter_dimension=0, tiled=False)
    mine3, other3 = reduce_ring(slots, "y")
    own1, own2, mine3, other3 = together(own1, own2, mine3, other3)

    bins = [own2[8 * r : 8 * r + 8] for r in range(4)]
    own2 = jnp.zeros((8, R2, C), jnp.float32)
    for r in range(4):
        piece = bins[r] if r == 0 else shift(bins[r], "y", r)
        own2 = lax.dynamic_update_slice(own2, piece, (0, quarter * ((y + 4 - r) % 4), 0))
    other3 = shift(other3, "x_lo")
    own3 = jnp.where(x_lo == 0, jnp.concatenate([mine3, other3], axis=1), jnp.concatenate([other3, mine3], axis=1))
    rest = jnp.concatenate([own2, own3], axis=1)

    left, right = [], []
    for part in (own1, rest):
        far = shift(part, "x_hi")
        right.append(lax.all_gather(part, "row", axis=0, tiled=False))
        left.append((part, shift(part, "core"), far, shift(far, "core")))
    return product(jnp.stack([col]), left, right, (0, R1), (R1, R2 + R3))


def solution(mesh):
    in_specs = (P(("freq", "row"), None, "col"),)
    out_specs = P(None, "freq", "row", "col")
    return jax.shard_map(local, mesh=mesh, in_specs=in_specs, out_specs=out_specs, check_vma=False)
```

time: 596 us -> 337 us (0.57)
  waiting for transfers between devices: 439 us -> 186 us
  starting transfers between devices: 10 us -> 69.3 us
  blocking collectives: 43.9 us -> 0 us
  matrix products: 42.7 us -> 0 us
  Pallas kernels: 0 us -> 33.8 us
  local copies, waits for them, and re-layouts: 39.1 us -> 21.3 us
  other arithmetic: 1.77 us -> 12.2 us
    all_to_all x1 -> x2, waiting for transfers between devices: 294 us -> 0.01 us  [the longest x1 0.01 us: local(): lax.all_to_all(first, 'row', split_axis=0, concat_axis=0, tiled=True)]
    ppermute x0 -> x28, waiting for transfers between devices: none -> 145 us  [the longest x18 107 us: shift(): return lax.ppermute(x, 'freq', [(i, (i + 2 * by) % 8) for i in range(8)])]
    all_gather x2, waiting for transfers between devices: 145 us -> 41.4 us  [local(): right.append(lax.all_gather(part, 'row', axis=0, tiled=False))]
    ppermute x0 -> x28, starting transfers between devices: none -> 57.7 us  [the longest x4 26.9 us: shift(): return lax.ppermute(x, 'col', [(i, i ^ 1) for i in range(4)])]
    all_to_all x1 -> x0, blocking collectives: 43.9 us -> none  [local(): lax.all_to_all(spectra, 'freq', split_axis=1, concat_axis=2, tiled=True)]
    dot_general x6 -> x0, matrix products: 42.7 us -> none  [the longest x1 10.1 us: local(): jnp.einsum('bgd,bw->wgd', shifted_blocks, cosine_lookup, precision=highes...]
    pallas_call x0 -> x4, Pallas kernels: none -> 33.8 us  [the longest x2 15.6 us: dft_by_owner(): pl.pallas_call(functools.partial(dft_owner_kernel, block), grid_spec=pltp...]
    reshape x1 -> x0, local copies, waits for them, and re-layouts: 22.8 us -> none  [local(): jnp.transpose(ordered, (0, 2, 1, 3, 4)).reshape(width, sources, columns)]
  transfers between devices with their start and end apart: 3 -> 33, of which waited for: 3 -> 18; matrix products, arithmetic and copies ran while one was open for 0% -> 6% of each run, Pallas kernels for 0% -> 7%
where the time goes in v1:
time: 337 us; the launch traced here: 336 us
  waiting for transfers between devices  186 us (55%)
  starting transfers between devices  69.3 us (21%)
  Pallas kernels  33.8 us (10%)
  local copies, waits for them, and re-layouts  21.3 us (6%)
  between operations  13.4 us (4%)
  other arithmetic  12.2 us (4%)
    ppermute x18, waiting for transfers between devices, shift(): return lax.ppermute(x, 'freq', [(i, (i + 2 * by) % 8) for i in range(8)])  107 us
    all_gather x2, waiting for transfers between devices, local(): right.append(lax.all_gather(part, 'row', axis=0, tiled=False))  41.4 us
    ppermute x4, starting transfers between devices, shift(): return lax.ppermute(x, 'col', [(i, i ^ 1) for i in range(4)])  26.9 us
    ppermute x18, starting transfers between devices, shift(): return lax.ppermute(x, 'freq', [(i, (i + 2 * by) % 8) for i in range(8)])  23 us
    ppermute x2, waiting for transfers between devices, shift(): return lax.ppermute(x, 'col', [(i, i ^ 2) for i in range(4)])  20.7 us
    pallas_call x2, Pallas kernels, dft_by_owner(): pl.pallas_call(functools.partial(dft_owner_kernel, block), grid_spec=pltp...  15.6 us
    ppermute x4, waiting for transfers between devices, shift(): return lax.ppermute(x, 'freq', [(i, i ^ 1) for i in range(8)])  15.1 us
    pallas_call x1, Pallas kernels, product(): pl.pallas_call(functools.partial(product_kernel, starts, sizes), grid_spe...  11.7 us
  transfers between devices with their start and end apart: 33, of which 18 were waited for; matrix products, arithmetic and copies ran while one was open for 6% of the time, Pallas kernels for 7%

profile of v1, /device:TPU:1, one launch (start us, length us, event | category | flops | bytes accessed | tf_op | source)
XLA Modules:
  0.0 336.4 jit_solution(16334325907708404369)
XLA Ops:
  6.5 3.5 %slice_bitcast_fusion = f32[4,16,96,256]{3,2,0,1:T(8,128)S(1)} fusion(f32[16,4,256,256]{3,2,1,0:T(8,128)} %bitcast.16), kind=kLoop, calls=%fused_computation | loop fusion | bytes 12582912 | tf_op jit(solution)/shard_map/transpose | solution.py:225
  10.1 3.4 %copy.7 = f32[4,16,96,256]{3,2,1,0:T(8,128)} copy(f32[4,16,96,256]{3,2,0,1:T(8,128)S(1)} %slice_bitcast_fusion) | data formatting | bytes 12582912 | tf_op jit(solution)/shard_map/transpose | solution.py:225
  13.5 5.9 %all-to-all-start = ((f32[4,16,96,256]{3,2,1,0:T(8,128)}), f32[4,16,96,256]{3,2,1,0:T(8,128)}, u32[]{:S(2)}, u32[]{:S(2)}) async-start(f32[4,16,96,256]{3,2,1,0:T(8,128)} %copy.7), calls=%async_computation | async-start | bytes 12582912 | tf_op jit(solution)/shard_map/all_to_all | solution.py:226
  19.4 6.2 %constant_dynamic-slice_fusion.4 = (f32[16,4,48,256]{3,2,1,0:T(8,128)}, f32[16,4,48,256]{3,2,1,0:T(8,128)}) fusion(f32[16,4,256,256]{3,2,1,0:T(8,128)} %bitcast.17, s32[]{:T(128)S(6)} %select_n.77, s32[]{:T(128)S(6)} %select_n.76), kind=kLoop, calls=%fused_computation.16 | loop fusion | bytes 12582920 | tf_op jit(solution)/shard_map/dynamic_slice | solution.py:222
  25.6 1.5 collective-permute-start
  27.1 2.7 constant_dynamic-slice_fusion
  29.8 1.4 collective-permute-start.1
  31.2 2.6 collective-permute-start.2
  33.8 1.1 collective-permute-start.3
  34.9 20.2 %collective-permute-done.1.refs_1_ = f32[16,4,16,256]{3,2,1,0:T(8,128)S(1)} collective-permute-done((f32[16,4,16,256]{3,2,1,0:T(8,128)S(1)}, f32[16,4,16,256]{3,2,1,0:T(8,128)S(1)}, u32[]{:S(2)}, u32[]{:S(2)}) %collective-permute-start.1) | collective-permute-done | bytes 1048608 | tf_op jit(solution)/shard_map/ppermute | solution.py:24
  55.1 23.6 %collective-permute-done.2.refs_2_ = f32[16,4,16,256]{3,2,1,0:T(8,128)S(1)} collective-permute-done((f32[16,4,16,256]{3,2,1,0:T(8,128)S(1)}, f32[16,4,16,256]{3,2,1,0:T(8,128)S(1)}, u32[]{:S(2)}, u32[]{:S(2)}) %collective-permute-start.2) | collective-permute-done | bytes 1048608 | tf_op jit(solution)/shard_map/ppermute | solution.py:24
  78.6 1.0 copy-done.6
  79.6 15.1 %collective-permute-done = f32[16,4,48,256]{3,2,1,0:T(8,128)} collective-permute-done((f32[16,4,48,256]{3,2,1,0:T(8,128)}, f32[16,4,48,256]{3,2,1,0:T(8,128)}, u32[]{:S(2)}, u32[]{:S(2)}) %collective-permute-start) | collective-permute-done | bytes 3145760 | tf_op jit(solution)/shard_map/ppermute | solution.py:26
  94.7 3.5 %maximum_bitcast_fusion = f32[4,2,16,48,256]{4,3,0,2,1:T(8,128)S(1)} fusion(f32[1,16,4,48,256]{4,3,2,1,0:T(8,128)} %bitcast.6, f32[1,16,4,48,256]{4,3,2,1,0:T(8,128)} %bitcast.21), kind=kLoop, calls=%fused_computation.1 | loop fusion | flops 1572864 | bytes 12582912 | tf_op jit(solution)/shard_map/transpose | solution.py:233
  98.3 3.2 copy.8
  101.4 5.7 %all-to-all-start.1 = ((f32[4,2,16,48,256]{4,3,2,1,0:T(8,128)}), f32[4,2,16,48,256]{4,3,2,1,0:T(8,128)}, u32[]{:S(2)}, u32[]{:S(2)}) async-start(f32[4,2,16,48,256]{4,3,2,1,0:T(8,128)} %copy.8), calls=%async_computation.1 | async-start | bytes 12582912 | tf_op jit(solution)/shard_map/all_to_all | solution.py:234
  107.1 9.1 %shard_map.46 = (f32[8,96,256]{2,1,0:T(8,128)S(1)}, f32[8,96,256]{2,1,0:T(8,128)S(1)}, f32[8,96,256]{2,1,0:T(8,128)S(1)}, f32[8,96,256]{2,1,0:T(8,128)S(1)}, f32...) custom-call(s32[1]{0:T(128)} %bitcast.1._, ...), custom_call_target="tpu_custom_call" | custom-call | bytes 43200000 | tf_op jit(solution)/shard_map/pallas_call | solution.py:89
  116.3 6.6 %shard_map.47 = (f32[4,32,16,256]{3,2,1,0:T(8,128)}, f32[4,32,16,256]{3,2,1,0:T(8,128)}) custom-call(s32[1]{0:T(128)} %bitcast.4._, f32[32,64,64]{2,1,0:T(8,128)S(1)} %copy-done.1, f32[16,4,16,256]{3,2,1,0:T(8,128)S(1)} %get-tuple-element.57.refs_0_, f32[16,4,16,256]{3,2,1,0:T(8,128)S(1)} %collective-permute-done.1.refs_1_, f32[16,4,16,256]{3,2,1,0:T(8,128)} %copy-done.5, ...), custom_call_target="tpu_custom_call" | custom-call | bytes 25200000 | tf_op jit(solution)/shard_map/pallas_call | solution.py:122
  122.8 1.6 collective-permute-start.4
  124.4 1.2 collective-permute-start.10
  125.6 1.5 collective-permute-start.8
  127.1 1.4 collective-permute-start.6
  128.5 13.5 %collective-permute-done.4 = f32[8,96,256]{2,1,0:T(8,128)S(1)} collective-permute-done((f32[8,96,256]{2,1,0:T(8,128)S(1)}, f32[8,96,256]{2,1,0:T(8,128)S(1)}, u32[]{:S(2)}, u32[]{:S(2)}) %collective-permute-start.4) | collective-permute-done | bytes 786464 | tf_op jit(solution)/shard_map/ppermute | solution.py:24
  142.2 1.2 collective-permute-start.7
  143.6 2.1 collective-permute-start.9
  145.7 13.8 %collective-permute-done.6 = f32[8,96,256]{2,1,0:T(8,128)S(1)} collective-permute-done((f32[8,96,256]{2,1,0:T(8,128)S(1)}, f32[8,96,256]{2,1,0:T(8,128)S(1)}, u32[]{:S(2)}, u32[]{:S(2)}) %collective-permute-start.6) | collective-permute-done | bytes 786464 | tf_op jit(solution)/shard_map/ppermute | solution.py:24
  159.5 0.8 collective-permute-done.5
  160.5 16.7 %collective-permute-done.7 = f32[8,96,256]{2,1,0:T(8,128)S(1)} collective-permute-done((f32[8,96,256]{2,1,0:T(8,128)S(1)}, f32[8,96,256]{2,1,0:T(8,128)S(1)}, u32[]{:S(2)}, u32[]{:S(2)}) %collective-permute-start.7) | collective-permute-done | bytes 786464 | tf_op jit(solution)/shard_map/ppermute | solution.py:24
  177.3 1.8 add.181
  179.2 1.5 collective-permute-start.11
  180.7 6.5 %shard_map.48 = (f32[8,48,256]{2,1,0:T(8,128)S(1)}, f32[8,48,256]{2,1,0:T(8,128)S(1)}, f32[8,48,256]{2,1,0:T(8,128)S(1)}, f32[8,48,256]{2,1,0:T(8,128)S(1)}, f32...) custom-call(s32[1]{0:T(128)} %bitcast.1._, ...), custom_call_target="tpu_custom_call" | custom-call | bytes 43200000 | tf_op jit(solution)/shard_map/pallas_call | solution.py:89
  187.2 0.2 collective-permute-start.12
  187.4 2.5 collective-permute-start.16
  189.9 0.4 collective-permute-start.14
  190.4 5.4 %collective-permute-done.12 = f32[8,48,256]{2,1,0:T(8,128)S(1)} collective-permute-done((f32[8,48,256]{2,1,0:T(8,128)S(1)}, f32[8,48,256]{2,1,0:T(8,128)S(1)}, u32[]{:S(2)}, u32[]{:S(2)}) %collective-permute-start.12) | collective-permute-done | bytes 393248 | tf_op jit(solution)/shard_map/ppermute | solution.py:24
  195.7 0.8 add.183
  196.5 1.0 collective-permute-start.15
  197.6 0.8 add.187
  198.4 1.7 collective-permute-start.17
  200.1 1.0 add.182.refs_0_.refs_1_
  201.1 2.2 collective-permute-done.14
  203.3 1.7 collective-permute-done.13
  205.0 1.2 add_add_fusion.3
  206.2 6.6 %collective-permute-done.15 = f32[8,48,256]{2,1,0:T(8,128)} collective-permute-done((f32[8,48,256]{2,1,0:T(8,128)S(1)}, f32[8,48,256]{2,1,0:T(8,128)}, u32[]{:S(2)}, u32[]{:S(2)}) %collective-permute-start.15) | collective-permute-done | bytes 393248 | tf_op jit(solution)/shard_map/ppermute | solution.py:24
  212.8 1.2 add_add_fusion.2
  214.2 1.1 fusion
  215.3 0.6 collective-permute-start.21
  215.9 0.5 collective-permute-start.24
  216.4 2.6 collective-permute-start.22
  219.1 0.9 collective-permute-start.23
  220.0 0.4 collective-permute-done.21
  220.5 2.0 collective-permute-done.22
  222.5 0.4 collective-permute-done.23
  223.0 1.2 pad_maximum_fusion.refs_8_.refs_9_
  224.2 2.8 collective-permute-start.26
  227.0 0.2 collective-permute-start.19
  227.3 7.2 %collective-permute-start.25 = (f32[8,160,256]{2,1,0:T(8,128)}, f32[8,160,256]{2,1,0:T(8,128)}, u32[]{:S(2)}, u32[]{:S(2)}) collective-permute-start(f32[8,160,256]{2,1,0:T(8,128)} %pad_maximum_fusion.refs_8_.refs_9_), channel_id=1, source_target_pairs={{0,1},{1,0},{2,3},{3,2},{4,5},{5,4},{6,7},{7,6},{8,9},{9,8},{10,11... | collective-permute-start | bytes 3932168 | tf_op jit(solution)/shard_map/ppermute | solution.py:29
  234.5 17.0 %collective-permute-done.26.refs_12_.refs_13_ = f32[8,160,256]{2,1,0:T(8,128)} collective-permute-done((f32[8,160,256]{2,1,0:T(8,128)}, f32[8,160,256]{2,1,0:T(8,128)}, u32[]{:S(2)}, u32[]{:S(2)}) %collective-permute-start.26) | collective-permute-done | bytes 1310752 | tf_op jit(solution)/shard_map/ppermute | solution.py:28
  251.4 13.0 %collective-permute-start.27 = (f32[8,160,256]{2,1,0:T(8,128)}, f32[8,160,256]{2,1,0:T(8,128)}, u32[]{:S(2)}, u32[]{:S(2)}) collective-permute-start(f32[8,160,256]{2,1,0:T(8,128)} %collective-permute-done.26.refs_12_.refs_13_), channel_id=1, source_target_pairs={{0,1},{1,0},{2,3},{3,2},{4,5},{5,4},{6,7},{7,6},{8,9},{9,8},{10,11... | collective-permute-start | bytes 3932168 | tf_op jit(solution)/shard_map/ppermute | solution.py:29
  264.5 3.7 %collective-permute-done.19.refs_4_.refs_5_ = f32[8,96,256]{2,1,0:T(8,128)S(1)} collective-permute-done((f32[8,96,256]{2,1,0:T(8,128)S(1)}, f32[8,96,256]{2,1,0:T(8,128)S(1)}, u32[]{:S(2)}, u32[]{:S(2)}) %collective-permute-start.19) | collective-permute-done | bytes 786464 | tf_op jit(solution)/shard_map/ppermute | solution.py:28
  268.2 6.7 %collective-permute-start.20 = (f32[8,96,256]{2,1,0:T(8,128)S(1)}, f32[8,96,256]{2,1,0:T(8,128)S(1)}, u32[]{:S(2)}, u32[]{:S(2)}) collective-permute-start(f32[8,96,256]{2,1,0:T(8,128)S(1)} %collective-permute-done.19.refs_4_.refs_5_), channel_id=1, source_target_pairs={{0,1},{1,0},{2,3},{3,2},{4,5},{5,4},{6,7},{7,6},{8,9},{9,8},{10,11... | collective-permute-start | bytes 2359304 | tf_op jit(solution)/shard_map/ppermute | solution.py:29
  274.9 1.9 collective-permute-done.20.refs_6_.refs_7_
  276.8 41.4 %all-gather.7.cloned.1.call-done = f32[32,160,256]{2,1,0:T(8,128)} async-done(((f32[8,160,256]{2,1,0:T(8,128)}), f32[32,160,256]{2,1,0:T(8,128)}) %all-gather.7.cloned.1.call-update) | async-done | bytes 5242896 | tf_op jit(solution)/shard_map/all_gather | solution.py:260
  318.2 11.7 %shard_map.49 = f32[2,4,256,256]{3,2,1,0:T(8,128)} custom-call(s32[1]{0:T(128)} %bitcast.index, f32[8,96,256]{2,1,0:T(8,128)S(1)} %copy-done, f32[8,96,256]{2,1,0:T(8,128)S(1)} %copy-done, f32[8,96,256]{2,1,0:T(8,128)S(1)} %collective-permute-done.18.refs_2_.refs_3_, f32[8,96,256]{2,1,0:T(8,128)S(1)} %collective-permute-done.18.refs_2_.refs_3_, ...), custom_call_target="tpu_custom_call" | custom-call | bytes 46800000 | tf_op jit(solution)/shard_map/pallas_call | solution.py:194
  (54 shorter events, 1.0 us)
Async XLA Ops:
  13.5 81.2 %all-to-all-start = ((f32[4,16,96,256]{3,2,1,0:T(8,128)}), f32[4,16,96,256]{3,2,1,0:T(8,128)}, u32[]{:S(2)}, u32[]{:S(2)}) async-start(f32[4,16,96,256]{3,2,1,0:T(8,128)} %copy.7), calls=%async_computation | async-start | bytes 12582912 | tf_op jit(solution)/shard_map/all_to_all | solution.py:226
  25.6 69.1 %collective-permute-start = (f32[16,4,48,256]{3,2,1,0:T(8,128)}, f32[16,4,48,256]{3,2,1,0:T(8,128)}, u32[]{:S(2)}, u32[]{:S(2)}) collective-permute-start(f32[16,4,48,256]{3,2,1,0:T(8,128)} %get-tuple-element.95), channel_id=1, source_target_pairs={{0,16},{16,0},{32,48},{48,32},{64,80},{80,64},{96,112},{112,96},{1... | collective-permute-start | bytes 9437192 | tf_op jit(solution)/shard_map/ppermute | solution.py:26
  29.8 25.2 %collective-permute-start.1 = (f32[16,4,16,256]{3,2,1,0:T(8,128)S(1)}, f32[16,4,16,256]{3,2,1,0:T(8,128)S(1)}, u32[]{:S(2)}, u32[]{:S(2)}) collective-permute-start(f32[16,4,16,256]{3,2,1,0:T(8,128)S(1)} %get-tuple-element.93), channel_id=1, source_target_pairs={{0,32},{16,48},{32,64},{48,80},{64,96},{80,112},{96,0},{112,16},{1... | collective-permute-start | bytes 3145736 | tf_op jit(solution)/shard_map/ppermute | solution.py:24
  31.2 47.4 %collective-permute-start.2 = (f32[16,4,16,256]{3,2,1,0:T(8,128)S(1)}, f32[16,4,16,256]{3,2,1,0:T(8,128)S(1)}, u32[]{:S(2)}, u32[]{:S(2)}) collective-permute-start(f32[16,4,16,256]{3,2,1,0:T(8,128)S(1)} %get-tuple-element.92), channel_id=1, source_target_pairs={{0,64},{16,80},{32,96},{48,112},{64,0},{80,16},{96,32},{112,48},{1... | collective-permute-start | bytes 3145736 | tf_op jit(solution)/shard_map/ppermute | solution.py:24
  33.8 44.8 %collective-permute-start.3 = (f32[16,4,16,256]{3,2,1,0:T(8,128)S(1)}, f32[16,4,16,256]{3,2,1,0:T(8,128)S(1)}, u32[]{:S(2)}, u32[]{:S(2)}) collective-permute-start(f32[16,4,16,256]{3,2,1,0:T(8,128)S(1)} %get-tuple-element.91), channel_id=1, source_target_pairs={{0,96},{16,112},{32,0},{48,16},{64,32},{80,48},{96,64},{112,80},{1... | collective-permute-start | bytes 3145736 | tf_op jit(solution)/shard_map/ppermute | solution.py:24
  78.6 19.6 %copy-start.5 = (f32[16,4,16,256]{3,2,1,0:T(8,128)}, f32[16,4,16,256]{3,2,1,0:T(8,128)S(1)}, u32[]{:S(2)}) copy-start(f32[16,4,16,256]{3,2,1,0:T(8,128)S(1)} %collective-permute-done.2.refs_2_) | copy-start | bytes 3145732
  78.6 1.0 copy-start.6
  101.4 5.7 %copy-start.3 = (f32[8,64,64]{2,1,0:T(8,128)S(1)}, f32[8,64,64]{2,1,0:T(8,128)}, u32[]{:S(2)}) copy-start(f32[8,64,64]{2,1,0:T(8,128)} %constant.111.clone.w_ref) | copy-start | bytes 393220
  101.4 77.7 %all-to-all-start.1 = ((f32[4,2,16,48,256]{4,3,2,1,0:T(8,128)}), f32[4,2,16,48,256]{4,3,2,1,0:T(8,128)}, u32[]{:S(2)}, u32[]{:S(2)}) async-start(f32[4,2,16,48,256]{4,3,2,1,0:T(8,128)} %copy.8), calls=%async_computation.1 | async-start | bytes 12582912 | tf_op jit(solution)/shard_map/all_to_all | solution.py:234
  107.1 106.9 %reduce-scatter.2.cloned.1.call-start = ((), (), s32[]{:S(2)}) async-start(), calls=%async_computation.3 | async-start | bytes 2621440 | tf_op jit(solution)/shard_map/reduce_scatter | solution.py:244
  107.1 9.1 %copy-start.1 = (f32[32,64,64]{2,1,0:T(8,128)S(1)}, f32[32,64,64]{2,1,0:T(8,128)}, u32[]{:S(2)}) copy-start(f32[32,64,64]{2,1,0:T(8,128)} %constant.112.clone.w_ref) | copy-start | bytes 1572868
  116.2 6.6 %copy-start.10 = (f32[8,96,256]{2,1,0:T(8,128)S(1)}, f32[8,96,256]{2,1,0:T(8,128)}, u32[]{:S(2)}) copy-start(f32[8,96,256]{2,1,0:T(8,128)} %get-tuple-element.65) | copy-start | bytes 2359300
  116.2 9.4 %copy-start.9 = (f32[8,96,256]{2,1,0:T(8,128)S(1)}, f32[8,96,256]{2,1,0:T(8,128)}, u32[]{:S(2)}) copy-start(f32[8,96,256]{2,1,0:T(8,128)} %get-tuple-element.70) | copy-start | bytes 2359300
  116.2 10.9 %copy-start.8 = (f32[8,96,256]{2,1,0:T(8,128)S(1)}, f32[8,96,256]{2,1,0:T(8,128)}, u32[]{:S(2)}) copy-start(f32[8,96,256]{2,1,0:T(8,128)} %get-tuple-element.66) | copy-start | bytes 2359300
  116.3 27.2 %copy-start.7 = (f32[8,96,256]{2,1,0:T(8,128)S(1)}, f32[8,96,256]{2,1,0:T(8,128)}, u32[]{:S(2)}) copy-start(f32[8,96,256]{2,1,0:T(8,128)} %get-tuple-element.69) | copy-start | bytes 2359300
  122.8 19.2 %collective-permute-start.4 = (f32[8,96,256]{2,1,0:T(8,128)S(1)}, f32[8,96,256]{2,1,0:T(8,128)S(1)}, u32[]{:S(2)}, u32[]{:S(2)}) collective-permute-start(f32[8,96,256]{2,1,0:T(8,128)S(1)} %copy-done.10), channel_id=1, source_target_pairs={{0,32},{16,48},{32,64},{48,80},{64,96},{80,112},{96,0},{112,16},{1... | collective-permute-start | bytes 2359304 | tf_op jit(solution)/shard_map/ppermute | solution.py:24
  124.4 52.9 %collective-permute-start.10 = (f32[4,32,16,256]{3,2,1,0:T(8,128)}, f32[4,32,16,256]{3,2,1,0:T(8,128)S(1)}, u32[]{:S(2)}, u32[]{:S(2)}) collective-permute-start(f32[4,32,16,256]{3,2,1,0:T(8,128)} %get-tuple-element.72), channel_id=1, source_target_pairs={{0,16},{16,0},{32,48},{48,32},{64,80},{80,64},{96,112},{112,96},{1... | collective-permute-start | bytes 6291464 | tf_op jit(solution)/shard_map/ppermute | solution.py:26
  125.6 17.9 %collective-permute-start.8 = (f32[8,96,256]{2,1,0:T(8,128)S(1)}, f32[8,96,256]{2,1,0:T(8,128)S(1)}, u32[]{:S(2)}, u32[]{:S(2)}) collective-permute-start(f32[8,96,256]{2,1,0:T(8,128)S(1)} %copy-done.9), channel_id=1, source_target_pairs={{0,96},{16,112},{32,0},{48,16},{64,32},{80,48},{96,64},{112,80},{1... | collective-permute-start | bytes 2359304 | tf_op jit(solution)/shard_map/ppermute | solution.py:24
  127.1 32.4 %collective-permute-start.6 = (f32[8,96,256]{2,1,0:T(8,128)S(1)}, f32[8,96,256]{2,1,0:T(8,128)S(1)}, u32[]{:S(2)}, u32[]{:S(2)}) collective-permute-start(f32[8,96,256]{2,1,0:T(8,128)S(1)} %copy-done.8), channel_id=1, source_target_pairs={{0,96},{16,112},{32,0},{48,16},{64,32},{80,48},{96,64},{112,80},{1... | collective-permute-start | bytes 2359304 | tf_op jit(solution)/shard_map/ppermute | solution.py:24
  142.1 18.1 %collective-permute-start.5 = (f32[8,96,256]{2,1,0:T(8,128)S(1)}, f32[8,96,256]{2,1,0:T(8,128)S(1)}, u32[]{:S(2)}, u32[]{:S(2)}) collective-permute-start(f32[8,96,256]{2,1,0:T(8,128)S(1)} %add.175), channel_id=1, source_target_pairs={{0,32},{16,48},{32,64},{48,80},{64,96},{80,112},{96,0},{112,16},{1... | collective-permute-start | bytes 2359304 | tf_op jit(solution)/shard_map/ppermute | solution.py:24
  142.2 34.9 %collective-permute-start.7 = (f32[8,96,256]{2,1,0:T(8,128)S(1)}, f32[8,96,256]{2,1,0:T(8,128)S(1)}, u32[]{:S(2)}, u32[]{:S(2)}) collective-permute-start(f32[8,96,256]{2,1,0:T(8,128)S(1)} %get-tuple-element.68), channel_id=1, source_target_pairs={{0,32},{16,48},{32,64},{48,80},{64,96},{80,112},{96,0},{112,16},{1... | collective-permute-start | bytes 2359304 | tf_op jit(solution)/shard_map/ppermute | solution.py:24
  143.6 33.7 %copy-start.4 = (f32[4,32,16,256]{3,2,1,0:T(8,128)S(1)}, f32[4,32,16,256]{3,2,1,0:T(8,128)}, u32[]{:S(2)}) copy-start(f32[4,32,16,256]{3,2,1,0:T(8,128)} %get-tuple-element.71) | copy-start | bytes 6291460
  143.6 33.5 %collective-permute-start.9 = (f32[8,96,256]{2,1,0:T(8,128)S(1)}, f32[8,96,256]{2,1,0:T(8,128)S(1)}, u32[]{:S(2)}, u32[]{:S(2)}) collective-permute-start(f32[8,96,256]{2,1,0:T(8,128)S(1)} %add.179), channel_id=1, source_target_pairs={{0,96},{16,112},{32,0},{48,16},{64,32},{80,48},{96,64},{112,80},{1... | collective-permute-start | bytes 2359304 | tf_op jit(solution)/shard_map/ppermute | solution.py:24
  177.3 3.4 %copy-start.2 = (f32[8,64,128]{2,1,0:T(8,128)S(1)}, f32[8,64,128]{2,1,0:T(8,128)}, u32[]{:S(2)}) copy-start(f32[8,64,128]{2,1,0:T(8,128)} %constant.113.clone.w_ref) | copy-start | bytes 786436
  179.2 97.6 %all-gather.5.cloned.1.call-start = ((), (), s32[]{:S(2)}) async-start(), calls=%async_computation.4 | async-start | bytes 3932160 | tf_op jit(solution)/shard_map/all_gather | solution.py:260
  179.2 20.8 %collective-permute-start.11 = (f32[8,96,256]{2,1,0:T(8,128)S(1)}, f32[8,96,256]{2,1,0:T(8,128)S(1)}, u32[]{:S(2)}, u32[]{:S(2)}) collective-permute-start(f32[8,96,256]{2,1,0:T(8,128)S(1)} %add_add_fusion), channel_id=1, source_target_pairs={{0,16},{16,0},{32,48},{48,32},{64,80},{80,64},{96,112},{112,96},{1... | collective-permute-start | bytes 2359304 | tf_op jit(solution)/shard_map/ppermute | solution.py:26
  187.2 8.5 %collective-permute-start.12 = (f32[8,48,256]{2,1,0:T(8,128)S(1)}, f32[8,48,256]{2,1,0:T(8,128)S(1)}, u32[]{:S(2)}, u32[]{:S(2)}) collective-permute-start(f32[8,48,256]{2,1,0:T(8,128)S(1)} %get-tuple-element.81), channel_id=1, source_target_pairs={{0,32},{16,48},{32,64},{48,80},{64,96},{80,112},{96,0},{112,16},{1... | collective-permute-start | bytes 1179656 | tf_op jit(solution)/shard_map/ppermute | solution.py:24
  187.4 10.1 %collective-permute-start.16 = (f32[8,48,256]{2,1,0:T(8,128)S(1)}, f32[8,48,256]{2,1,0:T(8,128)S(1)}, u32[]{:S(2)}, u32[]{:S(2)}) collective-permute-start(f32[8,48,256]{2,1,0:T(8,128)S(1)} %get-tuple-element.86), channel_id=1, source_target_pairs={{0,96},{16,112},{32,0},{48,16},{64,32},{80,48},{96,64},{112,80},{1... | collective-permute-start | bytes 1179656 | tf_op jit(solution)/shard_map/ppermute | solution.py:24
  189.9 13.3 %collective-permute-start.14 = (f32[8,48,256]{2,1,0:T(8,128)S(1)}, f32[8,48,256]{2,1,0:T(8,128)}, u32[]{:S(2)}, u32[]{:S(2)}) collective-permute-start(f32[8,48,256]{2,1,0:T(8,128)S(1)} %get-tuple-element.82), channel_id=1, source_target_pairs={{0,96},{16,112},{32,0},{48,16},{64,32},{80,48},{96,64},{112,80},{1... | collective-permute-start | bytes 1179656 | tf_op jit(solution)/shard_map/ppermute | solution.py:24
  196.5 8.4 %collective-permute-start.13 = (f32[8,48,256]{2,1,0:T(8,128)}, f32[8,48,256]{2,1,0:T(8,128)}, u32[]{:S(2)}, u32[]{:S(2)}) collective-permute-start(f32[8,48,256]{2,1,0:T(8,128)} %add.183), channel_id=1, source_target_pairs={{0,32},{16,48},{32,64},{48,80},{64,96},{80,112},{96,0},{112,16},{1... | collective-permute-start | bytes 1179656 | tf_op jit(solution)/shard_map/ppermute | solution.py:24
  196.5 16.3 %collective-permute-start.15 = (f32[8,48,256]{2,1,0:T(8,128)S(1)}, f32[8,48,256]{2,1,0:T(8,128)}, u32[]{:S(2)}, u32[]{:S(2)}) collective-permute-start(f32[8,48,256]{2,1,0:T(8,128)S(1)} %get-tuple-element.84), channel_id=1, source_target_pairs={{0,32},{16,48},{32,64},{48,80},{64,96},{80,112},{96,0},{112,16},{1... | collective-permute-start | bytes 1179656 | tf_op jit(solution)/shard_map/ppermute | solution.py:24
  198.4 14.5 %collective-permute-start.17 = (f32[8,48,256]{2,1,0:T(8,128)}, f32[8,48,256]{2,1,0:T(8,128)}, u32[]{:S(2)}, u32[]{:S(2)}) collective-permute-start(f32[8,48,256]{2,1,0:T(8,128)} %add.187), channel_id=1, source_target_pairs={{0,96},{16,112},{32,0},{48,16},{64,32},{80,48},{96,64},{112,80},{1... | collective-permute-start | bytes 1179656 | tf_op jit(solution)/shard_map/ppermute | solution.py:24
  214.1 104.1 %all-gather.7.cloned.1.call-start = ((), (), s32[]{:S(2)}) async-start(), calls=%async_computation.5 | async-start | bytes 6553600 | tf_op jit(solution)/shard_map/all_gather | solution.py:260
  215.3 5.1 %collective-permute-start.21 = (f32[8,16,256]{2,1,0:T(8,128)S(1)}, f32[8,16,256]{2,1,0:T(8,128)S(1)}, u32[]{:S(2)}, u32[]{:S(2)}) collective-permute-start(f32[8,16,256]{2,1,0:T(8,128)S(1)} %get-tuple-element.99), channel_id=1, source_target_pairs={{0,32},{16,48},{32,64},{48,80},{64,96},{80,112},{96,0},{112,16},{1... | collective-permute-start | bytes 393224 | tf_op jit(solution)/shard_map/ppermute | solution.py:24
  215.9 7.0 %collective-permute-start.24 = (f32[8,48,256]{2,1,0:T(8,128)S(1)}, f32[8,48,256]{2,1,0:T(8,128)S(1)}, u32[]{:S(2)}, u32[]{:S(2)}) collective-permute-start(f32[8,48,256]{2,1,0:T(8,128)S(1)} %add_add_fusion.2), channel_id=1, source_target_pairs={{0,16},{16,0},{32,48},{48,32},{64,80},{80,64},{96,112},{112,96},{1... | collective-permute-start | bytes 1179656 | tf_op jit(solution)/shard_map/ppermute | solution.py:26
  216.4 6.1 %collective-permute-start.22 = (f32[8,16,256]{2,1,0:T(8,128)S(1)}, f32[8,16,256]{2,1,0:T(8,128)S(1)}, u32[]{:S(2)}, u32[]{:S(2)}) collective-permute-start(f32[8,16,256]{2,1,0:T(8,128)S(1)} %get-tuple-element.98), channel_id=1, source_target_pairs={{0,64},{16,80},{32,96},{48,112},{64,0},{80,16},{96,32},{112,48},{1... | collective-permute-start | bytes 393224 | tf_op jit(solution)/shard_map/ppermute | solution.py:24
  219.1 3.8 %collective-permute-start.23 = (f32[8,16,256]{2,1,0:T(8,128)S(1)}, f32[8,16,256]{2,1,0:T(8,128)S(1)}, u32[]{:S(2)}, u32[]{:S(2)}) collective-permute-start(f32[8,16,256]{2,1,0:T(8,128)S(1)} %get-tuple-element.97), channel_id=1, source_target_pairs={{0,96},{16,112},{32,0},{48,16},{64,32},{80,48},{96,64},{112,80},{1... | collective-permute-start | bytes 393224 | tf_op jit(solution)/shard_map/ppermute | solution.py:24
  220.4 6.6 %copy-start = (f32[8,96,256]{2,1,0:T(8,128)S(1)}, f32[8,96,256]{2,1,0:T(8,128)}, u32[]{:S(2)}) copy-start(f32[8,96,256]{2,1,0:T(8,128)} %add.182.refs_0_.refs_1_) | copy-start | bytes 2359300
  224.2 27.2 %collective-permute-start.26 = (f32[8,160,256]{2,1,0:T(8,128)}, f32[8,160,256]{2,1,0:T(8,128)}, u32[]{:S(2)}, u32[]{:S(2)}) collective-permute-start(f32[8,160,256]{2,1,0:T(8,128)} %pad_maximum_fusion.refs_8_.refs_9_), channel_id=1, source_target_pairs={{0,2},{1,3},{2,0},{3,1},{4,6},{5,7},{6,4},{7,5},{8,10},{9,11},{10,... | collective-permute-start | bytes 3932168 | tf_op jit(solution)/shard_map/ppermute | solution.py:28
  227.0 41.2 %collective-permute-start.19 = (f32[8,96,256]{2,1,0:T(8,128)S(1)}, f32[8,96,256]{2,1,0:T(8,128)S(1)}, u32[]{:S(2)}, u32[]{:S(2)}) collective-permute-start(f32[8,96,256]{2,1,0:T(8,128)S(1)} %copy-done), channel_id=1, source_target_pairs={{0,2},{1,3},{2,0},{3,1},{4,6},{5,7},{6,4},{7,5},{8,10},{9,11},{10,... | collective-permute-start | bytes 2359304 | tf_op jit(solution)/shard_map/ppermute | solution.py:28
  227.3 49.6 %collective-permute-start.25 = (f32[8,160,256]{2,1,0:T(8,128)}, f32[8,160,256]{2,1,0:T(8,128)}, u32[]{:S(2)}, u32[]{:S(2)}) collective-permute-start(f32[8,160,256]{2,1,0:T(8,128)} %pad_maximum_fusion.refs_8_.refs_9_), channel_id=1, source_target_pairs={{0,1},{1,0},{2,3},{3,2},{4,5},{5,4},{6,7},{7,6},{8,9},{9,8},{10,11... | collective-permute-start | bytes 3932168 | tf_op jit(solution)/shard_map/ppermute | solution.py:29
  251.4 25.4 %collective-permute-start.27 = (f32[8,160,256]{2,1,0:T(8,128)}, f32[8,160,256]{2,1,0:T(8,128)}, u32[]{:S(2)}, u32[]{:S(2)}) collective-permute-start(f32[8,160,256]{2,1,0:T(8,128)} %collective-permute-done.26.refs_12_.refs_13_), channel_id=1, source_target_pairs={{0,1},{1,0},{2,3},{3,2},{4,5},{5,4},{6,7},{7,6},{8,9},{9,8},{10,11... | collective-permute-start | bytes 3932168 | tf_op jit(solution)/shard_map/ppermute | solution.py:29
  264.5 10.4 %collective-permute-start.18 = (f32[8,96,256]{2,1,0:T(8,128)S(1)}, f32[8,96,256]{2,1,0:T(8,128)S(1)}, u32[]{:S(2)}, u32[]{:S(2)}) collective-permute-start(f32[8,96,256]{2,1,0:T(8,128)S(1)} %copy-done), channel_id=1, source_target_pairs={{0,1},{1,0},{2,3},{3,2},{4,5},{5,4},{6,7},{7,6},{8,9},{9,8},{10,11... | collective-permute-start | bytes 2359304 | tf_op jit(solution)/shard_map/ppermute | solution.py:29
  268.2 8.6 %collective-permute-start.20 = (f32[8,96,256]{2,1,0:T(8,128)S(1)}, f32[8,96,256]{2,1,0:T(8,128)S(1)}, u32[]{:S(2)}, u32[]{:S(2)}) collective-permute-start(f32[8,96,256]{2,1,0:T(8,128)S(1)} %collective-permute-done.19.refs_4_.refs_5_), channel_id=1, source_target_pairs={{0,1},{1,0},{2,3},{3,2},{4,5},{5,4},{6,7},{7,6},{8,9},{9,8},{10,11... | collective-permute-start | bytes 2359304 | tf_op jit(solution)/shard_map/ppermute | solution.py:29
Sparse Core Ops, SparseCore 0:
  179.3 33.3 reduce-scatter.1
  214.4 44.7 all-gather.4
  261.0 57.1 all-gather.6

commit v2 on v1

v2 whole, which is shorter than its diff:
```python
import functools
import math

import jax
import jax.numpy as jnp
import numpy as np
from jax import lax
from jax.experimental import pallas as pl
from jax.experimental.pallas import tpu as pltpu
from jax.sharding import PartitionSpec as P

S = 1024
NT = 512
NF = 32
C = 256
R3, R2, R1 = 96, 64, 96
HALF, QUARTER = R3 // 2, R2 // 4
VMEM = 50 << 20


def shift(x, axis, by=1):
    if axis == "z":
        return lax.ppermute(x, "row", [(i, (i + by) % 4) for i in range(4)])
    if axis == "y":
        return lax.ppermute(x, "freq", [(i, (i + 2 * by) % 8) for i in range(8)])
    if axis == "x_lo":
        return lax.ppermute(x, "freq", [(i, i ^ 1) for i in range(8)])
    if axis == "x_hi":
        return lax.ppermute(x, "col", [(i, i ^ 2) for i in range(4)])
    return lax.ppermute(x, "col", [(i, i ^ 1) for i in range(4)])


def exchange(x, axis):
    if axis == "z":
        return lax.all_to_all(x, "row", split_axis=0, concat_axis=0, tiled=True)
    groups = [[2 * j + i for j in range(4)] for i in range(2)]
    return lax.all_to_all(x, "freq", split_axis=0, concat_axis=0, tiled=True, axis_index_groups=groups)


def together(*values):
    return lax.optimization_barrier(values)


def cost(us):
    return pl.CostEstimate(flops=0, bytes_accessed=int(us * 3.6e6), transcendentals=0)


def call(kernel, index, operands, grid, in_specs, out_specs, out_shape, us, scratch_shapes=()):
    return pl.pallas_call(
        kernel,
        grid_spec=pltpu.PrefetchScalarGridSpec(
            num_scalar_prefetch=1, grid=grid, in_specs=in_specs, out_specs=out_specs, scratch_shapes=scratch_shapes
        ),
        out_shape=out_shape,
        compiler_params=pltpu.CompilerParams(vmem_limit_bytes=VMEM),
        cost_estimate=cost(us),
    )(index, *operands)


def f32(*shape):
    return jax.ShapeDtypeStruct(shape, jnp.float32)


def tables():
    k = np.arange(NF) + 1
    phase = np.outer(k, np.arange(NT)) % NT * (2.0 * math.pi / NT)
    scale = 1.0 / math.sqrt(NT * math.sqrt(S))
    full = np.stack([np.cos(phase), -np.sin(phase)]) * scale
    full = full.reshape(2, 8, 4, NT).transpose(1, 0, 2, 3).reshape(8, 8, NT).astype(np.float32)
    one, two, three = [], [], []
    u = np.arange(16)
    for f in range(8):
        y, x_lo = f // 2, f % 2
        by_y = [2 * ((y + ry) % 4) + (x_lo + q) % 2 for ry in range(4) for q in range(2)]
        by_q = [2 * y_to + (x_lo + q) % 2 for q in range(2) for y_to in range(4)]
        by_y, by_q = full[by_y].reshape(64, NT), full[by_q].reshape(64, NT)
        near, far = 64 * f + np.arange(64), 64 * (f ^ 1) + np.arange(64)
        one.append(by_y[:, near])
        three.append(by_y[:, np.stack([near.reshape(4, 16), far.reshape(4, 16)], axis=1).reshape(-1)])
        for z in range(4):
            t = [128 * ((y - r) % 4) + 64 * x_lo + 16 * z + u for r in range(4)]
            two.append(by_q[:, np.concatenate(t)])
    return np.stack(one), np.stack(two), np.stack(three)


def staged(pairs, stage_ref, in_sem, out_sem):
    ins = [pltpu.make_async_copy(a, stage_ref.at[n], in_sem.at[n]) for n, (a, _) in enumerate(pairs)]
    outs = [pltpu.make_async_copy(stage_ref.at[n], b, out_sem.at[n]) for n, (_, b) in enumerate(pairs)]
    for copy in ins:
        copy.start()
    for copy_in, copy_out in zip(ins, outs):
        copy_in.wait()
        copy_out.start()
    for copy in outs:
        copy.wait()


def pack_kernel(index, x_ref, out_ref, *scratch, views):
    staged(views(index, x_ref, out_ref), *scratch)


def stage(n, shape):
    return [pltpu.VMEM((n, *shape), jnp.float32), pltpu.SemaphoreType.DMA((n,)), pltpu.SemaphoreType.DMA((n,))]


def pack(index, blocks, views, n, piece, shape, us):
    anywhere = pl.BlockSpec(memory_space=pl.ANY)
    return call(
        functools.partial(pack_kernel, views=views),
        index,
        (blocks,),
        (1,),
        [anywhere],
        anywhere,
        f32(*shape),
        us,
        stage(n, piece),
    )


def join_kernel(far_ref, joined_ref, out_ref, *scratch):
    del joined_ref
    staged([(far_ref.at[g], out_ref.at[g, 1]) for g in range(4)], *scratch)


def join(joined, far):
    anywhere = pl.BlockSpec(memory_space=pl.ANY)
    return pl.pallas_call(
        join_kernel,
        in_specs=[anywhere] * 2,
        out_specs=anywhere,
        out_shape=f32(*joined.shape),
        scratch_shapes=stage(4, far.shape[1:]),
        input_output_aliases={1: 0},
        compiler_params=pltpu.CompilerParams(vmem_limit_bytes=VMEM),
        cost_estimate=cost(3),
    )(far, joined)


def rows_at(start, size):
    return pl.ds(pl.multiple_of(start, 8), size)


def transform(w_ref, samples, store, rows):
    w = w_ref[0]
    wh = w.astype(jnp.bfloat16)
    wl = (w - wh.astype(jnp.float32)).astype(jnp.bfloat16)
    wcat = jnp.concatenate([wh, wh, wl], axis=1)
    for s in range(rows):
        x = samples(s)
        xh = x.astype(jnp.bfloat16)
        xl = (x - xh.astype(jnp.float32)).astype(jnp.bfloat16)
        xcat = jnp.concatenate([xh, xl, xh], axis=0)
        store(s, jnp.dot(wcat, xcat, preferred_element_type=jnp.float32))


def dft_owner_kernel(rows, _, w_ref, x_ref, *outs):
    def samples(s):
        return jnp.concatenate([x_ref[j, :, s, :] for j in range(x_ref.shape[0])], axis=0)

    def store(s, res):
        for i, out in enumerate(outs):
            out[:, s, :] = res[8 * i : 8 * i + 8]

    transform(w_ref, samples, store, rows)


def dft_by_owner(index, w, x, us):
    n, _, rows, _ = x.shape
    block = 16
    flat = call(
        functools.partial(dft_owner_kernel, block),
        index,
        (w, x),
        (rows // block,),
        [
            pl.BlockSpec((1, 64, w.shape[2]), lambda g, i: (i[0], 0, 0)),
            pl.BlockSpec((n, 16, block, C), lambda g, i: (0, 0, g, 0)),
        ],
        [pl.BlockSpec((8, block, C), lambda g, i: (0, g, 0))] * 8,
        [f32(8, rows, C)] * 8,
        us,
    )
    return [flat[2 * r : 2 * r + 2] for r in range(4)]


def dft_row_kernel(rows, _, w_ref, *refs):
    pieces, outs = refs[:4], refs[4:]

    def samples(s):
        return jnp.concatenate([p[:, 0, s, :] for p in pieces], axis=0)

    def store(s, res):
        for q in range(2):
            outs[q][0, :, s, :] = res[32 * q : 32 * q + 32]

    transform(w_ref, samples, store, rows)


def dft_by_row(index, w, blocks, pieces):
    at = R3 // QUARTER
    return call(
        functools.partial(dft_row_kernel, QUARTER),
        index,
        (w, blocks, *pieces),
        (4,),
        [
            pl.BlockSpec((1, 64, 64), lambda g, i: (i[0], 0, 0)),
            pl.BlockSpec((16, 1, QUARTER, C), lambda g, i: (0, g, at + i[1], 0)),
        ]
        + [pl.BlockSpec((16, 1, QUARTER, C), lambda g, i: (0, g, 0, 0))] * 3,
        [pl.BlockSpec((1, 32, QUARTER, C), lambda g, i: (g, 0, 0, 0))] * 2,
        [f32(4, 32, QUARTER, C)] * 2,
        7,
    )


def reduce_ring(slots, axis):
    up0 = shift(slots[2][0], axis, 1)
    down1 = shift(slots[2][1], axis, -1)
    up1 = shift(slots[1][1], axis, 1)
    down0 = shift(slots[3][0], axis, -1)
    up0 = shift(slots[1][0] + up0, axis, 1)
    down1 = shift(slots[3][1] + down1, axis, -1)
    return [slots[0][0] + up0 + down0, slots[0][1] + up1 + down1]


def near_z(x):
    return shift(x, "z", 1), shift(x, "z", -1)


def across_z(below, above):
    return shift(below[:4], "z", 1), shift(above[4:], "z", -1)


def split(x):
    hi = x.astype(jnp.bfloat16)
    return hi, (x - hi.astype(jnp.float32)).astype(jnp.bfloat16)


def dots(a, b, out, total):
    def dot(x, y):
        return jnp.dot(x, y, preferred_element_type=jnp.float32)

    rr, ri = total
    ii, ir = jnp.zeros((256, C), jnp.float32), jnp.zeros((256, C), jnp.float32)
    for (arh, arl, aih, ail), (brh, brl, bih, bil) in zip(a, b):
        rr += dot(arh, brh) + dot(arh, brl) + dot(arl, brh)
        ii += dot(aih, bih) + dot(aih, bil) + dot(ail, bih)
        ri += dot(arh, bih) + dot(arh, bil) + dot(arl, bih)
        ir += dot(aih, brh) + dot(aih, brl) + dot(ail, brh)
    out[0, 0] = rr - ii
    out[1, 0] = ri + ir


def near_kernel(segments, index, *refs):
    n = len(segments)
    left, right = refs[: 8 * n], refs[8 * n : 14 * n]
    out, kept, a_ref, b_ref = refs[14 * n :]
    col, z = index[0], index[1]
    for i, rows in enumerate(segments):
        for part in range(2):
            for e in range(4):
                hi, lo = split(left[8 * i + 2 * e + part][0])
                a_ref[col ^ e, 2 * part, rows] = hi
                a_ref[col ^ e, 2 * part + 1, rows] = lo
            for t in range(3):
                hi, lo = split(right[6 * i + 2 * t + part][0])
                b_ref[t, 2 * part, rows] = hi
                b_ref[t, 2 * part + 1, rows] = lo
    zero = jnp.zeros((256, C), jnp.float32)
    a = [[a_ref[(z + r) % 4, j] for j in range(4)] for r in (0, 1, 3)]
    dots(a, [[b_ref[t, j] for j in range(4)] for t in range(3)], out, (zero, zero))
    kept[0] = a_ref[(z + 2) % 4]


def far_kernel(segments, _, total, kept, *refs):
    out, b_ref = refs[-2:]
    for i, rows in enumerate(segments):
        for part in range(2):
            hi, lo = split(refs[2 * i + part][0])
            b_ref[2 * part, rows] = hi
            b_ref[2 * part + 1, rows] = lo
    a, b = [kept[0, j] for j in range(4)], [b_ref[j] for j in range(4)]
    dots([a], [b], out, (total[0, 0], total[1, 0]))


def product(index, left, right, across, starts):
    sizes = [part[0].shape[1] for part in left]
    segments = [slice(a, a + b) for a, b in zip(starts, sizes)]

    def spec(rows, first):
        return pl.BlockSpec((1, rows, C), lambda g, _: (first + g, 0, 0))

    def both(groups):
        operands, specs = [], []
        for arrays, rows in zip(groups, sizes):
            for array in arrays:
                operands += [array, array]
                specs += [spec(rows, 0), spec(rows, 4)]
        return operands, specs

    left, left_specs = both(left)
    right, right_specs = both(right)
    out_spec = pl.BlockSpec((2, 1, 256, C), lambda g, _: (0, g, 0, 0))
    kept_spec = pl.BlockSpec((1, 4, 256, C), lambda g, _: (g, 0, 0, 0))
    total, kept = call(
        functools.partial(near_kernel, segments),
        index,
        left + right,
        (4,),
        left_specs + right_specs,
        [out_spec, kept_spec],
        [f32(2, 4, 256, C), jax.ShapeDtypeStruct((4, 4, 256, C), jnp.bfloat16)],
        11,
        [pltpu.VMEM((4, 4, 256, C), jnp.bfloat16), pltpu.VMEM((3, 4, 256, C), jnp.bfloat16)],
    )
    return call(
        functools.partial(far_kernel, segments),
        index,
        [total, kept] + [array for pair in across for array in pair],
        (4,),
        [out_spec, kept_spec] + [spec(rows, 0) for rows in sizes for _ in range(2)],
        out_spec,
        f32(2, 4, 256, C),
        4,
        [pltpu.VMEM((4, 256, C), jnp.bfloat16)],
    )


def local(x):
    f = lax.axis_index("freq")
    y, x_lo = f // 2, f % 2
    z = lax.axis_index("row")
    col = lax.axis_index("col")
    one, two, three = tables()
    blocks = x.reshape(16, 4, 256, C)
    place = jnp.stack([f, y, x_lo, jnp.int32(R3 + R2)])

    def for_partner(index, x_ref, out_ref):
        rows = rows_at(HALF * (1 - index[2]), HALF)
        return [(x_ref.at[:, g, rows, :], out_ref.at[g]) for g in range(4)]

    def for_self(index, x_ref, out_ref):
        rows = rows_at(HALF * index[2], HALF)
        return [(x_ref.at[:, g, rows, :], out_ref.at[g, 0]) for g in range(4)]

    def for_z(index, x_ref, out_ref):
        return [(x_ref.at[:, g, rows_at(index[3], R1), :], out_ref.at[g]) for g in range(4)]

    def for_y(r):
        def views(index, x_ref, out_ref):
            rows = rows_at(R3 + QUARTER * ((index[1] + r) % 4), QUARTER)
            return [(x_ref.at[:, :, rows, :], out_ref)]

        return pack(place, blocks, views, 1, (16, 4, QUARTER, C), (16, 4, QUARTER, C), 2)

    third_far = shift(pack(place, blocks, for_partner, 4, (16, HALF, C), (4, 16, HALF, C), 3), "x_lo")
    first = exchange(pack(place, blocks, for_z, 4, (16, R1, C), (4, 16, R1, C), 5), "z")
    second = [shift(for_y(r), "y", r) for r in (1, 2, 3)]
    third = pack(place, blocks, for_self, 4, (16, HALF, C), (4, 2, 16, HALF, C), 3)
    first, second, third, third_far = together(first, second, third, third_far)

    third = exchange(join(third, third_far), "z")
    slots = dft_by_owner(place, one, first, 9)
    slots, second = together(slots, second)
    mine1, other1 = reduce_ring(slots, "y")
    mine, other = dft_by_row(jnp.stack([4 * f + z, y]), two, blocks, second)
    own2 = mine + shift(other, "x_lo")
    mine1, other1, own2, third = together(mine1, other1, own2, third)

    own2 = jnp.sum(exchange(own2, "z"), axis=0)
    own1 = mine1 + shift(other1, "x_lo")
    below1, above1 = near_z(own1)
    far1 = shift(own1, "x_hi")
    mine3, other3 = reduce_ring(dft_by_owner(place, three, third.reshape(8, 16, HALF, C), 7), "y")
    own2 = exchange(own2.reshape(4, 8, QUARTER, C), "y")
    own2 = jnp.transpose(own2, (1, 0, 2, 3)).reshape(8, R2, C)
    own1, below1, above1, far1, own2, mine3, other3 = together(own1, below1, above1, far1, own2, mine3, other3)

    other3 = shift(other3, "x_lo")
    below2, above2 = near_z(own2)
    across1 = across_z(below1, above1)
    far2 = shift(own2, "x_hi")
    own3 = jnp.where(x_lo == 0, jnp.concatenate([mine3, other3], axis=1), jnp.concatenate([other3, mine3], axis=1))
    own3, below2, above2, across1, far2 = together(own3, below2, above2, across1, far2)

    below3, above3 = near_z(own3)
    across2 = across_z(below2, above2)
    far3 = shift(own3, "x_hi")
    across3 = across_z(below3, above3)

    def columns(own, far):
        return [own, shift(own, "core"), far, shift(far, "core")]

    left = [columns(own3, far3), columns(own2, far2), columns(own1, far1)]
    right = [(own3, above3, below3), (own2, above2, below2), (own1, above1, below1)]
    return product(jnp.stack([col, z]), left, right, [across3, across2, across1], (0, R3, R3 + R2))


def solution(mesh):
    in_specs = (P(("freq", "row"), None, "col"),)
    out_specs = P(None, "freq", "row", "col")
    return jax.shard_map(local, mesh=mesh, in_specs=in_specs, out_specs=out_specs, check_vma=False)
```

time: 337 us -> 295 us (0.88)
  waiting for transfers between devices: 186 us -> 130 us
  Pallas kernels: 33.8 us -> 59.9 us
  between operations: 13.4 us -> 0.41 us
  starting transfers between devices: 69.3 us -> 77.9 us
  local copies, waits for them, and re-layouts: 21.3 us -> 13.7 us
    all_gather x2 -> x0, waiting for transfers between devices: 41.4 us -> none  [local(): right.append(lax.all_gather(part, 'row', axis=0, tiled=False))]
    pallas_call x4 -> x12, Pallas kernels: 33.8 us -> 59.9 us  [the longest x11 58 us: call(): pl.pallas_call(kernel, grid_spec=pltpu.PrefetchScalarGridSpec(num_scalar_...]
    ppermute x18 -> x15, waiting for transfers between devices: 107 us -> 89.2 us  [shift(): return lax.ppermute(x, 'freq', [(i, (i + 2 * by) % 8) for i in range(8)])]
    ppermute x0 -> x12, starting transfers between devices: none -> 17.7 us  [shift(): return lax.ppermute(x, 'row', [(i, (i + by) % 4) for i in range(4)])]
    ppermute x0 -> x12, waiting for transfers between devices: none -> 17 us  [shift(): return lax.ppermute(x, 'row', [(i, (i + by) % 4) for i in range(4)])]
    ppermute x2 -> x3, waiting for transfers between devices: 20.7 us -> 4.08 us  [shift(): return lax.ppermute(x, 'col', [(i, i ^ 2) for i in range(4)])]
    ppermute x4 -> x6, starting transfers between devices: 26.9 us -> 14 us  [shift(): return lax.ppermute(x, 'col', [(i, i ^ 1) for i in range(4)])]
    transpose x3 -> x1, local copies, waits for them, and re-layouts: 10.1 us -> 0.03 us  [local(): own2 = jnp.transpose(own2, (1, 0, 2, 3)).reshape(8, R2, C)]
  transfers between devices with their start and end apart: 33 -> 44, of which waited for: 18 -> 18; matrix products, arithmetic and copies ran while one was open for 6% -> 6% of each run, Pallas kernels for 7% -> 16%
where the time goes in v2:
time: 295 us; the launch traced here: 294 us
  waiting for transfers between devices  130 us (44%)
  starting transfers between devices  77.9 us (26%)
  Pallas kernels  59.9 us (20%)
  local copies, waits for them, and re-layouts  13.7 us (5%)
  other arithmetic  12.7 us (4%)
    ppermute x15, waiting for transfers between devices, shift(): return lax.ppermute(x, 'freq', [(i, (i + 2 * by) % 8) for i in range(8)])  89.2 us
    pallas_call x11, Pallas kernels, call(): pl.pallas_call(kernel, grid_spec=pltpu.PrefetchScalarGridSpec(num_scalar_...  58 us
    ppermute x12, starting transfers between devices, shift(): return lax.ppermute(x, 'row', [(i, (i + by) % 4) for i in range(4)])  17.7 us
    ppermute x12, waiting for transfers between devices, shift(): return lax.ppermute(x, 'row', [(i, (i + by) % 4) for i in range(4)])  17 us
    all_to_all x3, starting transfers between devices, exchange(): return lax.all_to_all(x, 'row', split_axis=0, concat_axis=0, tiled=True)  16.2 us
    ppermute x15, starting transfers between devices, shift(): return lax.ppermute(x, 'freq', [(i, (i + 2 * by) % 8) for i in range(8)])  15.5 us
    ppermute x4, waiting for transfers between devices, shift(): return lax.ppermute(x, 'freq', [(i, i ^ 1) for i in range(8)])  14.2 us
    ppermute x6, starting transfers between devices, shift(): return lax.ppermute(x, 'col', [(i, i ^ 1) for i in range(4)])  14 us
  transfers between devices with their start and end apart: 44, of which 18 were waited for; matrix products, arithmetic and copies ran while one was open for 6% of the time, Pallas kernels for 16%

profile of v2, /device:TPU:1, one launch (start us, length us, event | category | flops | bytes accessed | tf_op | source)
XLA Modules:
  0.0 294.1 jit_solution(2474826560202010573)
XLA Ops:
  0.1 5.7 %shard_map.46 = f32[4,16,96,256]{3,2,1,0:T(8,128)} custom-call(s32[4]{0:T(128)S(1)} %pad_add_fusion.1.index._, f32[16,4,256,256]{3,2,1,0:T(8,128)} %bitcast.19), custom_call_target="tpu_custom_call" | custom-call | bytes 18000000 | tf_op jit(solution)/shard_map/pallas_call | solution.py:49
  5.8 5.9 %all-to-all-start = ((f32[4,16,96,256]{3,2,1,0:T(8,128)}), f32[4,16,96,256]{3,2,1,0:T(8,128)}, u32[]{:S(2)}, u32[]{:S(2)}) async-start(f32[4,16,96,256]{3,2,1,0:T(8,128)} %shard_map.46), calls=%async_computation | async-start | bytes 12582912 | tf_op jit(solution)/shard_map/all_to_all | solution.py:35
  11.7 2.5 shard_map.51
  14.2 1.6 collective-permute-start.3
  15.8 1.9 shard_map.47
  17.7 1.4 collective-permute-start
  19.1 1.9 shard_map.48
  20.9 2.7 collective-permute-start.1
  23.6 1.9 shard_map.49
  25.5 1.1 collective-permute-start.2
  26.6 3.4 %shard_map.50.joined_ref = f32[4,2,16,48,256]{4,3,2,1,0:T(8,128)} custom-call(s32[4]{0:T(128)S(1)} %pad_add_fusion.1.index._, f32[16,4,256,256]{3,2,1,0:T(8,128)} %bitcast.24), custom_call_target="tpu_custom_call" | custom-call | bytes 10800000 | tf_op jit(solution)/shard_map/pallas_call | solution.py:49
  30.0 12.9 %collective-permute-done.refs_1_ = f32[16,4,16,256]{3,2,1,0:T(8,128)S(1)} collective-permute-done((f32[16,4,16,256]{3,2,1,0:T(8,128)S(1)}, f32[16,4,16,256]{3,2,1,0:T(8,128)S(1)}, u32[]{:S(2)}, u32[]{:S(2)}) %collective-permute-start) | collective-permute-done | bytes 1048608 | tf_op jit(solution)/shard_map/ppermute | solution.py:25
  42.9 1.0 copy-done.3
  43.9 22.6 %collective-permute-done.1.refs_2_ = f32[16,4,16,256]{3,2,1,0:T(8,128)S(1)} collective-permute-done((f32[16,4,16,256]{3,2,1,0:T(8,128)S(1)}, f32[16,4,16,256]{3,2,1,0:T(8,128)S(1)}, u32[]{:S(2)}, u32[]{:S(2)}) %collective-permute-start.1) | collective-permute-done | bytes 1048608 | tf_op jit(solution)/shard_map/ppermute | solution.py:25
  66.5 1.0 copy-done.5
  68.1 1.0 copy-done.19
  69.1 14.1 %collective-permute-done.3.far_ref = f32[4,16,48,256]{3,2,1,0:T(8,128)S(1)} collective-permute-done((f32[4,16,48,256]{3,2,1,0:T(8,128)S(1)}, f32[4,16,48,256]{3,2,1,0:T(8,128)S(1)}, u32[]{:S(2)}, u32[]{:S(2)}) %collective-permute-start.3) | collective-permute-done | bytes 3145760 | tf_op jit(solution)/shard_map/ppermute | solution.py:27
  83.6 1.9 shard_map.54
  85.6 5.4 %all-to-all-start.1 = ((f32[4,2,16,48,256]{4,3,2,1,0:T(8,128)}), f32[4,2,16,48,256]{4,3,2,1,0:T(8,128)}, u32[]{:S(2)}, u32[]{:S(2)}) async-start(f32[4,2,16,48,256]{4,3,2,1,0:T(8,128)} %shard_map.54), calls=%async_computation.1 | async-start | bytes 12582912 | tf_op jit(solution)/shard_map/all_to_all | solution.py:35
  91.1 9.8 %shard_map.52 = (f32[8,96,256]{2,1,0:T(8,128)S(1)}, f32[8,96,256]{2,1,0:T(8,128)S(1)}, f32[8,96,256]{2,1,0:T(8,128)S(1)}, f32[8,96,256]{2,1,0:T(8,128)S(1)}, f32...) custom-call(s32[4]{0:T(128)S(1)} %pad_add_fusion.1.index._, ...), custom_call_target="tpu_custom_call" | custom-call | bytes 32400000 | tf_op jit(solution)/shard_map/pallas_call | solution.py:49
  100.9 2.8 collective-permute-start.8
  103.8 7.0 %shard_map.53 = (f32[4,32,16,256]{3,2,1,0:T(8,128)}, f32[4,32,16,256]{3,2,1,0:T(8,128)}) custom-call(s32[2]{0:T(128)S(1)} %pad_add_fusion.2._, f32[32,64,64]{2,1,0:T(8,128)S(1)} %copy-done.2, f32[16,4,256,256]{3,2,1,0:T(8,128)} %bitcast.25, f32[16,4,16,256]{3,2,1,0:T(8,128)S(1)} %copy-done.4, f32[16,4,16,256]{3,2,1,0:T(8,128)S(1)} %copy-done.6, ...), custom_call_target="tpu_custom_call" | custom-call | bytes 25200000 | tf_op jit(solution)/shard_map/pallas_call | solution.py:49
  110.8 1.2 collective-permute-start.10
  112.1 7.3 %collective-permute-done.8 = f32[8,96,256]{2,1,0:T(8,128)S(1)} collective-permute-done((f32[8,96,256]{2,1,0:T(8,128)}, f32[8,96,256]{2,1,0:T(8,128)S(1)}, u32[]{:S(2)}, u32[]{:S(2)}) %collective-permute-start.8) | collective-permute-done | bytes 786464 | tf_op jit(solution)/shard_map/ppermute | solution.py:25
  119.5 3.5 %collective-permute-start.9 = (f32[8,96,256]{2,1,0:T(8,128)S(1)}, f32[8,96,256]{2,1,0:T(8,128)S(1)}, u32[]{:S(2)}, u32[]{:S(2)}) collective-permute-start(f32[8,96,256]{2,1,0:T(8,128)S(1)} %add.55), channel_id=1, source_target_pairs={{0,96},{16,112},{32,0},{48,16},{64,32},{80,48},{96,64},{112,80},{1... | collective-permute-start | bytes 2359304 | tf_op jit(solution)/shard_map/ppermute | solution.py:25
  123.1 7.3 %collective-permute-done.4 = f32[8,96,256]{2,1,0:T(8,128)S(1)} collective-permute-done((f32[8,96,256]{2,1,0:T(8,128)S(1)}, f32[8,96,256]{2,1,0:T(8,128)S(1)}, u32[]{:S(2)}, u32[]{:S(2)}) %collective-permute-start.4) | collective-permute-done | bytes 786464 | tf_op jit(solution)/shard_map/ppermute | solution.py:25
  130.6 16.7 %collective-permute-done.7 = f32[8,96,256]{2,1,0:T(8,128)S(1)} collective-permute-done((f32[8,96,256]{2,1,0:T(8,128)S(1)}, f32[8,96,256]{2,1,0:T(8,128)S(1)}, u32[]{:S(2)}, u32[]{:S(2)}) %collective-permute-start.7) | collective-permute-done | bytes 786464 | tf_op jit(solution)/shard_map/ppermute | solution.py:25
  147.2 1.0 add_add_fusion
  148.3 6.1 %collective-permute-done.6 = f32[8,96,256]{2,1,0:T(8,128)S(1)} collective-permute-done((f32[8,96,256]{2,1,0:T(8,128)S(1)}, f32[8,96,256]{2,1,0:T(8,128)S(1)}, u32[]{:S(2)}, u32[]{:S(2)}) %collective-permute-start.6) | collective-permute-done | bytes 786464 | tf_op jit(solution)/shard_map/ppermute | solution.py:25
  154.4 9.6 %collective-permute-done.5 = f32[8,96,256]{2,1,0:T(8,128)S(1)} collective-permute-done((f32[8,96,256]{2,1,0:T(8,128)S(1)}, f32[8,96,256]{2,1,0:T(8,128)S(1)}, u32[]{:S(2)}, u32[]{:S(2)}) %collective-permute-start.5) | collective-permute-done | bytes 786464 | tf_op jit(solution)/shard_map/ppermute | solution.py:25
  164.2 1.8 add.58
  166.0 4.9 %all-to-all-start.2 = ((f32[4,32,16,256]{3,2,1,0:T(8,128)}), f32[4,32,16,256]{3,2,1,0:T(8,128)}, u32[]{:S(2)}, u32[]{:S(2)}) async-start(f32[4,32,16,256]{3,2,1,0:T(8,128)} %add.58), calls=%async_computation.2 | async-start | bytes 4194304 | tf_op jit(solution)/shard_map/all_to_all | solution.py:35
  171.1 7.1 %shard_map.55 = (f32[8,48,256]{2,1,0:T(8,128)S(1)}, f32[8,48,256]{2,1,0:T(8,128)S(1)}, f32[8,48,256]{2,1,0:T(8,128)S(1)}, f32[8,48,256]{2,1,0:T(8,128)S(1)}, f32...) custom-call(s32[4]{0:T(128)S(1)} %pad_add_fusion.1.index._, ...), custom_call_target="tpu_custom_call" | custom-call | bytes 25200000 | tf_op jit(solution)/shard_map/pallas_call | solution.py:49
  178.3 1.5 collective-permute-start.15
  179.7 5.6 %collective-permute-done.19 = f32[8,48,256]{2,1,0:T(8,128)S(1)} collective-permute-done((f32[8,48,256]{2,1,0:T(8,128)S(1)}, f32[8,48,256]{2,1,0:T(8,128)S(1)}, u32[]{:S(2)}, u32[]{:S(2)}) %collective-permute-start.19) | collective-permute-done | bytes 393248 | tf_op jit(solution)/shard_map/ppermute | solution.py:25
  185.4 1.6 collective-permute-start.20
  187.1 1.1 collective-permute-start.12
  188.3 2.7 collective-permute-start.13
  190.9 2.8 collective-permute-start.14
  197.3 2.7 reduce_sum.9
  200.0 3.5 %all-to-all-start.3 = ((f32[4,8,16,256]{3,2,1,0:T(8,128)}), f32[4,8,16,256]{3,2,1,0:T(8,128)S(1)}, u32[]{:S(2)}, u32[]{:S(2)}) async-start(f32[4,8,16,256]{3,2,1,0:T(8,128)} %bitcast.27), calls=%async_computation.3 | async-start | bytes 1048576 | tf_op jit(solution)/shard_map/all_to_all | solution.py:37
  203.4 1.9 add_add_fusion.2
  205.4 2.0 add_add_fusion.3
  207.4 4.6 %all-to-all-done.3 = f32[4,8,16,256]{3,2,1,0:T(8,128)S(1)} async-done(((f32[4,8,16,256]{3,2,1,0:T(8,128)}), f32[4,8,16,256]{3,2,1,0:T(8,128)S(1)}, u32[]{:S(2)}, u32[]{:S(2)}) %all-to-all-start.3) | async-done | bytes 524320 | tf_op jit(solution)/shard_map/all_to_all | solution.py:37
  212.0 1.7 collective-permute-done.12.refs_40_.refs_41_
  214.7 2.2 collective-permute-start.23
  216.9 2.5 collective-permute-start.26
  220.1 1.8 slice.19
  222.0 2.6 collective-permute-start.25
  224.6 1.7 maximum_select_fusion.refs_0_.refs_1_.refs_24_.refs_25_
  226.3 6.7 %collective-permute-done.24.refs_4_ = f32[4,96,256]{2,1,0:T(8,128)S(1)} collective-permute-done((f32[4,96,256]{2,1,0:T(8,128)}, f32[4,96,256]{2,1,0:T(8,128)S(1)}, u32[]{:S(2)}, u32[]{:S(2)}) %collective-permute-start.24) | collective-permute-done | bytes 393248 | tf_op jit(solution)/shard_map/ppermute | solution.py:23
  233.8 2.6 collective-permute-start.28
  236.3 5.5 %collective-permute-start.30 = (f32[8,64,256]{2,1,0:T(8,128)S(1)}, f32[8,64,256]{2,1,0:T(8,128)S(1)}, u32[]{:S(2)}, u32[]{:S(2)}) collective-permute-start(f32[8,64,256]{2,1,0:T(8,128)S(1)} %bitcast.14), channel_id=1, source_target_pairs={{0,1},{1,0},{2,3},{3,2},{4,5},{5,4},{6,7},{7,6},{8,9},{9,8},{10,11... | collective-permute-start | bytes 1572872 | tf_op jit(solution)/shard_map/ppermute | solution.py:30
  241.8 2.9 collective-permute-start.34
  245.2 4.1 %collective-permute-done.28.refs_4_.refs_5_ = f32[8,96,256]{2,1,0:T(8,128)} collective-permute-done((f32[8,96,256]{2,1,0:T(8,128)S(1)}, f32[8,96,256]{2,1,0:T(8,128)}, u32[]{:S(2)}, u32[]{:S(2)}) %collective-permute-start.28) | collective-permute-done | bytes 786464 | tf_op jit(solution)/shard_map/ppermute | solution.py:29
  249.3 6.1 %collective-permute-start.27 = (f32[8,96,256]{2,1,0:T(8,128)S(1)}, f32[8,96,256]{2,1,0:T(8,128)S(1)}, u32[]{:S(2)}, u32[]{:S(2)}) collective-permute-start(f32[8,96,256]{2,1,0:T(8,128)S(1)} %maximum_select_fusion.refs_0_.refs_1_.refs_24_.refs_25_), channel_id=1, source_target_pairs={{0,1},{1,0},{2,3},{3,2},{4,5},{5,4},{6,7},{7,6},{8,9},{9,8},{10,11... | collective-permute-start | bytes 2359304 | tf_op jit(solution)/shard_map/ppermute | solution.py:30
  255.4 6.3 %collective-permute-done.34.refs_26_.refs_27_ = f32[8,96,256]{2,1,0:T(8,128)S(1)} collective-permute-done((f32[8,96,256]{2,1,0:T(8,128)S(1)}, f32[8,96,256]{2,1,0:T(8,128)S(1)}, u32[]{:S(2)}, u32[]{:S(2)}) %collective-permute-start.34) | collective-permute-done | bytes 786464 | tf_op jit(solution)/shard_map/ppermute | solution.py:23
  262.5 2.3 collective-permute-done.35.refs_28_.refs_29_
  264.8 1.1 collective-permute-start.31
  267.5 2.7 collective-permute-start.37
  273.4 2.7 collective-permute-start.39
  276.1 1.0 copy-done.1
  277.2 10.7 %shard_map.56 = (f32[2,4,256,256]{3,2,1,0:T(8,128)}, bf16[4,4,256,256]{3,2,1,0:T(8,128)(2,1)}) custom-call(s32[2]{0:T(128)S(1)} %pad_add_fusion.index._, f32[8,96,256]{2,1,0:T(8,128)S(1)} %maximum_select_fusion.refs_0_.refs_1_.refs_24_.refs_25_, f32[8,96,256]{2,1,0:T(8,128)S(1)} %maximum_select_fusion.refs_0_.refs_1_.refs_24_.refs_25_, ...), custom_call_target="tpu_custom_call" | custom-call | bytes 39600000 | tf_op jit(solution)/shard_map/pallas_call | solution.py:49
  288.0 6.1 %shard_map.57 = f32[2,4,256,256]{3,2,1,0:T(8,128)} custom-call(s32[2]{0:T(128)S(1)} %pad_add_fusion.index._, f32[2,4,256,256]{3,2,1,0:T(8,128)} %get-tuple-element.109.total, bf16[4,4,256,256]{3,2,1,0:T(8,128)(2,1)} %get-tuple-element.110.kept, f32[4,96,256]{2,1,0:T(8,128)} %collective-permute-done.36.refs_0_, ...), custom_call_target="tpu_custom_call" | custom-call | bytes 14400000 | tf_op jit(solution)/shard_map/pallas_call | solution.py:49
  (108 shorter events, 14.6 us)
Async XLA Ops:
  5.8 77.8 %all-to-all-start = ((f32[4,16,96,256]{3,2,1,0:T(8,128)}), f32[4,16,96,256]{3,2,1,0:T(8,128)}, u32[]{:S(2)}, u32[]{:S(2)}) async-start(f32[4,16,96,256]{3,2,1,0:T(8,128)} %shard_map.46), calls=%async_computation | async-start | bytes 12582912 | tf_op jit(solution)/shard_map/all_to_all | solution.py:35
  14.2 69.0 %collective-permute-start.3 = (f32[4,16,48,256]{3,2,1,0:T(8,128)S(1)}, f32[4,16,48,256]{3,2,1,0:T(8,128)S(1)}, u32[]{:S(2)}, u32[]{:S(2)}) collective-permute-start(f32[4,16,48,256]{3,2,1,0:T(8,128)S(1)} %shard_map.51), channel_id=1, source_target_pairs={{0,16},{16,0},{32,48},{48,32},{64,80},{80,64},{96,112},{112,96},{1... | collective-permute-start | bytes 9437192 | tf_op jit(solution)/shard_map/ppermute | solution.py:27
  17.7 25.2 %collective-permute-start = (f32[16,4,16,256]{3,2,1,0:T(8,128)S(1)}, f32[16,4,16,256]{3,2,1,0:T(8,128)S(1)}, u32[]{:S(2)}, u32[]{:S(2)}) collective-permute-start(f32[16,4,16,256]{3,2,1,0:T(8,128)S(1)} %shard_map.47), channel_id=1, source_target_pairs={{0,32},{16,48},{32,64},{48,80},{64,96},{80,112},{96,0},{112,16},{1... | collective-permute-start | bytes 3145736 | tf_op jit(solution)/shard_map/ppermute | solution.py:25
  20.9 45.6 %collective-permute-start.1 = (f32[16,4,16,256]{3,2,1,0:T(8,128)S(1)}, f32[16,4,16,256]{3,2,1,0:T(8,128)S(1)}, u32[]{:S(2)}, u32[]{:S(2)}) collective-permute-start(f32[16,4,16,256]{3,2,1,0:T(8,128)S(1)} %shard_map.48), channel_id=1, source_target_pairs={{0,64},{16,80},{32,96},{48,112},{64,0},{80,16},{96,32},{112,48},{1... | collective-permute-start | bytes 3145736 | tf_op jit(solution)/shard_map/ppermute | solution.py:25
  25.5 42.6 %collective-permute-start.2 = (f32[16,4,16,256]{3,2,1,0:T(8,128)S(1)}, f32[16,4,16,256]{3,2,1,0:T(8,128)S(1)}, u32[]{:S(2)}, u32[]{:S(2)}) collective-permute-start(f32[16,4,16,256]{3,2,1,0:T(8,128)S(1)} %shard_map.49), channel_id=1, source_target_pairs={{0,96},{16,112},{32,0},{48,16},{64,32},{80,48},{96,64},{112,80},{1... | collective-permute-start | bytes 3145736 | tf_op jit(solution)/shard_map/ppermute | solution.py:25
  42.9 1.0 copy-start.3
  66.5 1.0 copy-start.5
  68.1 1.0 copy-start.19
  85.6 5.5 %copy-start.10 = (f32[8,64,64]{2,1,0:T(8,128)S(1)}, f32[8,64,64]{2,1,0:T(8,128)}, u32[]{:S(2)}) copy-start(f32[8,64,64]{2,1,0:T(8,128)} %constant.50.clone.w_ref) | copy-start | bytes 393220
  85.6 80.4 %all-to-all-start.1 = ((f32[4,2,16,48,256]{4,3,2,1,0:T(8,128)}), f32[4,2,16,48,256]{4,3,2,1,0:T(8,128)}, u32[]{:S(2)}, u32[]{:S(2)}) async-start(f32[4,2,16,48,256]{4,3,2,1,0:T(8,128)} %shard_map.54), calls=%async_computation.1 | async-start | bytes 12582912 | tf_op jit(solution)/shard_map/all_to_all | solution.py:35
  91.1 12.7 %copy-start.2 = (f32[32,64,64]{2,1,0:T(8,128)S(1)}, f32[32,64,64]{2,1,0:T(8,128)}, u32[]{:S(2)}) copy-start(f32[32,64,64]{2,1,0:T(8,128)} %constant.51.clone.w_ref) | copy-start | bytes 1572868
  91.1 12.7 %copy-start.4 = (f32[16,4,16,256]{3,2,1,0:T(8,128)S(1)}, f32[16,4,16,256]{3,2,1,0:T(8,128)}, u32[]{:S(2)}) copy-start(f32[16,4,16,256]{3,2,1,0:T(8,128)} %copy-done.3) | copy-start | bytes 3145732
  91.1 12.7 %copy-start.6 = (f32[16,4,16,256]{3,2,1,0:T(8,128)S(1)}, f32[16,4,16,256]{3,2,1,0:T(8,128)}, u32[]{:S(2)}) copy-start(f32[16,4,16,256]{3,2,1,0:T(8,128)} %copy-done.5) | copy-start | bytes 3145732
  100.9 18.5 %collective-permute-start.8 = (f32[8,96,256]{2,1,0:T(8,128)}, f32[8,96,256]{2,1,0:T(8,128)S(1)}, u32[]{:S(2)}, u32[]{:S(2)}) collective-permute-start(f32[8,96,256]{2,1,0:T(8,128)} %get-tuple-element.78), channel_id=1, source_target_pairs={{0,96},{16,112},{32,0},{48,16},{64,32},{80,48},{96,64},{112,80},{1... | collective-permute-start | bytes 2359304 | tf_op jit(solution)/shard_map/ppermute | solution.py:25
  103.8 8.3 %copy-start.24 = (f32[8,96,256]{2,1,0:T(8,128)S(1)}, f32[8,96,256]{2,1,0:T(8,128)}, u32[]{:S(2)}) copy-start(f32[8,96,256]{2,1,0:T(8,128)} %get-tuple-element.73) | copy-start | bytes 2359300
  103.8 15.6 %copy-start.20 = (f32[8,96,256]{2,1,0:T(8,128)S(1)}, f32[8,96,256]{2,1,0:T(8,128)}, u32[]{:S(2)}) copy-start(f32[8,96,256]{2,1,0:T(8,128)} %get-tuple-element.77) | copy-start | bytes 2359300
  103.8 19.2 %copy-start.23 = (f32[8,96,256]{2,1,0:T(8,128)S(1)}, f32[8,96,256]{2,1,0:T(8,128)}, u32[]{:S(2)}) copy-start(f32[8,96,256]{2,1,0:T(8,128)} %get-tuple-element.74) | copy-start | bytes 2359300
  110.8 53.3 %collective-permute-start.10 = (f32[4,32,16,256]{3,2,1,0:T(8,128)}, f32[4,32,16,256]{3,2,1,0:T(8,128)S(1)}, u32[]{:S(2)}, u32[]{:S(2)}) collective-permute-start(f32[4,32,16,256]{3,2,1,0:T(8,128)} %get-tuple-element.83), channel_id=1, source_target_pairs={{0,16},{16,0},{32,48},{48,32},{64,80},{80,64},{96,112},{112,96},{1... | collective-permute-start | bytes 6291464 | tf_op jit(solution)/shard_map/ppermute | solution.py:27
  112.0 18.3 %collective-permute-start.4 = (f32[8,96,256]{2,1,0:T(8,128)S(1)}, f32[8,96,256]{2,1,0:T(8,128)S(1)}, u32[]{:S(2)}, u32[]{:S(2)}) collective-permute-start(f32[8,96,256]{2,1,0:T(8,128)S(1)} %copy-done.24), channel_id=1, source_target_pairs={{0,32},{16,48},{32,64},{48,80},{64,96},{80,112},{96,0},{112,16},{1... | collective-permute-start | bytes 2359304 | tf_op jit(solution)/shard_map/ppermute | solution.py:25
  112.1 35.2 %collective-permute-start.7 = (f32[8,96,256]{2,1,0:T(8,128)S(1)}, f32[8,96,256]{2,1,0:T(8,128)S(1)}, u32[]{:S(2)}, u32[]{:S(2)}) collective-permute-start(f32[8,96,256]{2,1,0:T(8,128)S(1)} %get-tuple-element.76), channel_id=1, source_target_pairs={{0,32},{16,48},{32,64},{48,80},{64,96},{80,112},{96,0},{112,16},{1... | collective-permute-start | bytes 2359304 | tf_op jit(solution)/shard_map/ppermute | solution.py:25
  119.5 27.7 %collective-permute-start.9 = (f32[8,96,256]{2,1,0:T(8,128)S(1)}, f32[8,96,256]{2,1,0:T(8,128)S(1)}, u32[]{:S(2)}, u32[]{:S(2)}) collective-permute-start(f32[8,96,256]{2,1,0:T(8,128)S(1)} %add.55), channel_id=1, source_target_pairs={{0,96},{16,112},{32,0},{48,16},{64,32},{80,48},{96,64},{112,80},{1... | collective-permute-start | bytes 2359304 | tf_op jit(solution)/shard_map/ppermute | solution.py:25
  123.0 31.4 %collective-permute-start.6 = (f32[8,96,256]{2,1,0:T(8,128)S(1)}, f32[8,96,256]{2,1,0:T(8,128)S(1)}, u32[]{:S(2)}, u32[]{:S(2)}) collective-permute-start(f32[8,96,256]{2,1,0:T(8,128)S(1)} %copy-done.23), channel_id=1, source_target_pairs={{0,96},{16,112},{32,0},{48,16},{64,32},{80,48},{96,64},{112,80},{1... | collective-permute-start | bytes 2359304 | tf_op jit(solution)/shard_map/ppermute | solution.py:25
  130.5 33.7 %copy-start.18 = (f32[4,32,16,256]{3,2,1,0:T(8,128)S(1)}, f32[4,32,16,256]{3,2,1,0:T(8,128)}, u32[]{:S(2)}) copy-start(f32[4,32,16,256]{3,2,1,0:T(8,128)} %get-tuple-element.82) | copy-start | bytes 6291460
  130.5 33.5 %collective-permute-start.5 = (f32[8,96,256]{2,1,0:T(8,128)S(1)}, f32[8,96,256]{2,1,0:T(8,128)S(1)}, u32[]{:S(2)}, u32[]{:S(2)}) collective-permute-start(f32[8,96,256]{2,1,0:T(8,128)S(1)} %add.51), channel_id=1, source_target_pairs={{0,32},{16,48},{32,64},{48,80},{64,96},{80,112},{96,0},{112,16},{1... | collective-permute-start | bytes 2359304 | tf_op jit(solution)/shard_map/ppermute | solution.py:25
  166.0 5.1 %copy-start.9 = (f32[8,64,128]{2,1,0:T(8,128)S(1)}, f32[8,64,128]{2,1,0:T(8,128)}, u32[]{:S(2)}) copy-start(f32[8,64,128]{2,1,0:T(8,128)} %constant.52.clone.w_ref) | copy-start | bytes 786436
  166.0 31.3 %all-to-all-start.2 = ((f32[4,32,16,256]{3,2,1,0:T(8,128)}), f32[4,32,16,256]{3,2,1,0:T(8,128)}, u32[]{:S(2)}, u32[]{:S(2)}) async-start(f32[4,32,16,256]{3,2,1,0:T(8,128)} %add.58), calls=%async_computation.2 | async-start | bytes 4194304 | tf_op jit(solution)/shard_map/all_to_all | solution.py:35
  170.8 16.1 %collective-permute-start.11 = (f32[8,96,256]{2,1,0:T(8,128)}, f32[8,96,256]{2,1,0:T(8,128)S(1)}, u32[]{:S(2)}, u32[]{:S(2)}) collective-permute-start(f32[8,96,256]{2,1,0:T(8,128)} %add_add_fusion), channel_id=1, source_target_pairs={{0,16},{16,0},{32,48},{48,32},{64,80},{80,64},{96,112},{112,96},{1... | collective-permute-start | bytes 2359304 | tf_op jit(solution)/shard_map/ppermute | solution.py:27
  178.2 7.2 %collective-permute-start.19 = (f32[8,48,256]{2,1,0:T(8,128)S(1)}, f32[8,48,256]{2,1,0:T(8,128)S(1)}, u32[]{:S(2)}, u32[]{:S(2)}) collective-permute-start(f32[8,48,256]{2,1,0:T(8,128)S(1)} %get-tuple-element.97), channel_id=1, source_target_pairs={{0,96},{16,112},{32,0},{48,16},{64,32},{80,48},{96,64},{112,80},{1... | collective-permute-start | bytes 1179656 | tf_op jit(solution)/shard_map/ppermute | solution.py:25
  178.3 12.7 %collective-permute-start.15 = (f32[8,48,256]{2,1,0:T(8,128)S(1)}, f32[8,48,256]{2,1,0:T(8,128)S(1)}, u32[]{:S(2)}, u32[]{:S(2)}) collective-permute-start(f32[8,48,256]{2,1,0:T(8,128)S(1)} %get-tuple-element.92), channel_id=1, source_target_pairs={{0,32},{16,48},{32,64},{48,80},{64,96},{80,112},{96,0},{112,16},{1... | collective-permute-start | bytes 1179656 | tf_op jit(solution)/shard_map/ppermute | solution.py:25
  179.7 15.4 %collective-permute-start.18 = (f32[8,48,256]{2,1,0:T(8,128)S(1)}, f32[8,48,256]{2,1,0:T(8,128)S(1)}, u32[]{:S(2)}, u32[]{:S(2)}) collective-permute-start(f32[8,48,256]{2,1,0:T(8,128)S(1)} %get-tuple-element.95), channel_id=1, source_target_pairs={{0,32},{16,48},{32,64},{48,80},{64,96},{80,112},{96,0},{112,16},{1... | collective-permute-start | bytes 1179656 | tf_op jit(solution)/shard_map/ppermute | solution.py:25
  185.4 10.4 %collective-permute-start.20 = (f32[8,48,256]{2,1,0:T(8,128)S(1)}, f32[8,48,256]{2,1,0:T(8,128)S(1)}, u32[]{:S(2)}, u32[]{:S(2)}) collective-permute-start(f32[8,48,256]{2,1,0:T(8,128)S(1)} %add.64), channel_id=1, source_target_pairs={{0,96},{16,112},{32,0},{48,16},{64,32},{80,48},{96,64},{112,80},{1... | collective-permute-start | bytes 1179656 | tf_op jit(solution)/shard_map/ppermute | solution.py:25
  187.1 18.3 %copy-start.11 = (f32[8,96,256]{2,1,0:T(8,128)}, f32[8,96,256]{2,1,0:T(8,128)S(1)}, u32[]{:S(2)}) copy-start(f32[8,96,256]{2,1,0:T(8,128)S(1)} %add.59.refs_16_.refs_17_.refs_36_.refs_37_) | copy-start | bytes 2359300
  187.1 26.6 %collective-permute-start.12 = (f32[8,96,256]{2,1,0:T(8,128)S(1)}, f32[8,96,256]{2,1,0:T(8,128)S(1)}, u32[]{:S(2)}, u32[]{:S(2)}) collective-permute-start(f32[8,96,256]{2,1,0:T(8,128)S(1)} %add.59.refs_16_.refs_17_.refs_36_.refs_37_), channel_id=1, source_target_pairs={{0,4},{4,8},{8,12},{12,0},{1,5},{5,9},{9,13},{13,1},{2,6},{6,10},{... | collective-permute-start | bytes 2359304 | tf_op jit(solution)/shard_map/ppermute | solution.py:23
  188.3 25.5 %collective-permute-start.13 = (f32[8,96,256]{2,1,0:T(8,128)S(1)}, f32[8,96,256]{2,1,0:T(8,128)}, u32[]{:S(2)}, u32[]{:S(2)}) collective-permute-start(f32[8,96,256]{2,1,0:T(8,128)S(1)} %add.59.refs_16_.refs_17_.refs_36_.refs_37_), channel_id=1, source_target_pairs={{0,12},{4,0},{8,4},{12,8},{1,13},{5,1},{9,5},{13,9},{2,14},{6,2},{... | collective-permute-start | bytes 2359304 | tf_op jit(solution)/shard_map/ppermute | solution.py:23
  190.9 22.8 %collective-permute-start.14 = (f32[8,96,256]{2,1,0:T(8,128)S(1)}, f32[8,96,256]{2,1,0:T(8,128)}, u32[]{:S(2)}, u32[]{:S(2)}) collective-permute-start(f32[8,96,256]{2,1,0:T(8,128)S(1)} %add.59.refs_16_.refs_17_.refs_36_.refs_37_), channel_id=1, source_target_pairs={{0,2},{1,3},{2,0},{3,1},{4,6},{5,7},{6,4},{7,5},{8,10},{9,11},{10,... | collective-permute-start | bytes 2359304 | tf_op jit(solution)/shard_map/ppermute | solution.py:29
  195.1 10.3 %collective-permute-start.17 = (f32[8,48,256]{2,1,0:T(8,128)S(1)}, f32[8,48,256]{2,1,0:T(8,128)}, u32[]{:S(2)}, u32[]{:S(2)}) collective-permute-start(f32[8,48,256]{2,1,0:T(8,128)S(1)} %get-tuple-element.93), channel_id=1, source_target_pairs={{0,96},{16,112},{32,0},{48,16},{64,32},{80,48},{96,64},{112,80},{1... | collective-permute-start | bytes 1179656 | tf_op jit(solution)/shard_map/ppermute | solution.py:25
  196.6 8.8 %collective-permute-start.16 = (f32[8,48,256]{2,1,0:T(8,128)}, f32[8,48,256]{2,1,0:T(8,128)}, u32[]{:S(2)}, u32[]{:S(2)}) collective-permute-start(f32[8,48,256]{2,1,0:T(8,128)} %add.60), channel_id=1, source_target_pairs={{0,32},{16,48},{32,64},{48,80},{64,96},{80,112},{96,0},{112,16},{1... | collective-permute-start | bytes 1179656 | tf_op jit(solution)/shard_map/ppermute | solution.py:25
  200.0 12.0 %all-to-all-start.3 = ((f32[4,8,16,256]{3,2,1,0:T(8,128)}), f32[4,8,16,256]{3,2,1,0:T(8,128)S(1)}, u32[]{:S(2)}, u32[]{:S(2)}) async-start(f32[4,8,16,256]{3,2,1,0:T(8,128)} %bitcast.27), calls=%async_computation.3 | async-start | bytes 1048576 | tf_op jit(solution)/shard_map/all_to_all | solution.py:37
  213.8 10.9 %copy-start.12 = (f32[8,96,256]{2,1,0:T(8,128)}, f32[8,96,256]{2,1,0:T(8,128)S(1)}, u32[]{:S(2)}) copy-start(f32[8,96,256]{2,1,0:T(8,128)S(1)} %collective-permute-done.12.refs_40_.refs_41_) | copy-start | bytes 2359300
  213.8 8.2 %collective-permute-start.21 = (f32[8,48,256]{2,1,0:T(8,128)}, f32[8,48,256]{2,1,0:T(8,128)}, u32[]{:S(2)}, u32[]{:S(2)}) collective-permute-start(f32[8,48,256]{2,1,0:T(8,128)} %add_add_fusion.2), channel_id=1, source_target_pairs={{0,16},{16,0},{32,48},{48,32},{64,80},{80,64},{96,112},{112,96},{1... | collective-permute-start | bytes 1179656 | tf_op jit(solution)/shard_map/ppermute | solution.py:27
  213.9 19.9 %collective-permute-start.22 = (f32[8,64,256]{2,1,0:T(8,128)S(1)}, f32[8,64,256]{2,1,0:T(8,128)S(1)}, u32[]{:S(2)}, u32[]{:S(2)}) collective-permute-start(f32[8,64,256]{2,1,0:T(8,128)S(1)} %bitcast.11), channel_id=1, source_target_pairs={{0,4},{4,8},{8,12},{12,0},{1,5},{5,9},{9,13},{13,1},{2,6},{6,10},{... | collective-permute-start | bytes 1572872 | tf_op jit(solution)/shard_map/ppermute | solution.py:23
  214.7 19.1 %collective-permute-start.23 = (f32[8,64,256]{2,1,0:T(8,128)S(1)}, f32[8,64,256]{2,1,0:T(8,128)S(1)}, u32[]{:S(2)}, u32[]{:S(2)}) collective-permute-start(f32[8,64,256]{2,1,0:T(8,128)S(1)} %bitcast.12), channel_id=1, source_target_pairs={{0,12},{4,0},{8,4},{12,8},{1,13},{5,1},{9,5},{13,9},{2,14},{6,2},{... | collective-permute-start | bytes 1572872 | tf_op jit(solution)/shard_map/ppermute | solution.py:23
  216.9 16.9 %collective-permute-start.26 = (f32[8,64,256]{2,1,0:T(8,128)S(1)}, f32[8,64,256]{2,1,0:T(8,128)S(1)}, u32[]{:S(2)}, u32[]{:S(2)}) collective-permute-start(f32[8,64,256]{2,1,0:T(8,128)S(1)} %bitcast.13), channel_id=1, source_target_pairs={{0,2},{1,3},{2,0},{3,1},{4,6},{5,7},{6,4},{7,5},{8,10},{9,11},{10,... | collective-permute-start | bytes 1572872 | tf_op jit(solution)/shard_map/ppermute | solution.py:29
  220.1 12.9 %collective-permute-start.24 = (f32[4,96,256]{2,1,0:T(8,128)}, f32[4,96,256]{2,1,0:T(8,128)S(1)}, u32[]{:S(2)}, u32[]{:S(2)}) collective-permute-start(f32[4,96,256]{2,1,0:T(8,128)} %slice.18), channel_id=1, source_target_pairs={{0,4},{4,8},{8,12},{12,0},{1,5},{5,9},{9,13},{13,1},{2,6},{6,10},{... | collective-permute-start | bytes 1179656 | tf_op jit(solution)/shard_map/ppermute | solution.py:23
  222.0 11.8 %collective-permute-start.25 = (f32[4,96,256]{2,1,0:T(8,128)}, f32[4,96,256]{2,1,0:T(8,128)}, u32[]{:S(2)}, u32[]{:S(2)}) collective-permute-start(f32[4,96,256]{2,1,0:T(8,128)} %slice.19), channel_id=1, source_target_pairs={{0,12},{4,0},{8,4},{12,8},{1,13},{5,1},{9,5},{13,9},{2,14},{6,2},{... | collective-permute-start | bytes 1179656 | tf_op jit(solution)/shard_map/ppermute | solution.py:23
  233.8 15.5 %collective-permute-start.28 = (f32[8,96,256]{2,1,0:T(8,128)S(1)}, f32[8,96,256]{2,1,0:T(8,128)}, u32[]{:S(2)}, u32[]{:S(2)}) collective-permute-start(f32[8,96,256]{2,1,0:T(8,128)S(1)} %maximum_select_fusion.refs_0_.refs_1_.refs_24_.refs_25_), channel_id=1, source_target_pairs={{0,2},{1,3},{2,0},{3,1},{4,6},{5,7},{6,4},{7,5},{8,10},{9,11},{10,... | collective-permute-start | bytes 2359304 | tf_op jit(solution)/shard_map/ppermute | solution.py:29
  236.3 8.7 %collective-permute-start.30 = (f32[8,64,256]{2,1,0:T(8,128)S(1)}, f32[8,64,256]{2,1,0:T(8,128)S(1)}, u32[]{:S(2)}, u32[]{:S(2)}) collective-permute-start(f32[8,64,256]{2,1,0:T(8,128)S(1)} %bitcast.14), channel_id=1, source_target_pairs={{0,1},{1,0},{2,3},{3,2},{4,5},{5,4},{6,7},{7,6},{8,9},{9,8},{10,11... | collective-permute-start | bytes 1572872 | tf_op jit(solution)/shard_map/ppermute | solution.py:30
  241.8 19.9 %collective-permute-start.34 = (f32[8,96,256]{2,1,0:T(8,128)S(1)}, f32[8,96,256]{2,1,0:T(8,128)S(1)}, u32[]{:S(2)}, u32[]{:S(2)}) collective-permute-start(f32[8,96,256]{2,1,0:T(8,128)S(1)} %maximum_select_fusion.refs_0_.refs_1_.refs_24_.refs_25_), channel_id=1, source_target_pairs={{0,12},{4,0},{8,4},{12,8},{1,13},{5,1},{9,5},{13,9},{2,14},{6,2},{... | collective-permute-start | bytes 2359304 | tf_op jit(solution)/shard_map/ppermute | solution.py:23
  244.7 20.1 %collective-permute-start.35 = (f32[8,96,256]{2,1,0:T(8,128)S(1)}, f32[8,96,256]{2,1,0:T(8,128)S(1)}, u32[]{:S(2)}, u32[]{:S(2)}) collective-permute-start(f32[8,96,256]{2,1,0:T(8,128)S(1)} %maximum_select_fusion.refs_0_.refs_1_.refs_24_.refs_25_), channel_id=1, source_target_pairs={{0,4},{4,8},{8,12},{12,0},{1,5},{5,9},{9,13},{13,1},{2,6},{6,10},{... | collective-permute-start | bytes 2359304 | tf_op jit(solution)/shard_map/ppermute | solution.py:23
  244.7 22.7 %collective-permute-start.32 = (f32[8,96,256]{2,1,0:T(8,128)}, f32[8,96,256]{2,1,0:T(8,128)S(1)}, u32[]{:S(2)}, u32[]{:S(2)}) collective-permute-start(f32[8,96,256]{2,1,0:T(8,128)} %copy-done.11), channel_id=1, source_target_pairs={{0,1},{1,0},{2,3},{3,2},{4,5},{5,4},{6,7},{7,6},{8,9},{9,8},{10,11... | collective-permute-start | bytes 2359304 | tf_op jit(solution)/shard_map/ppermute | solution.py:30
  245.0 22.5 %collective-permute-start.33 = (f32[8,96,256]{2,1,0:T(8,128)}, f32[8,96,256]{2,1,0:T(8,128)S(1)}, u32[]{:S(2)}, u32[]{:S(2)}) collective-permute-start(f32[8,96,256]{2,1,0:T(8,128)} %collective-permute-done.14.refs_20_.refs_21_), channel_id=1, source_target_pairs={{0,1},{1,0},{2,3},{3,2},{4,5},{5,4},{6,7},{7,6},{8,9},{9,8},{10,11... | collective-permute-start | bytes 2359304 | tf_op jit(solution)/shard_map/ppermute | solution.py:30
  249.3 23.1 %collective-permute-start.27 = (f32[8,96,256]{2,1,0:T(8,128)S(1)}, f32[8,96,256]{2,1,0:T(8,128)S(1)}, u32[]{:S(2)}, u32[]{:S(2)}) collective-permute-start(f32[8,96,256]{2,1,0:T(8,128)S(1)} %maximum_select_fusion.refs_0_.refs_1_.refs_24_.refs_25_), channel_id=1, source_target_pairs={{0,1},{1,0},{2,3},{3,2},{4,5},{5,4},{6,7},{7,6},{8,9},{9,8},{10,11... | collective-permute-start | bytes 2359304 | tf_op jit(solution)/shard_map/ppermute | solution.py:30
  261.7 10.8 %copy-start.13 = (f32[8,96,256]{2,1,0:T(8,128)}, f32[8,96,256]{2,1,0:T(8,128)S(1)}, u32[]{:S(2)}) copy-start(f32[8,96,256]{2,1,0:T(8,128)S(1)} %collective-permute-done.34.refs_26_.refs_27_) | copy-start | bytes 2359300
  261.7 14.4 %collective-permute-start.29 = (f32[8,96,256]{2,1,0:T(8,128)}, f32[8,96,256]{2,1,0:T(8,128)}, u32[]{:S(2)}, u32[]{:S(2)}) collective-permute-start(f32[8,96,256]{2,1,0:T(8,128)} %collective-permute-done.28.refs_4_.refs_5_), channel_id=1, source_target_pairs={{0,1},{1,0},{2,3},{3,2},{4,5},{5,4},{6,7},{7,6},{8,9},{9,8},{10,11... | collective-permute-start | bytes 2359304 | tf_op jit(solution)/shard_map/ppermute | solution.py:30
  264.8 7.7 %copy-start.14 = (f32[8,96,256]{2,1,0:T(8,128)}, f32[8,96,256]{2,1,0:T(8,128)S(1)}, u32[]{:S(2)}) copy-start(f32[8,96,256]{2,1,0:T(8,128)S(1)} %collective-permute-done.35.refs_28_.refs_29_) | copy-start | bytes 2359300
  264.8 6.8 %collective-permute-start.31 = (f32[8,64,256]{2,1,0:T(8,128)S(1)}, f32[8,64,256]{2,1,0:T(8,128)S(1)}, u32[]{:S(2)}, u32[]{:S(2)}) collective-permute-start(f32[8,64,256]{2,1,0:T(8,128)S(1)} %collective-permute-done.26.refs_12_.refs_13_), channel_id=1, source_target_pairs={{0,1},{1,0},{2,3},{3,2},{4,5},{5,4},{6,7},{7,6},{8,9},{9,8},{10,11... | collective-permute-start | bytes 1572872 | tf_op jit(solution)/shard_map/ppermute | solution.py:30
  267.5 5.0 %copy-start.15 = (f32[8,96,256]{2,1,0:T(8,128)}, f32[8,96,256]{2,1,0:T(8,128)S(1)}, u32[]{:S(2)}) copy-start(f32[8,96,256]{2,1,0:T(8,128)S(1)} %collective-permute-done.32.refs_18_.refs_19_) | copy-start | bytes 2359300
  267.5 20.4 %collective-permute-start.36 = (f32[4,96,256]{2,1,0:T(8,128)}, f32[4,96,256]{2,1,0:T(8,128)}, u32[]{:S(2)}, u32[]{:S(2)}) collective-permute-start(f32[4,96,256]{2,1,0:T(8,128)} %slice.24), channel_id=1, source_target_pairs={{0,4},{4,8},{8,12},{12,0},{1,5},{5,9},{9,13},{13,1},{2,6},{6,10},{... | collective-permute-start | bytes 1179656 | tf_op jit(solution)/shard_map/ppermute | solution.py:23
  267.5 5.0 %copy-start.16 = (f32[8,96,256]{2,1,0:T(8,128)}, f32[8,96,256]{2,1,0:T(8,128)S(1)}, u32[]{:S(2)}) copy-start(f32[8,96,256]{2,1,0:T(8,128)S(1)} %collective-permute-done.33.refs_22_.refs_23_) | copy-start | bytes 2359300
  267.5 20.4 %collective-permute-start.37 = (f32[4,96,256]{2,1,0:T(8,128)}, f32[4,96,256]{2,1,0:T(8,128)}, u32[]{:S(2)}, u32[]{:S(2)}) collective-permute-start(f32[4,96,256]{2,1,0:T(8,128)} %slice.25), channel_id=1, source_target_pairs={{0,12},{4,0},{8,4},{12,8},{1,13},{5,1},{9,5},{13,9},{2,14},{6,2},{... | collective-permute-start | bytes 1179656 | tf_op jit(solution)/shard_map/ppermute | solution.py:23
  272.5 15.5 %collective-permute-start.38 = (f32[4,64,256]{2,1,0:T(8,128)}, f32[4,64,256]{2,1,0:T(8,128)}, u32[]{:S(2)}, u32[]{:S(2)}) collective-permute-start(f32[4,64,256]{2,1,0:T(8,128)} %slice.22), channel_id=1, source_target_pairs={{0,4},{4,8},{8,12},{12,0},{1,5},{5,9},{9,13},{13,1},{2,6},{6,10},{... | collective-permute-start | bytes 786440 | tf_op jit(solution)/shard_map/ppermute | solution.py:23
  273.4 14.5 %collective-permute-start.39 = (f32[4,64,256]{2,1,0:T(8,128)}, f32[4,64,256]{2,1,0:T(8,128)}, u32[]{:S(2)}, u32[]{:S(2)}) collective-permute-start(f32[4,64,256]{2,1,0:T(8,128)} %slice.23), channel_id=1, source_target_pairs={{0,12},{4,0},{8,4},{12,8},{1,13},{5,1},{9,5},{13,9},{2,14},{6,2},{... | collective-permute-start | bytes 786440 | tf_op jit(solution)/shard_map/ppermute | solution.py:23
  276.1 1.0 copy-start.1
  277.2 10.8 %copy-start.8 = (f32[4,96,256]{2,1,0:T(8,128)S(1)}, f32[4,96,256]{2,1,0:T(8,128)}, u32[]{:S(2)}) copy-start(f32[4,96,256]{2,1,0:T(8,128)} %copy-done.7) | copy-start | bytes 1179652
  (5 other events, 4.0 us)

commit v3 on v2

--- a/solution.py
+++ b/solution.py
@@ -253,17 +253,18 @@
     out[1, 0] = ri + ir
 
 
-def near_kernel(segments, index, *refs):
-    n = len(segments)
-    left, right = refs[: 8 * n], refs[8 * n : 14 * n]
-    out, kept, a_ref, b_ref = refs[14 * n :]
+def near_kernel(left_rows, right_rows, index, *refs):
+    n, m = 8 * len(left_rows), 6 * len(right_rows)
+    left, right = refs[:n], refs[n : n + m]
+    out, kept, a_ref, b_ref = refs[n + m :]
     col, z = index[0], index[1]
-    for i, rows in enumerate(segments):
-        for part in range(2):
+    for part in range(2):
+        for i, rows in enumerate(left_rows):
             for e in range(4):
                 hi, lo = split(left[8 * i + 2 * e + part][0])
                 a_ref[col ^ e, 2 * part, rows] = hi
                 a_ref[col ^ e, 2 * part + 1, rows] = lo
+        for i, rows in enumerate(right_rows):
             for t in range(3):
                 hi, lo = split(right[6 * i + 2 * t + part][0])
                 b_ref[t, 2 * part, rows] = hi
@@ -274,9 +275,9 @@
     kept[0] = a_ref[(z + 2) % 4]
 
 
-def far_kernel(segments, _, total, kept, *refs):
+def far_kernel(right_rows, _, total, kept, *refs):
     out, b_ref = refs[-2:]
-    for i, rows in enumerate(segments):
+    for i, rows in enumerate(right_rows):
         for part in range(2):
             hi, lo = split(refs[2 * i + part][0])
             b_ref[2 * part, rows] = hi
@@ -285,19 +286,22 @@
     dots([a], [b], out, (total[0, 0], total[1, 0]))
 
 
-def product(index, left, right, across, starts):
-    sizes = [part[0].shape[1] for part in left]
-    segments = [slice(a, a + b) for a, b in zip(starts, sizes)]
+def product(index, left, right, across, left_starts, right_starts):
+    def segments(parts, starts):
+        return [slice(a, a + part[0].shape[1]) for a, part in zip(starts, parts)]
+
+    left_rows, right_rows = segments(left, left_starts), segments(right, right_starts)
+    sizes = [part[0].shape[1] for part in right]
 
     def spec(rows, first):
         return pl.BlockSpec((1, rows, C), lambda g, _: (first + g, 0, 0))
 
     def both(groups):
         operands, specs = [], []
-        for arrays, rows in zip(groups, sizes):
+        for arrays in groups:
             for array in arrays:
                 operands += [array, array]
-                specs += [spec(rows, 0), spec(rows, 4)]
+                specs += [spec(array.shape[1], 0), spec(array.shape[1], 4)]
         return operands, specs
 
     left, left_specs = both(left)
@@ -305,7 +309,7 @@
     out_spec = pl.BlockSpec((2, 1, 256, C), lambda g, _: (0, g, 0, 0))
     kept_spec = pl.BlockSpec((1, 4, 256, C), lambda g, _: (g, 0, 0, 0))
     total, kept = call(
-        functools.partial(near_kernel, segments),
+        functools.partial(near_kernel, left_rows, right_rows),
         index,
         left + right,
         (4,),
@@ -316,7 +320,7 @@
         [pltpu.VMEM((4, 4, 256, C), jnp.bfloat16), pltpu.VMEM((3, 4, 256, C), jnp.bfloat16)],
     )
     return call(
-        functools.partial(far_kernel, segments),
+        functools.partial(far_kernel, right_rows),
         index,
         [total, kept] + [array for pair in across for array in pair],
         (4,),
@@ -359,14 +363,12 @@
     first = exchange(pack(place, blocks, for_z, 4, (16, R1, C), (4, 16, R1, C), 5), "z")
     second = [shift(for_y(r), "y", r) for r in (1, 2, 3)]
     third = pack(place, blocks, for_self, 4, (16, HALF, C), (4, 2, 16, HALF, C), 3)
+    second = dft_by_row(jnp.stack([4 * f + z, y]), two, blocks, second)
     first, second, third, third_far = together(first, second, third, third_far)
 
     third = exchange(join(third, third_far), "z")
-    slots = dft_by_owner(place, one, first, 9)
-    slots, second = together(slots, second)
-    mine1, other1 = reduce_ring(slots, "y")
-    mine, other = dft_by_row(jnp.stack([4 * f + z, y]), two, blocks, second)
-    own2 = mine + shift(other, "x_lo")
+    own2 = second[0] + shift(second[1], "x_lo")
+    mine1, other1 = reduce_ring(dft_by_owner(place, one, first, 9), "y")
     mine1, other1, own2, third = together(mine1, other1, own2, third)
 
     own2 = jnp.sum(exchange(own2, "z"), axis=0)
@@ -376,26 +378,25 @@
     mine3, other3 = reduce_ring(dft_by_owner(place, three, third.reshape(8, 16, HALF, C), 7), "y")
     own2 = exchange(own2.reshape(4, 8, QUARTER, C), "y")
     own2 = jnp.transpose(own2, (1, 0, 2, 3)).reshape(8, R2, C)
-    own1, below1, above1, far1, own2, mine3, other3 = together(own1, below1, above1, far1, own2, mine3, other3)
+    across1 = across_z(below1, above1)
+    below2, above2 = near_z(own2)
+    mine3, other3 = together(mine3, other3)
 
     other3 = shift(other3, "x_lo")
-    below2, above2 = near_z(own2)
-    across1 = across_z(below1, above1)
+    own3 = jnp.where(x_lo == 0, jnp.concatenate([mine3, other3], axis=1), jnp.concatenate([other3, mine3], axis=1))
     far2 = shift(own2, "x_hi")
-    own3 = jnp.where(x_lo == 0, jnp.concatenate([mine3, other3], axis=1), jnp.concatenate([other3, mine3], axis=1))
-    own3, below2, above2, across1, far2 = together(own3, below2, above2, across1, far2)
+    own3, below2, above2, across1 = together(own3, below2, above2, across1)
 
     below3, above3 = near_z(own3)
     across2 = across_z(below2, above2)
     far3 = shift(own3, "x_hi")
+    below3, above3, far2, far3, across2 = together(below3, above3, far2, far3, across2)
     across3 = across_z(below3, above3)
 
-    def columns(own, far):
-        return [own, shift(own, "core"), far, shift(far, "core")]
-
-    left = [columns(own3, far3), columns(own2, far2), columns(own1, far1)]
+    left = [[own, shift(own, "core"), far, shift(far, "core")] for own, far in ((own3, far3), (own2, far2), (own1, far1))]
     right = [(own3, above3, below3), (own2, above2, below2), (own1, above1, below1)]
-    return product(jnp.stack([col, z]), left, right, [across3, across2, across1], (0, R3, R3 + R2))
+    starts = (0, R3, R3 + R2)
+    return product(jnp.stack([col, z]), left, right, [across3, across2, across1], starts, starts)
 
 
 def solution(mesh):

time: 295 us -> 284 us (0.963)
  waiting for transfers between devices: 130 us -> 112 us
  starting transfers between devices: 77.9 us -> 86.8 us
  local copies, waits for them, and re-layouts: 13.7 us -> 7.27 us
  Pallas kernels: 59.9 us -> 63.8 us
    ppermute x4, waiting for transfers between devices: 14.2 us -> 4.65 us  [shift(): return lax.ppermute(x, 'freq', [(i, i ^ 1) for i in range(8)])]
    ppermute x12, waiting for transfers between devices: 17 us -> 8.69 us  [shift(): return lax.ppermute(x, 'row', [(i, (i + by) % 4) for i in range(4)])]
    unnamed x50 -> x36, local copies, waits for them, and re-layouts: 8.03 us -> 2.85 us
    ppermute x15, starting transfers between devices: 15.5 us -> 20.2 us  [shift(): return lax.ppermute(x, 'freq', [(i, (i + 2 * by) % 8) for i in range(8)])]
    all_to_all x1, waiting for transfers between devices: 4.6 us -> 0.02 us  [exchange(): lax.all_to_all(x, 'freq', split_axis=0, concat_axis=0, tiled=True, axis_i...]
    ppermute x6, starting transfers between devices: 14 us -> 18.5 us  [shift(): return lax.ppermute(x, 'col', [(i, i ^ 1) for i in range(4)])]
    pallas_call x11, Pallas kernels: 58 us -> 61.8 us  [call(): pl.pallas_call(kernel, grid_spec=pltpu.PrefetchScalarGridSpec(num_scalar_...]
    all_to_all x3, waiting for transfers between devices: 0.44 us -> 3.91 us  [exchange(): return lax.all_to_all(x, 'row', split_axis=0, concat_axis=0, tiled=True)]
  transfers between devices with their start and end apart: 44 -> 44, of which waited for: 18 -> 16; matrix products, arithmetic and copies ran while one was open for 6% -> 6% of each run, Pallas kernels for 16% -> 18%
where the time goes in v3:
time: 284 us; the launch traced here: 283 us
  waiting for transfers between devices  112 us (39%)
  starting transfers between devices  86.8 us (31%)
  Pallas kernels  63.8 us (22%)
  other arithmetic  12.6 us (4%)
  local copies, waits for them, and re-layouts  7.27 us (3%)
    ppermute x15, waiting for transfers between devices, shift(): return lax.ppermute(x, 'freq', [(i, (i + 2 * by) % 8) for i in range(8)])  88.4 us
    pallas_call x11, Pallas kernels, call(): pl.pallas_call(kernel, grid_spec=pltpu.PrefetchScalarGridSpec(num_scalar_...  61.8 us
    ppermute x15, starting transfers between devices, shift(): return lax.ppermute(x, 'freq', [(i, (i + 2 * by) % 8) for i in range(8)])  20.2 us
    ppermute x6, starting transfers between devices, shift(): return lax.ppermute(x, 'col', [(i, i ^ 1) for i in range(4)])  18.5 us
    ppermute x12, starting transfers between devices, shift(): return lax.ppermute(x, 'row', [(i, (i + by) % 4) for i in range(4)])  17.6 us
    all_to_all x3, starting transfers between devices, exchange(): return lax.all_to_all(x, 'row', split_axis=0, concat_axis=0, tiled=True)  15.1 us
    ppermute x12, waiting for transfers between devices, shift(): return lax.ppermute(x, 'row', [(i, (i + by) % 4) for i in range(4)])  8.69 us
    ppermute x3, starting transfers between devices, shift(): return lax.ppermute(x, 'col', [(i, i ^ 2) for i in range(4)])  6.99 us
  transfers between devices with their start and end apart: 44, of which 16 were waited for; matrix products, arithmetic and copies ran while one was open for 6% of the time, Pallas kernels for 18%

profile of v3, /device:TPU:1, one launch (start us, length us, event | category | flops | bytes accessed | tf_op | source)
XLA Modules:
  0.0 282.9 jit_solution(6083343752046098095)
XLA Ops:
  0.1 5.8 %shard_map.46 = f32[4,16,96,256]{3,2,1,0:T(8,128)} custom-call(s32[4]{0:T(128)S(1)} %pad_add_fusion.1.index._, f32[16,4,256,256]{3,2,1,0:T(8,128)} %bitcast.19), custom_call_target="tpu_custom_call" | custom-call | bytes 18000000 | tf_op jit(solution)/shard_map/pallas_call | solution.py:49
  5.9 5.9 %all-to-all-start = ((f32[4,16,96,256]{3,2,1,0:T(8,128)}), f32[4,16,96,256]{3,2,1,0:T(8,128)}, u32[]{:S(2)}, u32[]{:S(2)}) async-start(f32[4,16,96,256]{3,2,1,0:T(8,128)} %shard_map.46), calls=%async_computation | async-start | bytes 12582912 | tf_op jit(solution)/shard_map/all_to_all | solution.py:35
  11.7 3.4 %shard_map.52 = f32[4,16,48,256]{3,2,1,0:T(8,128)} custom-call(s32[4]{0:T(128)S(1)} %pad_add_fusion.1.index._, f32[16,4,256,256]{3,2,1,0:T(8,128)} %bitcast.20), custom_call_target="tpu_custom_call" | custom-call | bytes 10800000 | tf_op jit(solution)/shard_map/pallas_call | solution.py:49
  15.2 1.5 collective-permute-start.3
  16.7 2.8 shard_map.47
  19.5 1.4 collective-permute-start
  20.8 2.8 shard_map.48
  23.6 2.7 collective-permute-start.1
  26.3 2.8 shard_map.49
  30.2 3.4 %shard_map.51.joined_ref = f32[4,2,16,48,256]{4,3,2,1,0:T(8,128)} custom-call(s32[4]{0:T(128)S(1)} %pad_add_fusion.1.index._, f32[16,4,256,256]{3,2,1,0:T(8,128)} %bitcast.24), custom_call_target="tpu_custom_call" | custom-call | bytes 10800000 | tf_op jit(solution)/shard_map/pallas_call | solution.py:49
  33.7 11.1 %collective-permute-done.refs_1_ = f32[16,4,16,256]{3,2,1,0:T(8,128)} collective-permute-done((f32[16,4,16,256]{3,2,1,0:T(8,128)}, f32[16,4,16,256]{3,2,1,0:T(8,128)}, u32[]{:S(2)}, u32[]{:S(2)}) %collective-permute-start) | collective-permute-done | bytes 1048608 | tf_op jit(solution)/shard_map/ppermute | solution.py:25
  44.9 23.6 %collective-permute-done.1.refs_2_ = f32[16,4,16,256]{3,2,1,0:T(8,128)} collective-permute-done((f32[16,4,16,256]{3,2,1,0:T(8,128)}, f32[16,4,16,256]{3,2,1,0:T(8,128)}, u32[]{:S(2)}, u32[]{:S(2)}) %collective-permute-start.1) | collective-permute-done | bytes 1048608 | tf_op jit(solution)/shard_map/ppermute | solution.py:25
  68.4 2.7 collective-permute-done.2.refs_3_
  71.1 1.2 copy-done
  72.3 7.2 %shard_map.50 = (f32[4,32,16,256]{3,2,1,0:T(8,128)}, f32[4,32,16,256]{3,2,1,0:T(8,128)}) custom-call(s32[2]{0:T(128)S(1)} %pad_add_fusion.2._, f32[32,64,64]{2,1,0:T(8,128)S(1)} %copy-done, f32[16,4,256,256]{3,2,1,0:T(8,128)} %bitcast.25, f32[16,4,16,256]{3,2,1,0:T(8,128)} %collective-permute-done.refs_1_, ...), custom_call_target="tpu_custom_call" | custom-call | bytes 25200000 | tf_op jit(solution)/shard_map/pallas_call | solution.py:49
  79.6 4.6 %collective-permute-done.3.far_ref = f32[4,16,48,256]{3,2,1,0:T(8,128)S(1)} collective-permute-done((f32[4,16,48,256]{3,2,1,0:T(8,128)}, f32[4,16,48,256]{3,2,1,0:T(8,128)S(1)}, u32[]{:S(2)}, u32[]{:S(2)}) %collective-permute-start.3) | collective-permute-done | bytes 3145760 | tf_op jit(solution)/shard_map/ppermute | solution.py:27
  84.2 2.0 shard_map.54
  86.2 5.6 %all-to-all-start.1 = ((f32[4,2,16,48,256]{4,3,2,1,0:T(8,128)}), f32[4,2,16,48,256]{4,3,2,1,0:T(8,128)}, u32[]{:S(2)}, u32[]{:S(2)}) async-start(f32[4,2,16,48,256]{4,3,2,1,0:T(8,128)} %shard_map.54), calls=%async_computation.1 | async-start | bytes 12582912 | tf_op jit(solution)/shard_map/all_to_all | solution.py:35
  91.8 9.6 %shard_map.53 = (f32[8,96,256]{2,1,0:T(8,128)S(1)}, f32[8,96,256]{2,1,0:T(8,128)S(1)}, f32[8,96,256]{2,1,0:T(8,128)S(1)}, f32[8,96,256]{2,1,0:T(8,128)S(1)}, f32...) custom-call(s32[4]{0:T(128)S(1)} %pad_add_fusion.1.index._, ...), custom_call_target="tpu_custom_call" | custom-call | bytes 32400000 | tf_op jit(solution)/shard_map/pallas_call | solution.py:49
  101.5 1.6 collective-permute-start.4
  103.1 1.2 collective-permute-start.10
  104.3 1.5 collective-permute-start.8
  105.8 1.4 collective-permute-start.6
  107.2 13.8 %collective-permute-done.4 = f32[8,96,256]{2,1,0:T(8,128)S(1)} collective-permute-done((f32[8,96,256]{2,1,0:T(8,128)}, f32[8,96,256]{2,1,0:T(8,128)S(1)}, u32[]{:S(2)}, u32[]{:S(2)}) %collective-permute-start.4) | collective-permute-done | bytes 786464 | tf_op jit(solution)/shard_map/ppermute | solution.py:25
  121.1 1.2 collective-permute-start.7
  122.4 1.3 add.56
  123.6 2.1 collective-permute-start.9
  125.7 12.6 %collective-permute-done.6 = f32[8,96,256]{2,1,0:T(8,128)S(1)} collective-permute-done((f32[8,96,256]{2,1,0:T(8,128)}, f32[8,96,256]{2,1,0:T(8,128)S(1)}, u32[]{:S(2)}, u32[]{:S(2)}) %collective-permute-start.6) | collective-permute-done | bytes 786464 | tf_op jit(solution)/shard_map/ppermute | solution.py:25
  140.3 15.8 %collective-permute-done.7 = f32[8,96,256]{2,1,0:T(8,128)S(1)} collective-permute-done((f32[8,96,256]{2,1,0:T(8,128)S(1)}, f32[8,96,256]{2,1,0:T(8,128)S(1)}, u32[]{:S(2)}, u32[]{:S(2)}) %collective-permute-start.7) | collective-permute-done | bytes 786464 | tf_op jit(solution)/shard_map/ppermute | solution.py:25
  157.1 1.8 add.58
  158.9 3.9 %all-to-all-done.1 = f32[4,2,16,48,256]{4,3,2,1,0:T(8,128)} async-done(((f32[4,2,16,48,256]{4,3,2,1,0:T(8,128)}), f32[4,2,16,48,256]{4,3,2,1,0:T(8,128)}, u32[]{:S(2)}, u32[]{:S(2)}) %all-to-all-start.1) | async-done | bytes 6291488 | tf_op jit(solution)/shard_map/all_to_all | solution.py:35
  162.8 3.6 %all-to-all-start.2 = ((f32[4,32,16,256]{3,2,1,0:T(8,128)}), f32[4,32,16,256]{3,2,1,0:T(8,128)S(1)}, u32[]{:S(2)}, u32[]{:S(2)}) async-start(f32[4,32,16,256]{3,2,1,0:T(8,128)} %add.58), calls=%async_computation.2 | async-start | bytes 4194304 | tf_op jit(solution)/shard_map/all_to_all | solution.py:35
  166.4 1.3 collective-permute-start.20
  167.7 7.1 %shard_map.55 = (f32[8,48,256]{2,1,0:T(8,128)S(1)}, f32[8,48,256]{2,1,0:T(8,128)S(1)}, f32[8,48,256]{2,1,0:T(8,128)S(1)}, f32[8,48,256]{2,1,0:T(8,128)S(1)}, f32...) custom-call(s32[4]{0:T(128)S(1)} %pad_add_fusion.1.index._, ...), custom_call_target="tpu_custom_call" | custom-call | bytes 25200000 | tf_op jit(solution)/shard_map/pallas_call | solution.py:49
  174.8 1.4 collective-permute-start.11
  176.2 1.5 collective-permute-start.15
  177.7 1.4 collective-permute-start.13
  179.1 5.1 %collective-permute-done.11 = f32[8,48,256]{2,1,0:T(8,128)S(1)} collective-permute-done((f32[8,48,256]{2,1,0:T(8,128)S(1)}, f32[8,48,256]{2,1,0:T(8,128)S(1)}, u32[]{:S(2)}, u32[]{:S(2)}) %collective-permute-start.11) | collective-permute-done | bytes 393248 | tf_op jit(solution)/shard_map/ppermute | solution.py:25
  184.3 1.2 collective-permute-start.14
  186.3 1.5 collective-permute-start.16
  190.0 2.3 collective-permute-done.13
  192.3 2.3 collective-permute-start.23
  196.4 4.1 %all-to-all-start.3 = ((f32[4,8,16,256]{3,2,1,0:T(8,128)}), f32[4,8,16,256]{3,2,1,0:T(8,128)S(1)}, u32[]{:S(2)}, u32[]{:S(2)}) async-start(f32[4,8,16,256]{3,2,1,0:T(8,128)} %bitcast.8), calls=%async_computation.3 | async-start | bytes 1048576 | tf_op jit(solution)/shard_map/all_to_all | solution.py:37
  201.1 1.8 add_add_fusion.2
  203.2 2.8 collective-permute-start.36
  207.9 1.4 collective-permute-start.18
  209.3 1.3 collective-permute-start.19
  210.6 1.8 slice.25
  212.4 1.4 collective-permute-start.24
  213.7 1.5 collective-permute-done.22.refs_4_
  215.9 1.9 collective-permute-start.28
  217.9 1.6 maximum_select_fusion.refs_0_.refs_1_.refs_24_.refs_25_
  219.4 3.9 %collective-permute-done.24.refs_5_ = f32[4,96,256]{2,1,0:T(8,128)S(1)} collective-permute-done((f32[4,96,256]{2,1,0:T(8,128)}, f32[4,96,256]{2,1,0:T(8,128)S(1)}, u32[]{:S(2)}, u32[]{:S(2)}) %collective-permute-start.24) | collective-permute-done | bytes 393248 | tf_op jit(solution)/shard_map/ppermute | solution.py:23
  223.3 1.8 collective-permute-start.26
  225.1 1.5 collective-permute-start.27
  226.6 2.3 collective-permute-start.29
  229.5 6.4 %collective-permute-done.28.refs_12_.refs_13_ = f32[8,64,256]{2,1,0:T(8,128)S(1)} collective-permute-done((f32[8,64,256]{2,1,0:T(8,128)S(1)}, f32[8,64,256]{2,1,0:T(8,128)S(1)}, u32[]{:S(2)}, u32[]{:S(2)}) %collective-permute-start.28) | collective-permute-done | bytes 524320 | tf_op jit(solution)/shard_map/ppermute | solution.py:29
  235.9 2.9 %collective-permute-start.31 = (f32[4,64,256]{2,1,0:T(8,128)S(1)}, f32[4,64,256]{2,1,0:T(8,128)S(1)}, u32[]{:S(2)}, u32[]{:S(2)}) collective-permute-start(f32[4,64,256]{2,1,0:T(8,128)S(1)} %slice.21), channel_id=1, source_target_pairs={{0,12},{4,0},{8,4},{12,8},{1,13},{5,1},{9,5},{13,9},{2,14},{6,2},{... | collective-permute-start | bytes 786440 | tf_op jit(solution)/shard_map/ppermute | solution.py:23
  238.7 3.3 %collective-permute-done.30.refs_2_ = f32[4,64,256]{2,1,0:T(8,128)S(1)} collective-permute-done((f32[4,64,256]{2,1,0:T(8,128)S(1)}, f32[4,64,256]{2,1,0:T(8,128)S(1)}, u32[]{:S(2)}, u32[]{:S(2)}) %collective-permute-start.30) | collective-permute-done | bytes 262176 | tf_op jit(solution)/shard_map/ppermute | solution.py:23
  242.0 11.8 %collective-permute-start.35 = (f32[8,96,256]{2,1,0:T(8,128)}, f32[8,96,256]{2,1,0:T(8,128)}, u32[]{:S(2)}, u32[]{:S(2)}) collective-permute-start(f32[8,96,256]{2,1,0:T(8,128)} %add.65.refs_16_.refs_17_.refs_36_.refs_37_), channel_id=1, source_target_pairs={{0,1},{1,0},{2,3},{3,2},{4,5},{5,4},{6,7},{7,6},{8,9},{9,8},{10,11... | collective-permute-start | bytes 2359304 | tf_op jit(solution)/shard_map/ppermute | solution.py:30
  254.5 5.1 %collective-permute-start.37 = (f32[8,96,256]{2,1,0:T(8,128)}, f32[8,96,256]{2,1,0:T(8,128)S(1)}, u32[]{:S(2)}, u32[]{:S(2)}) collective-permute-start(f32[8,96,256]{2,1,0:T(8,128)} %collective-permute-done.36.refs_20_.refs_21_), channel_id=1, source_target_pairs={{0,1},{1,0},{2,3},{3,2},{4,5},{5,4},{6,7},{7,6},{8,9},{9,8},{10,11... | collective-permute-start | bytes 2359304 | tf_op jit(solution)/shard_map/ppermute | solution.py:30
  263.7 1.9 collective-permute-start.39
  265.8 11.1 %shard_map.56 = (f32[2,4,256,256]{3,2,1,0:T(8,128)}, bf16[4,4,256,256]{3,2,1,0:T(8,128)(2,1)}) custom-call(s32[2]{0:T(128)S(1)} %pad_add_fusion.index._, f32[8,96,256]{2,1,0:T(8,128)S(1)} %maximum_select_fusion.refs_0_.refs_1_.refs_24_.refs_25_, f32[8,96,256]{2,1,0:T(8,128)S(1)} %maximum_select_fusion.refs_0_.refs_1_.refs_24_.refs_25_, ...), custom_call_target="tpu_custom_call" | custom-call | bytes 39600000 | tf_op jit(solution)/shard_map/pallas_call | solution.py:49
  277.0 6.0 %shard_map.57 = f32[2,4,256,256]{3,2,1,0:T(8,128)} custom-call(s32[2]{0:T(128)S(1)} %pad_add_fusion.index._, f32[2,4,256,256]{3,2,1,0:T(8,128)} %get-tuple-element.83.total, bf16[4,4,256,256]{3,2,1,0:T(8,128)(2,1)} %get-tuple-element.84.kept, f32[4,96,256]{2,1,0:T(8,128)} %collective-permute-done.38.refs_0_, f32[4,96,256]{2,1,0:T(8,128)} %collective-permute-done.39.refs_1_, ...), custom_call_target="tpu_custom_call" | custom-call | bytes 14400000 | tf_op jit(solution)/shard_map/pallas_call | solution.py:49
  (94 shorter events, 18.3 us)
Async XLA Ops:
  5.9 78.3 %all-to-all-start = ((f32[4,16,96,256]{3,2,1,0:T(8,128)}), f32[4,16,96,256]{3,2,1,0:T(8,128)}, u32[]{:S(2)}, u32[]{:S(2)}) async-start(f32[4,16,96,256]{3,2,1,0:T(8,128)} %shard_map.46), calls=%async_computation | async-start | bytes 12582912 | tf_op jit(solution)/shard_map/all_to_all | solution.py:35
  15.2 69.0 %collective-permute-start.3 = (f32[4,16,48,256]{3,2,1,0:T(8,128)}, f32[4,16,48,256]{3,2,1,0:T(8,128)S(1)}, u32[]{:S(2)}, u32[]{:S(2)}) collective-permute-start(f32[4,16,48,256]{3,2,1,0:T(8,128)} %shard_map.52), channel_id=1, source_target_pairs={{0,16},{16,0},{32,48},{48,32},{64,80},{80,64},{96,112},{112,96},{1... | collective-permute-start | bytes 9437192 | tf_op jit(solution)/shard_map/ppermute | solution.py:27
  19.5 25.4 %collective-permute-start = (f32[16,4,16,256]{3,2,1,0:T(8,128)}, f32[16,4,16,256]{3,2,1,0:T(8,128)}, u32[]{:S(2)}, u32[]{:S(2)}) collective-permute-start(f32[16,4,16,256]{3,2,1,0:T(8,128)} %shard_map.47), channel_id=1, source_target_pairs={{0,32},{16,48},{32,64},{48,80},{64,96},{80,112},{96,0},{112,16},{1... | collective-permute-start | bytes 3145736 | tf_op jit(solution)/shard_map/ppermute | solution.py:25
  23.6 44.8 %collective-permute-start.1 = (f32[16,4,16,256]{3,2,1,0:T(8,128)}, f32[16,4,16,256]{3,2,1,0:T(8,128)}, u32[]{:S(2)}, u32[]{:S(2)}) collective-permute-start(f32[16,4,16,256]{3,2,1,0:T(8,128)} %shard_map.48), channel_id=1, source_target_pairs={{0,64},{16,80},{32,96},{48,112},{64,0},{80,16},{96,32},{112,48},{1... | collective-permute-start | bytes 3145736 | tf_op jit(solution)/shard_map/ppermute | solution.py:25
  29.1 42.0 %collective-permute-start.2 = (f32[16,4,16,256]{3,2,1,0:T(8,128)}, f32[16,4,16,256]{3,2,1,0:T(8,128)}, u32[]{:S(2)}, u32[]{:S(2)}) collective-permute-start(f32[16,4,16,256]{3,2,1,0:T(8,128)} %shard_map.49), channel_id=1, source_target_pairs={{0,96},{16,112},{32,0},{48,16},{64,32},{80,48},{96,64},{112,80},{1... | collective-permute-start | bytes 3145736 | tf_op jit(solution)/shard_map/ppermute | solution.py:25
  71.1 1.2 copy-start
  86.2 5.6 %copy-start.10 = (f32[8,64,64]{2,1,0:T(8,128)S(1)}, f32[8,64,64]{2,1,0:T(8,128)}, u32[]{:S(2)}) copy-start(f32[8,64,64]{2,1,0:T(8,128)} %constant.51.clone.w_ref) | copy-start | bytes 393220
  86.2 76.6 %all-to-all-start.1 = ((f32[4,2,16,48,256]{4,3,2,1,0:T(8,128)}), f32[4,2,16,48,256]{4,3,2,1,0:T(8,128)}, u32[]{:S(2)}, u32[]{:S(2)}) async-start(f32[4,2,16,48,256]{4,3,2,1,0:T(8,128)} %shard_map.54), calls=%async_computation.1 | async-start | bytes 12582912 | tf_op jit(solution)/shard_map/all_to_all | solution.py:35
  91.8 11.3 %copy-start.17 = (f32[4,32,16,256]{3,2,1,0:T(8,128)S(1)}, f32[4,32,16,256]{3,2,1,0:T(8,128)}, u32[]{:S(2)}) copy-start(f32[4,32,16,256]{3,2,1,0:T(8,128)} %get-tuple-element.59) | copy-start | bytes 6291460
  101.5 19.5 %collective-permute-start.4 = (f32[8,96,256]{2,1,0:T(8,128)}, f32[8,96,256]{2,1,0:T(8,128)S(1)}, u32[]{:S(2)}, u32[]{:S(2)}) collective-permute-start(f32[8,96,256]{2,1,0:T(8,128)} %get-tuple-element.52), channel_id=1, source_target_pairs={{0,32},{16,48},{32,64},{48,80},{64,96},{80,112},{96,0},{112,16},{1... | collective-permute-start | bytes 2359304 | tf_op jit(solution)/shard_map/ppermute | solution.py:25
  103.1 54.0 %collective-permute-start.10 = (f32[4,32,16,256]{3,2,1,0:T(8,128)S(1)}, f32[4,32,16,256]{3,2,1,0:T(8,128)S(1)}, u32[]{:S(2)}, u32[]{:S(2)}) collective-permute-start(f32[4,32,16,256]{3,2,1,0:T(8,128)S(1)} %copy-done.17), channel_id=1, source_target_pairs={{0,16},{16,0},{32,48},{48,32},{64,80},{80,64},{96,112},{112,96},{1... | collective-permute-start | bytes 6291464 | tf_op jit(solution)/shard_map/ppermute | solution.py:27
  104.3 18.1 %collective-permute-start.8 = (f32[8,96,256]{2,1,0:T(8,128)}, f32[8,96,256]{2,1,0:T(8,128)S(1)}, u32[]{:S(2)}, u32[]{:S(2)}) collective-permute-start(f32[8,96,256]{2,1,0:T(8,128)} %get-tuple-element.57), channel_id=1, source_target_pairs={{0,96},{16,112},{32,0},{48,16},{64,32},{80,48},{96,64},{112,80},{1... | collective-permute-start | bytes 2359304 | tf_op jit(solution)/shard_map/ppermute | solution.py:25
  105.8 32.6 %collective-permute-start.6 = (f32[8,96,256]{2,1,0:T(8,128)}, f32[8,96,256]{2,1,0:T(8,128)S(1)}, u32[]{:S(2)}, u32[]{:S(2)}) collective-permute-start(f32[8,96,256]{2,1,0:T(8,128)} %get-tuple-element.53), channel_id=1, source_target_pairs={{0,96},{16,112},{32,0},{48,16},{64,32},{80,48},{96,64},{112,80},{1... | collective-permute-start | bytes 2359304 | tf_op jit(solution)/shard_map/ppermute | solution.py:25
  121.1 18.2 %collective-permute-start.5 = (f32[8,96,256]{2,1,0:T(8,128)S(1)}, f32[8,96,256]{2,1,0:T(8,128)S(1)}, u32[]{:S(2)}, u32[]{:S(2)}) collective-permute-start(f32[8,96,256]{2,1,0:T(8,128)S(1)} %add.52), channel_id=1, source_target_pairs={{0,32},{16,48},{32,64},{48,80},{64,96},{80,112},{96,0},{112,16},{1... | collective-permute-start | bytes 2359304 | tf_op jit(solution)/shard_map/ppermute | solution.py:25
  121.1 34.9 %collective-permute-start.7 = (f32[8,96,256]{2,1,0:T(8,128)S(1)}, f32[8,96,256]{2,1,0:T(8,128)S(1)}, u32[]{:S(2)}, u32[]{:S(2)}) collective-permute-start(f32[8,96,256]{2,1,0:T(8,128)S(1)} %get-tuple-element.55), channel_id=1, source_target_pairs={{0,32},{16,48},{32,64},{48,80},{64,96},{80,112},{96,0},{112,16},{1... | collective-permute-start | bytes 2359304 | tf_op jit(solution)/shard_map/ppermute | solution.py:25
  123.6 32.4 %collective-permute-start.9 = (f32[8,96,256]{2,1,0:T(8,128)S(1)}, f32[8,96,256]{2,1,0:T(8,128)S(1)}, u32[]{:S(2)}, u32[]{:S(2)}) collective-permute-start(f32[8,96,256]{2,1,0:T(8,128)S(1)} %add.56), channel_id=1, source_target_pairs={{0,96},{16,112},{32,0},{48,16},{64,32},{80,48},{96,64},{112,80},{1... | collective-permute-start | bytes 2359304 | tf_op jit(solution)/shard_map/ppermute | solution.py:25
  139.2 17.9 %copy-start.15 = (f32[4,32,16,256]{3,2,1,0:T(8,128)S(1)}, f32[4,32,16,256]{3,2,1,0:T(8,128)}, u32[]{:S(2)}) copy-start(f32[4,32,16,256]{3,2,1,0:T(8,128)} %get-tuple-element.58) | copy-start | bytes 6291460
  158.9 8.8 %copy-start.9 = (f32[8,64,128]{2,1,0:T(8,128)S(1)}, f32[8,64,128]{2,1,0:T(8,128)}, u32[]{:S(2)}) copy-start(f32[8,64,128]{2,1,0:T(8,128)} %constant.52.clone.w_ref) | copy-start | bytes 786436
  162.8 32.6 %all-to-all-start.2 = ((f32[4,32,16,256]{3,2,1,0:T(8,128)}), f32[4,32,16,256]{3,2,1,0:T(8,128)S(1)}, u32[]{:S(2)}, u32[]{:S(2)}) async-start(f32[4,32,16,256]{3,2,1,0:T(8,128)} %add.58), calls=%async_computation.2 | async-start | bytes 4194304 | tf_op jit(solution)/shard_map/all_to_all | solution.py:35
  166.4 21.4 %collective-permute-start.20 = (f32[8,96,256]{2,1,0:T(8,128)}, f32[8,96,256]{2,1,0:T(8,128)S(1)}, u32[]{:S(2)}, u32[]{:S(2)}) collective-permute-start(f32[8,96,256]{2,1,0:T(8,128)} %add_add_fusion), channel_id=1, source_target_pairs={{0,16},{16,0},{32,48},{48,32},{64,80},{80,64},{96,112},{112,96},{1... | collective-permute-start | bytes 2359304 | tf_op jit(solution)/shard_map/ppermute | solution.py:27
  167.7 20.1 %copy-start.13 = (f32[8,96,256]{2,1,0:T(8,128)S(1)}, f32[8,96,256]{2,1,0:T(8,128)}, u32[]{:S(2)}) copy-start(f32[8,96,256]{2,1,0:T(8,128)} %add_add_fusion.1) | copy-start | bytes 2359300
  174.8 9.4 %collective-permute-start.11 = (f32[8,48,256]{2,1,0:T(8,128)S(1)}, f32[8,48,256]{2,1,0:T(8,128)S(1)}, u32[]{:S(2)}, u32[]{:S(2)}) collective-permute-start(f32[8,48,256]{2,1,0:T(8,128)S(1)} %get-tuple-element.65), channel_id=1, source_target_pairs={{0,32},{16,48},{32,64},{48,80},{64,96},{80,112},{96,0},{112,16},{1... | collective-permute-start | bytes 1179656 | tf_op jit(solution)/shard_map/ppermute | solution.py:25
  176.2 9.4 %collective-permute-start.15 = (f32[8,48,256]{2,1,0:T(8,128)S(1)}, f32[8,48,256]{2,1,0:T(8,128)S(1)}, u32[]{:S(2)}, u32[]{:S(2)}) collective-permute-start(f32[8,48,256]{2,1,0:T(8,128)S(1)} %get-tuple-element.70), channel_id=1, source_target_pairs={{0,96},{16,112},{32,0},{48,16},{64,32},{80,48},{96,64},{112,80},{1... | collective-permute-start | bytes 1179656 | tf_op jit(solution)/shard_map/ppermute | solution.py:25
  177.7 14.6 %collective-permute-start.13 = (f32[8,48,256]{2,1,0:T(8,128)S(1)}, f32[8,48,256]{2,1,0:T(8,128)S(1)}, u32[]{:S(2)}, u32[]{:S(2)}) collective-permute-start(f32[8,48,256]{2,1,0:T(8,128)S(1)} %get-tuple-element.66), channel_id=1, source_target_pairs={{0,96},{16,112},{32,0},{48,16},{64,32},{80,48},{96,64},{112,80},{1... | collective-permute-start | bytes 1179656 | tf_op jit(solution)/shard_map/ppermute | solution.py:25
  184.2 10.3 %collective-permute-start.12 = (f32[8,48,256]{2,1,0:T(8,128)S(1)}, f32[8,48,256]{2,1,0:T(8,128)S(1)}, u32[]{:S(2)}, u32[]{:S(2)}) collective-permute-start(f32[8,48,256]{2,1,0:T(8,128)S(1)} %add.59), channel_id=1, source_target_pairs={{0,32},{16,48},{32,64},{48,80},{64,96},{80,112},{96,0},{112,16},{1... | collective-permute-start | bytes 1179656 | tf_op jit(solution)/shard_map/ppermute | solution.py:25
  184.3 16.8 %collective-permute-start.14 = (f32[8,48,256]{2,1,0:T(8,128)S(1)}, f32[8,48,256]{2,1,0:T(8,128)S(1)}, u32[]{:S(2)}, u32[]{:S(2)}) collective-permute-start(f32[8,48,256]{2,1,0:T(8,128)S(1)} %get-tuple-element.68), channel_id=1, source_target_pairs={{0,32},{16,48},{32,64},{48,80},{64,96},{80,112},{96,0},{112,16},{1... | collective-permute-start | bytes 1179656 | tf_op jit(solution)/shard_map/ppermute | solution.py:25
  186.3 14.8 %collective-permute-start.16 = (f32[8,48,256]{2,1,0:T(8,128)}, f32[8,48,256]{2,1,0:T(8,128)}, u32[]{:S(2)}, u32[]{:S(2)}) collective-permute-start(f32[8,48,256]{2,1,0:T(8,128)} %add.63), channel_id=1, source_target_pairs={{0,96},{16,112},{32,0},{48,16},{64,32},{80,48},{96,64},{112,80},{1... | collective-permute-start | bytes 1179656 | tf_op jit(solution)/shard_map/ppermute | solution.py:25
  188.9 17.1 %collective-permute-start.21 = (f32[8,96,256]{2,1,0:T(8,128)}, f32[8,96,256]{2,1,0:T(8,128)}, u32[]{:S(2)}, u32[]{:S(2)}) collective-permute-start(f32[8,96,256]{2,1,0:T(8,128)} %add.65.refs_16_.refs_17_.refs_36_.refs_37_), channel_id=1, source_target_pairs={{0,4},{4,8},{8,12},{12,0},{1,5},{5,9},{9,13},{13,1},{2,6},{6,10},{... | collective-permute-start | bytes 2359304 | tf_op jit(solution)/shard_map/ppermute | solution.py:23
  192.3 17.0 %collective-permute-start.23 = (f32[8,96,256]{2,1,0:T(8,128)}, f32[8,96,256]{2,1,0:T(8,128)}, u32[]{:S(2)}, u32[]{:S(2)}) collective-permute-start(f32[8,96,256]{2,1,0:T(8,128)} %add.65.refs_16_.refs_17_.refs_36_.refs_37_), channel_id=1, source_target_pairs={{0,12},{4,0},{8,4},{12,8},{1,13},{5,1},{9,5},{13,9},{2,14},{6,2},{... | collective-permute-start | bytes 2359304 | tf_op jit(solution)/shard_map/ppermute | solution.py:23
  196.4 11.4 %all-to-all-start.3 = ((f32[4,8,16,256]{3,2,1,0:T(8,128)}), f32[4,8,16,256]{3,2,1,0:T(8,128)S(1)}, u32[]{:S(2)}, u32[]{:S(2)}) async-start(f32[4,8,16,256]{3,2,1,0:T(8,128)} %bitcast.8), calls=%async_computation.3 | async-start | bytes 1048576 | tf_op jit(solution)/shard_map/all_to_all | solution.py:37
  202.9 9.4 %collective-permute-start.17 = (f32[8,48,256]{2,1,0:T(8,128)}, f32[8,48,256]{2,1,0:T(8,128)S(1)}, u32[]{:S(2)}, u32[]{:S(2)}) collective-permute-start(f32[8,48,256]{2,1,0:T(8,128)} %add_add_fusion.2), channel_id=1, source_target_pairs={{0,16},{16,0},{32,48},{48,32},{64,80},{80,64},{96,112},{112,96},{1... | collective-permute-start | bytes 1179656 | tf_op jit(solution)/shard_map/ppermute | solution.py:27
  203.2 25.8 %collective-permute-start.36 = (f32[8,96,256]{2,1,0:T(8,128)}, f32[8,96,256]{2,1,0:T(8,128)}, u32[]{:S(2)}, u32[]{:S(2)}) collective-permute-start(f32[8,96,256]{2,1,0:T(8,128)} %add.65.refs_16_.refs_17_.refs_36_.refs_37_), channel_id=1, source_target_pairs={{0,2},{1,3},{2,0},{3,1},{4,6},{5,7},{6,4},{7,5},{8,10},{9,11},{10,... | collective-permute-start | bytes 2359304 | tf_op jit(solution)/shard_map/ppermute | solution.py:29
  207.0 8.2 %collective-permute-start.22 = (f32[4,96,256]{2,1,0:T(8,128)S(1)}, f32[4,96,256]{2,1,0:T(8,128)S(1)}, u32[]{:S(2)}, u32[]{:S(2)}) collective-permute-start(f32[4,96,256]{2,1,0:T(8,128)S(1)} %slice.24), channel_id=1, source_target_pairs={{0,4},{4,8},{8,12},{12,0},{1,5},{5,9},{9,13},{13,1},{2,6},{6,10},{... | collective-permute-start | bytes 1179656 | tf_op jit(solution)/shard_map/ppermute | solution.py:23
  207.9 15.5 %collective-permute-start.18 = (f32[8,64,256]{2,1,0:T(8,128)S(1)}, f32[8,64,256]{2,1,0:T(8,128)S(1)}, u32[]{:S(2)}, u32[]{:S(2)}) collective-permute-start(f32[8,64,256]{2,1,0:T(8,128)S(1)} %bitcast.11), channel_id=1, source_target_pairs={{0,4},{4,8},{8,12},{12,0},{1,5},{5,9},{9,13},{13,1},{2,6},{6,10},{... | collective-permute-start | bytes 1572872 | tf_op jit(solution)/shard_map/ppermute | solution.py:23
  209.3 14.1 %collective-permute-start.19 = (f32[8,64,256]{2,1,0:T(8,128)S(1)}, f32[8,64,256]{2,1,0:T(8,128)S(1)}, u32[]{:S(2)}, u32[]{:S(2)}) collective-permute-start(f32[8,64,256]{2,1,0:T(8,128)S(1)} %bitcast.12), channel_id=1, source_target_pairs={{0,12},{4,0},{8,4},{12,8},{1,13},{5,1},{9,5},{13,9},{2,14},{6,2},{... | collective-permute-start | bytes 1572872 | tf_op jit(solution)/shard_map/ppermute | solution.py:23
  212.4 5.5 %copy-start.16 = (f32[8,48,256]{2,1,0:T(8,128)}, f32[8,48,256]{2,1,0:T(8,128)S(1)}, u32[]{:S(2)}) copy-start(f32[8,48,256]{2,1,0:T(8,128)S(1)} %collective-permute-done.17) | copy-start | bytes 1179652
  212.4 11.0 %collective-permute-start.24 = (f32[4,96,256]{2,1,0:T(8,128)}, f32[4,96,256]{2,1,0:T(8,128)S(1)}, u32[]{:S(2)}, u32[]{:S(2)}) collective-permute-start(f32[4,96,256]{2,1,0:T(8,128)} %slice.25), channel_id=1, source_target_pairs={{0,12},{4,0},{8,4},{12,8},{1,13},{5,1},{9,5},{13,9},{2,14},{6,2},{... | collective-permute-start | bytes 1179656 | tf_op jit(solution)/shard_map/ppermute | solution.py:23
  215.2 0.7 copy-start.1
  215.9 19.9 %collective-permute-start.28 = (f32[8,64,256]{2,1,0:T(8,128)S(1)}, f32[8,64,256]{2,1,0:T(8,128)S(1)}, u32[]{:S(2)}, u32[]{:S(2)}) collective-permute-start(f32[8,64,256]{2,1,0:T(8,128)S(1)} %bitcast.13), channel_id=1, source_target_pairs={{0,2},{1,3},{2,0},{3,1},{4,6},{5,7},{6,4},{7,5},{8,10},{9,11},{10,... | collective-permute-start | bytes 1572872 | tf_op jit(solution)/shard_map/ppermute | solution.py:29
  223.3 36.2 %copy-start.3 = (f32[4,96,256]{2,1,0:T(8,128)}, f32[4,96,256]{2,1,0:T(8,128)S(1)}, u32[]{:S(2)}) copy-start(f32[4,96,256]{2,1,0:T(8,128)S(1)} %collective-permute-done.24.refs_5_) | copy-start | bytes 1179652
  223.3 36.2 %collective-permute-start.26 = (f32[8,96,256]{2,1,0:T(8,128)S(1)}, f32[8,96,256]{2,1,0:T(8,128)S(1)}, u32[]{:S(2)}, u32[]{:S(2)}) collective-permute-start(f32[8,96,256]{2,1,0:T(8,128)S(1)} %maximum_select_fusion.refs_0_.refs_1_.refs_24_.refs_25_), channel_id=1, source_target_pairs={{0,4},{4,8},{8,12},{12,0},{1,5},{5,9},{9,13},{13,1},{2,6},{6,10},{... | collective-permute-start | bytes 2359304 | tf_op jit(solution)/shard_map/ppermute | solution.py:23
  225.1 34.5 %collective-permute-start.27 = (f32[8,96,256]{2,1,0:T(8,128)S(1)}, f32[8,96,256]{2,1,0:T(8,128)S(1)}, u32[]{:S(2)}, u32[]{:S(2)}) collective-permute-start(f32[8,96,256]{2,1,0:T(8,128)S(1)} %maximum_select_fusion.refs_0_.refs_1_.refs_24_.refs_25_), channel_id=1, source_target_pairs={{0,12},{4,0},{8,4},{12,8},{1,13},{5,1},{9,5},{13,9},{2,14},{6,2},{... | collective-permute-start | bytes 2359304 | tf_op jit(solution)/shard_map/ppermute | solution.py:23
  226.6 33.5 %collective-permute-start.29 = (f32[8,96,256]{2,1,0:T(8,128)S(1)}, f32[8,96,256]{2,1,0:T(8,128)}, u32[]{:S(2)}, u32[]{:S(2)}) collective-permute-start(f32[8,96,256]{2,1,0:T(8,128)S(1)} %maximum_select_fusion.refs_0_.refs_1_.refs_24_.refs_25_), channel_id=1, source_target_pairs={{0,2},{1,3},{2,0},{3,1},{4,6},{5,7},{6,4},{7,5},{8,10},{9,11},{10,... | collective-permute-start | bytes 2359304 | tf_op jit(solution)/shard_map/ppermute | solution.py:29
  229.0 13.0 %collective-permute-start.30 = (f32[4,64,256]{2,1,0:T(8,128)S(1)}, f32[4,64,256]{2,1,0:T(8,128)S(1)}, u32[]{:S(2)}, u32[]{:S(2)}) collective-permute-start(f32[4,64,256]{2,1,0:T(8,128)S(1)} %slice.20), channel_id=1, source_target_pairs={{0,4},{4,8},{8,12},{12,0},{1,5},{5,9},{9,13},{13,1},{2,6},{6,10},{... | collective-permute-start | bytes 786440 | tf_op jit(solution)/shard_map/ppermute | solution.py:23
  235.9 17.9 %collective-permute-start.31 = (f32[4,64,256]{2,1,0:T(8,128)S(1)}, f32[4,64,256]{2,1,0:T(8,128)S(1)}, u32[]{:S(2)}, u32[]{:S(2)}) collective-permute-start(f32[4,64,256]{2,1,0:T(8,128)S(1)} %slice.21), channel_id=1, source_target_pairs={{0,12},{4,0},{8,4},{12,8},{1,13},{5,1},{9,5},{13,9},{2,14},{6,2},{... | collective-permute-start | bytes 786440 | tf_op jit(solution)/shard_map/ppermute | solution.py:23
  242.0 21.6 %copy-start.5 = (f32[4,64,256]{2,1,0:T(8,128)}, f32[4,64,256]{2,1,0:T(8,128)S(1)}, u32[]{:S(2)}) copy-start(f32[4,64,256]{2,1,0:T(8,128)S(1)} %collective-permute-done.30.refs_2_) | copy-start | bytes 786436
  242.0 19.3 %collective-permute-start.35 = (f32[8,96,256]{2,1,0:T(8,128)}, f32[8,96,256]{2,1,0:T(8,128)}, u32[]{:S(2)}, u32[]{:S(2)}) collective-permute-start(f32[8,96,256]{2,1,0:T(8,128)} %add.65.refs_16_.refs_17_.refs_36_.refs_37_), channel_id=1, source_target_pairs={{0,1},{1,0},{2,3},{3,2},{4,5},{5,4},{6,7},{7,6},{8,9},{9,8},{10,11... | collective-permute-start | bytes 2359304 | tf_op jit(solution)/shard_map/ppermute | solution.py:30
  253.8 0.7 copy-start.7
  254.5 8.4 %collective-permute-start.37 = (f32[8,96,256]{2,1,0:T(8,128)}, f32[8,96,256]{2,1,0:T(8,128)S(1)}, u32[]{:S(2)}, u32[]{:S(2)}) collective-permute-start(f32[8,96,256]{2,1,0:T(8,128)} %collective-permute-done.36.refs_20_.refs_21_), channel_id=1, source_target_pairs={{0,1},{1,0},{2,3},{3,2},{4,5},{5,4},{6,7},{7,6},{8,9},{9,8},{10,11... | collective-permute-start | bytes 2359304 | tf_op jit(solution)/shard_map/ppermute | solution.py:30
  259.6 4.0 %copy-start.11 = (f32[8,96,256]{2,1,0:T(8,128)}, f32[8,96,256]{2,1,0:T(8,128)S(1)}, u32[]{:S(2)}) copy-start(f32[8,96,256]{2,1,0:T(8,128)S(1)} %collective-permute-done.26.refs_28_.refs_29_) | copy-start | bytes 2359300
  259.6 4.0 %collective-permute-start.33 = (f32[8,64,256]{2,1,0:T(8,128)S(1)}, f32[8,64,256]{2,1,0:T(8,128)S(1)}, u32[]{:S(2)}, u32[]{:S(2)}) collective-permute-start(f32[8,64,256]{2,1,0:T(8,128)S(1)} %bitcast.14), channel_id=1, source_target_pairs={{0,1},{1,0},{2,3},{3,2},{4,5},{5,4},{6,7},{7,6},{8,9},{9,8},{10,11... | collective-permute-start | bytes 1572872 | tf_op jit(solution)/shard_map/ppermute | solution.py:30
  259.7 3.9 %copy-start.12 = (f32[8,96,256]{2,1,0:T(8,128)}, f32[8,96,256]{2,1,0:T(8,128)S(1)}, u32[]{:S(2)}) copy-start(f32[8,96,256]{2,1,0:T(8,128)S(1)} %collective-permute-done.27.refs_26_.refs_27_) | copy-start | bytes 2359300
  259.7 6.1 %collective-permute-start.25 = (f32[8,96,256]{2,1,0:T(8,128)S(1)}, f32[8,96,256]{2,1,0:T(8,128)}, u32[]{:S(2)}, u32[]{:S(2)}) collective-permute-start(f32[8,96,256]{2,1,0:T(8,128)S(1)} %maximum_select_fusion.refs_0_.refs_1_.refs_24_.refs_25_), channel_id=1, source_target_pairs={{0,1},{1,0},{2,3},{3,2},{4,5},{5,4},{6,7},{7,6},{8,9},{9,8},{10,11... | collective-permute-start | bytes 2359304 | tf_op jit(solution)/shard_map/ppermute | solution.py:30
  260.2 5.6 %collective-permute-start.32 = (f32[8,96,256]{2,1,0:T(8,128)}, f32[8,96,256]{2,1,0:T(8,128)}, u32[]{:S(2)}, u32[]{:S(2)}) collective-permute-start(f32[8,96,256]{2,1,0:T(8,128)} %collective-permute-done.29.refs_4_.refs_5_), channel_id=1, source_target_pairs={{0,1},{1,0},{2,3},{3,2},{4,5},{5,4},{6,7},{7,6},{8,9},{9,8},{10,11... | collective-permute-start | bytes 2359304 | tf_op jit(solution)/shard_map/ppermute | solution.py:30
  261.3 4.5 %collective-permute-start.34 = (f32[8,64,256]{2,1,0:T(8,128)S(1)}, f32[8,64,256]{2,1,0:T(8,128)}, u32[]{:S(2)}, u32[]{:S(2)}) collective-permute-start(f32[8,64,256]{2,1,0:T(8,128)S(1)} %collective-permute-done.28.refs_12_.refs_13_), channel_id=1, source_target_pairs={{0,1},{1,0},{2,3},{3,2},{4,5},{5,4},{6,7},{7,6},{8,9},{9,8},{10,11... | collective-permute-start | bytes 1572872 | tf_op jit(solution)/shard_map/ppermute | solution.py:30
  262.9 0.9 copy-start.14
  262.9 14.0 %collective-permute-start.38 = (f32[4,96,256]{2,1,0:T(8,128)}, f32[4,96,256]{2,1,0:T(8,128)}, u32[]{:S(2)}, u32[]{:S(2)}) collective-permute-start(f32[4,96,256]{2,1,0:T(8,128)} %slice.22), channel_id=1, source_target_pairs={{0,4},{4,8},{8,12},{12,0},{1,5},{5,9},{9,13},{13,1},{2,6},{6,10},{... | collective-permute-start | bytes 1179656 | tf_op jit(solution)/shard_map/ppermute | solution.py:23
  263.7 13.2 %collective-permute-start.39 = (f32[4,96,256]{2,1,0:T(8,128)}, f32[4,96,256]{2,1,0:T(8,128)}, u32[]{:S(2)}, u32[]{:S(2)}) collective-permute-start(f32[4,96,256]{2,1,0:T(8,128)} %slice.23), channel_id=1, source_target_pairs={{0,12},{4,0},{8,4},{12,8},{1,13},{5,1},{9,5},{13,9},{2,14},{6,2},{... | collective-permute-start | bytes 1179656 | tf_op jit(solution)/shard_map/ppermute | solution.py:23
  265.8 11.2 %copy-start.2 = (f32[4,96,256]{2,1,0:T(8,128)S(1)}, f32[4,96,256]{2,1,0:T(8,128)}, u32[]{:S(2)}) copy-start(f32[4,96,256]{2,1,0:T(8,128)} %copy-done.1) | copy-start | bytes 1179652
  265.8 11.2 %copy-start.4 = (f32[4,96,256]{2,1,0:T(8,128)S(1)}, f32[4,96,256]{2,1,0:T(8,128)}, u32[]{:S(2)}) copy-start(f32[4,96,256]{2,1,0:T(8,128)} %copy-done.3) | copy-start | bytes 1179652
  265.8 11.2 %copy-start.6 = (f32[4,64,256]{2,1,0:T(8,128)S(1)}, f32[4,64,256]{2,1,0:T(8,128)}, u32[]{:S(2)}) copy-start(f32[4,64,256]{2,1,0:T(8,128)} %copy-done.5) | copy-start | bytes 786436
  265.8 11.2 %copy-start.8 = (f32[4,64,256]{2,1,0:T(8,128)S(1)}, f32[4,64,256]{2,1,0:T(8,128)}, u32[]{:S(2)}) copy-start(f32[4,64,256]{2,1,0:T(8,128)} %copy-done.7) | copy-start | bytes 786436

commit v4 on v3

--- a/solution.py
+++ b/solution.py
@@ -167,7 +167,7 @@
 
 def dft_by_owner(index, w, x, us):
     n, _, rows, _ = x.shape
-    block = 16
+    block = {96: 32, 48: 24}[rows]
     flat = call(
         functools.partial(dft_owner_kernel, block),
         index,
@@ -238,52 +238,66 @@
     return hi, (x - hi.astype(jnp.float32)).astype(jnp.bfloat16)
 
 
-def dots(a, b, out, total):
+def store_left(a_ref, block, rows, real, imag):
+    for part, x in enumerate((real, imag, real + imag)):
+        hi, lo = split(x)
+        a_ref[block, part, rows, 0:256] = hi
+        a_ref[block, part, rows, 256:512] = hi
+        a_ref[block, part, rows, 512:768] = lo
+
+
+def store_right(b_ref, block, rows, real, imag):
+    for part, x in enumerate((real, imag, real + imag)):
+        hi, lo = split(x)
+        b_ref[block, part, rows] = hi
+        b_ref[block, part, slice(256 + rows.start, 256 + rows.stop)] = lo
+        b_ref[block, part, slice(512 + rows.start, 512 + rows.stop)] = hi
+
+
+def dots(pairs, out, real, imag):
     def dot(x, y):
         return jnp.dot(x, y, preferred_element_type=jnp.float32)
 
-    rr, ri = total
-    ii, ir = jnp.zeros((256, C), jnp.float32), jnp.zeros((256, C), jnp.float32)
-    for (arh, arl, aih, ail), (brh, brl, bih, bil) in zip(a, b):
-        rr += dot(arh, brh) + dot(arh, brl) + dot(arl, brh)
-        ii += dot(aih, bih) + dot(aih, bil) + dot(ail, bih)
-        ri += dot(arh, bih) + dot(arh, bil) + dot(arl, bih)
-        ir += dot(aih, brh) + dot(aih, brl) + dot(ail, brh)
-    out[0, 0] = rr - ii
-    out[1, 0] = ri + ir
+    for a, b in pairs:
+        rr, ii, both = (dot(a[part], b[part]) for part in range(3))
+        real = real + (rr - ii)
+        imag = imag + (both - rr - ii)
+    out[0, 0] = real
+    out[1, 0] = imag
 
 
 def near_kernel(left_rows, right_rows, index, *refs):
-    n, m = 8 * len(left_rows), 6 * len(right_rows)
+    n, m = 4 * len(left_rows), 3 * len(right_rows)
     left, right = refs[:n], refs[n : n + m]
     out, kept, a_ref, b_ref = refs[n + m :]
     col, z = index[0], index[1]
-    for part in range(2):
-        for i, rows in enumerate(left_rows):
-            for e in range(4):
-                hi, lo = split(left[8 * i + 2 * e + part][0])
-                a_ref[col ^ e, 2 * part, rows] = hi
-                a_ref[col ^ e, 2 * part + 1, rows] = lo
-        for i, rows in enumerate(right_rows):
-            for t in range(3):
-                hi, lo = split(right[6 * i + 2 * t + part][0])
-                b_ref[t, 2 * part, rows] = hi
-                b_ref[t, 2 * part + 1, rows] = lo
-    zero = jnp.zeros((256, C), jnp.float32)
-    a = [[a_ref[(z + r) % 4, j] for j in range(4)] for r in (0, 1, 3)]
-    dots(a, [[b_ref[t, j] for j in range(4)] for t in range(3)], out, (zero, zero))
-    kept[0] = a_ref[(z + 2) % 4]
+    for i, rows in enumerate(left_rows):
+        for e in range(4):
+            x = left[4 * i + e]
+            store_left(a_ref, col ^ e, rows, x[0, 0], x[1, 0])
+
+            @pl.when((col ^ e) == (z + 2) % 4)
+            def _(x=x, rows=rows):
+                kept[:, 0, rows] = x[:, 0]
+
+    for i, rows in enumerate(right_rows):
+        for t in range(3):
+            x = right[3 * i + t]
+            store_right(b_ref, t, rows, x[0, 0], x[1, 0])
+    pairs = []
+    for t, r in enumerate((0, 1, 3)):
+        k = (z + r) % 4
+        pairs.append(([a_ref[k, part] for part in range(3)], [b_ref[t, part] for part in range(3)]))
+    dots(pairs, out, 0.0, 0.0)
 
 
 def far_kernel(right_rows, _, total, kept, *refs):
-    out, b_ref = refs[-2:]
+    out, a_ref, b_ref = refs[-3:]
+    store_left(a_ref, 0, slice(0, 256), kept[0, 0], kept[1, 0])
     for i, rows in enumerate(right_rows):
-        for part in range(2):
-            hi, lo = split(refs[2 * i + part][0])
-            b_ref[2 * part, rows] = hi
-            b_ref[2 * part + 1, rows] = lo
-    a, b = [kept[0, j] for j in range(4)], [b_ref[j] for j in range(4)]
-    dots([a], [b], out, (total[0, 0], total[1, 0]))
+        store_right(b_ref, 0, rows, refs[2 * i][0], refs[2 * i + 1][0])
+    pair = ([a_ref[0, part] for part in range(3)], [b_ref[0, part] for part in range(3)])
+    dots([pair], out, total[0, 0], total[1, 0])
 
 
 def product(index, left, right, across, left_starts, right_starts):
@@ -293,42 +307,42 @@
     left_rows, right_rows = segments(left, left_starts), segments(right, right_starts)
     sizes = [part[0].shape[1] for part in right]
 
-    def spec(rows, first):
-        return pl.BlockSpec((1, rows, C), lambda g, _: (first + g, 0, 0))
+    def spec(rows):
+        return pl.BlockSpec((1, rows, C), lambda g, _: (g, 0, 0))
 
     def both(groups):
         operands, specs = [], []
         for arrays in groups:
             for array in arrays:
-                operands += [array, array]
-                specs += [spec(array.shape[1], 0), spec(array.shape[1], 4)]
+                rows = array.shape[1]
+                operands.append(array.reshape(2, 4, rows, C))
+                specs.append(pl.BlockSpec((2, 1, rows, C), lambda g, _: (0, g, 0, 0)))
         return operands, specs
 
     left, left_specs = both(left)
     right, right_specs = both(right)
     out_spec = pl.BlockSpec((2, 1, 256, C), lambda g, _: (0, g, 0, 0))
-    kept_spec = pl.BlockSpec((1, 4, 256, C), lambda g, _: (g, 0, 0, 0))
     total, kept = call(
         functools.partial(near_kernel, left_rows, right_rows),
         index,
         left + right,
         (4,),
         left_specs + right_specs,
-        [out_spec, kept_spec],
-        [f32(2, 4, 256, C), jax.ShapeDtypeStruct((4, 4, 256, C), jnp.bfloat16)],
+        [out_spec, out_spec],
+        [f32(2, 4, 256, C)] * 2,
         11,
-        [pltpu.VMEM((4, 4, 256, C), jnp.bfloat16), pltpu.VMEM((3, 4, 256, C), jnp.bfloat16)],
+        [pltpu.VMEM((4, 3, 256, 768), jnp.bfloat16), pltpu.VMEM((3, 3, 768, C), jnp.bfloat16)],
     )
     return call(
         functools.partial(far_kernel, right_rows),
         index,
         [total, kept] + [array for pair in across for array in pair],
         (4,),
-        [out_spec, kept_spec] + [spec(rows, 0) for rows in sizes for _ in range(2)],
+        [out_spec, out_spec] + [spec(rows) for rows in sizes for _ in range(2)],
         out_spec,
         f32(2, 4, 256, C),
         4,
-        [pltpu.VMEM((4, 256, C), jnp.bfloat16)],
+        [pltpu.VMEM((1, 3, 256, 768), jnp.bfloat16), pltpu.VMEM((1, 3, 768, C), jnp.bfloat16)],
     )
 
 
@@ -380,7 +394,7 @@
     own2 = jnp.transpose(own2, (1, 0, 2, 3)).reshape(8, R2, C)
     across1 = across_z(below1, above1)
     below2, above2 = near_z(own2)
-    mine3, other3 = together(mine3, other3)
+    mine3, other3, far1 = together(mine3, other3, far1)
 
     other3 = shift(other3, "x_lo")
     own3 = jnp.where(x_lo == 0, jnp.concatenate([mine3, other3], axis=1), jnp.concatenate([other3, mine3], axis=1))

time: 284 us -> 282 us (level)
  waiting for transfers between devices: 112 us -> 120 us
  starting transfers between devices: 86.8 us -> 79.2 us
    ppermute x12, waiting for transfers between devices: 8.69 us -> 17.1 us  [shift(): return lax.ppermute(x, 'row', [(i, (i + by) % 4) for i in range(4)])]
    ppermute x6, starting transfers between devices: 18.5 us -> 11.2 us  [shift(): return lax.ppermute(x, 'col', [(i, i ^ 1) for i in range(4)])]
    ppermute x3, waiting for transfers between devices: 6.37 us -> 0.01 us  [shift(): return lax.ppermute(x, 'col', [(i, i ^ 2) for i in range(4)])]
    all_to_all x1, waiting for transfers between devices: 0.02 us -> 5.29 us  [exchange(): lax.all_to_all(x, 'freq', split_axis=0, concat_axis=0, tiled=True, axis_i...]
  transfers between devices with their start and end apart: 44 -> 44, of which waited for: 16 -> 19; matrix products, arithmetic and copies ran while one was open for 6% -> 6% of each run, Pallas kernels for 18% -> 17%
where the time goes in v4:
time: 282 us; the launch traced here: 280 us
  waiting for transfers between devices  120 us (43%)
  starting transfers between devices  79.2 us (28%)
  Pallas kernels  62.4 us (22%)
  other arithmetic  11.8 us (4%)
  local copies, waits for them, and re-layouts  7.19 us (3%)
    ppermute x15, waiting for transfers between devices, shift(): return lax.ppermute(x, 'freq', [(i, (i + 2 * by) % 8) for i in range(8)])  86.8 us
    pallas_call x11, Pallas kernels, call(): pl.pallas_call(kernel, grid_spec=pltpu.PrefetchScalarGridSpec(num_scalar_...  60.4 us
    ppermute x15, starting transfers between devices, shift(): return lax.ppermute(x, 'freq', [(i, (i + 2 * by) % 8) for i in range(8)])  20.1 us
    ppermute x12, waiting for transfers between devices, shift(): return lax.ppermute(x, 'row', [(i, (i + by) % 4) for i in range(4)])  17.1 us
    ppermute x12, starting transfers between devices, shift(): return lax.ppermute(x, 'row', [(i, (i + by) % 4) for i in range(4)])  17 us
    all_to_all x3, starting transfers between devices, exchange(): return lax.all_to_all(x, 'row', split_axis=0, concat_axis=0, tiled=True)  15.1 us
    ppermute x6, starting transfers between devices, shift(): return lax.ppermute(x, 'col', [(i, i ^ 1) for i in range(4)])  11.2 us
    ppermute x3, starting transfers between devices, shift(): return lax.ppermute(x, 'col', [(i, i ^ 2) for i in range(4)])  7.35 us
  transfers between devices with their start and end apart: 44, of which 19 were waited for; matrix products, arithmetic and copies ran while one was open for 6% of the time, Pallas kernels for 17%

profile of v4, /device:TPU:1, one launch (start us, length us, event | category | flops | bytes accessed | tf_op | source)
XLA Modules:
  0.0 280.5 jit_solution(8893669919657830602)
XLA Ops:
  0.1 5.8 %shard_map.46 = f32[4,16,96,256]{3,2,1,0:T(8,128)} custom-call(s32[4]{0:T(128)S(1)} %pad_add_fusion.1.index._, f32[16,4,256,256]{3,2,1,0:T(8,128)} %bitcast.41), custom_call_target="tpu_custom_call" | custom-call | bytes 18000000 | tf_op jit(solution)/shard_map/pallas_call | solution.py:49
  5.9 5.9 %all-to-all-start = ((f32[4,16,96,256]{3,2,1,0:T(8,128)}), f32[4,16,96,256]{3,2,1,0:T(8,128)}, u32[]{:S(2)}, u32[]{:S(2)}) async-start(f32[4,16,96,256]{3,2,1,0:T(8,128)} %shard_map.46), calls=%async_computation | async-start | bytes 12582912 | tf_op jit(solution)/shard_map/all_to_all | solution.py:35
  11.7 3.4 %shard_map.52 = f32[4,16,48,256]{3,2,1,0:T(8,128)} custom-call(s32[4]{0:T(128)S(1)} %pad_add_fusion.1.index._, f32[16,4,256,256]{3,2,1,0:T(8,128)} %bitcast.42), custom_call_target="tpu_custom_call" | custom-call | bytes 10800000 | tf_op jit(solution)/shard_map/pallas_call | solution.py:49
  15.2 1.6 collective-permute-start.3
  16.7 2.8 shard_map.47
  19.5 1.4 collective-permute-start
  20.9 2.8 shard_map.48
  23.7 2.7 collective-permute-start.1
  26.4 2.8 shard_map.49
  29.2 1.1 collective-permute-start.2
  30.3 3.4 %shard_map.51.joined_ref = f32[4,2,16,48,256]{4,3,2,1,0:T(8,128)} custom-call(s32[4]{0:T(128)S(1)} %pad_add_fusion.1.index._, f32[16,4,256,256]{3,2,1,0:T(8,128)} %bitcast.46), custom_call_target="tpu_custom_call" | custom-call | bytes 10800000 | tf_op jit(solution)/shard_map/pallas_call | solution.py:49
  33.8 11.2 %collective-permute-done.refs_1_ = f32[16,4,16,256]{3,2,1,0:T(8,128)} collective-permute-done((f32[16,4,16,256]{3,2,1,0:T(8,128)}, f32[16,4,16,256]{3,2,1,0:T(8,128)}, u32[]{:S(2)}, u32[]{:S(2)}) %collective-permute-start) | collective-permute-done | bytes 1048608 | tf_op jit(solution)/shard_map/ppermute | solution.py:25
  44.9 23.6 %collective-permute-done.1.refs_2_ = f32[16,4,16,256]{3,2,1,0:T(8,128)} collective-permute-done((f32[16,4,16,256]{3,2,1,0:T(8,128)}, f32[16,4,16,256]{3,2,1,0:T(8,128)}, u32[]{:S(2)}, u32[]{:S(2)}) %collective-permute-start.1) | collective-permute-done | bytes 1048608 | tf_op jit(solution)/shard_map/ppermute | solution.py:25
  68.5 2.7 collective-permute-done.2.refs_3_
  71.2 1.2 copy-done
  72.4 7.2 %shard_map.50 = (f32[4,32,16,256]{3,2,1,0:T(8,128)}, f32[4,32,16,256]{3,2,1,0:T(8,128)}) custom-call(s32[2]{0:T(128)S(1)} %pad_add_fusion.2._, f32[32,64,64]{2,1,0:T(8,128)S(1)} %copy-done, f32[16,4,256,256]{3,2,1,0:T(8,128)} %bitcast.47, f32[16,4,16,256]{3,2,1,0:T(8,128)} %collective-permute-done.refs_1_, ...), custom_call_target="tpu_custom_call" | custom-call | bytes 25200000 | tf_op jit(solution)/shard_map/pallas_call | solution.py:49
  79.6 4.7 %collective-permute-done.3.far_ref = f32[4,16,48,256]{3,2,1,0:T(8,128)S(1)} collective-permute-done((f32[4,16,48,256]{3,2,1,0:T(8,128)}, f32[4,16,48,256]{3,2,1,0:T(8,128)S(1)}, u32[]{:S(2)}, u32[]{:S(2)}) %collective-permute-start.3) | collective-permute-done | bytes 3145760 | tf_op jit(solution)/shard_map/ppermute | solution.py:27
  84.3 2.0 shard_map.54
  86.3 5.6 %all-to-all-start.1 = ((f32[4,2,16,48,256]{4,3,2,1,0:T(8,128)}), f32[4,2,16,48,256]{4,3,2,1,0:T(8,128)}, u32[]{:S(2)}, u32[]{:S(2)}) async-start(f32[4,2,16,48,256]{4,3,2,1,0:T(8,128)} %shard_map.54), calls=%async_computation.1 | async-start | bytes 12582912 | tf_op jit(solution)/shard_map/all_to_all | solution.py:35
  91.9 9.0 %shard_map.53 = (f32[8,96,256]{2,1,0:T(8,128)S(1)}, f32[8,96,256]{2,1,0:T(8,128)S(1)}, f32[8,96,256]{2,1,0:T(8,128)S(1)}, f32[8,96,256]{2,1,0:T(8,128)S(1)}, f32...) custom-call(s32[4]{0:T(128)S(1)} %pad_add_fusion.1.index._, ...), custom_call_target="tpu_custom_call" | custom-call | bytes 32400000 | tf_op jit(solution)/shard_map/pallas_call | solution.py:49
  100.9 1.6 collective-permute-start.4
  102.5 1.2 collective-permute-start.10
  103.7 1.5 collective-permute-start.8
  105.2 1.4 collective-permute-start.6
  106.6 13.7 %collective-permute-done.4 = f32[8,96,256]{2,1,0:T(8,128)S(1)} collective-permute-done((f32[8,96,256]{2,1,0:T(8,128)}, f32[8,96,256]{2,1,0:T(8,128)S(1)}, u32[]{:S(2)}, u32[]{:S(2)}) %collective-permute-start.4) | collective-permute-done | bytes 786464 | tf_op jit(solution)/shard_map/ppermute | solution.py:25
  120.5 1.2 collective-permute-start.7
  121.7 1.3 add.56
  123.0 2.1 collective-permute-start.9
  125.2 12.6 %collective-permute-done.6 = f32[8,96,256]{2,1,0:T(8,128)S(1)} collective-permute-done((f32[8,96,256]{2,1,0:T(8,128)}, f32[8,96,256]{2,1,0:T(8,128)S(1)}, u32[]{:S(2)}, u32[]{:S(2)}) %collective-permute-start.6) | collective-permute-done | bytes 786464 | tf_op jit(solution)/shard_map/ppermute | solution.py:25
  138.6 1.1 add_add_fusion.1
  139.7 15.8 %collective-permute-done.7 = f32[8,96,256]{2,1,0:T(8,128)S(1)} collective-permute-done((f32[8,96,256]{2,1,0:T(8,128)S(1)}, f32[8,96,256]{2,1,0:T(8,128)S(1)}, u32[]{:S(2)}, u32[]{:S(2)}) %collective-permute-start.7) | collective-permute-done | bytes 786464 | tf_op jit(solution)/shard_map/ppermute | solution.py:25
  156.5 1.8 add.58
  158.3 4.5 %all-to-all-done.1 = f32[4,2,16,48,256]{4,3,2,1,0:T(8,128)} async-done(((f32[4,2,16,48,256]{4,3,2,1,0:T(8,128)}), f32[4,2,16,48,256]{4,3,2,1,0:T(8,128)}, u32[]{:S(2)}, u32[]{:S(2)}) %all-to-all-start.1) | async-done | bytes 6291488 | tf_op jit(solution)/shard_map/all_to_all | solution.py:35
  162.8 3.6 %all-to-all-start.2 = ((f32[4,32,16,256]{3,2,1,0:T(8,128)}), f32[4,32,16,256]{3,2,1,0:T(8,128)S(1)}, u32[]{:S(2)}, u32[]{:S(2)}) async-start(f32[4,32,16,256]{3,2,1,0:T(8,128)} %add.58), calls=%async_computation.2 | async-start | bytes 4194304 | tf_op jit(solution)/shard_map/all_to_all | solution.py:35
  166.5 1.3 collective-permute-start.17
  167.8 7.0 %shard_map.55 = (f32[8,48,256]{2,1,0:T(8,128)S(1)}, f32[8,48,256]{2,1,0:T(8,128)S(1)}, f32[8,48,256]{2,1,0:T(8,128)S(1)}, f32[8,48,256]{2,1,0:T(8,128)S(1)}, f32...) custom-call(s32[4]{0:T(128)S(1)} %pad_add_fusion.1.index._, ...), custom_call_target="tpu_custom_call" | custom-call | bytes 25200000 | tf_op jit(solution)/shard_map/pallas_call | solution.py:49
  174.7 1.4 collective-permute-start.11
  176.1 1.5 collective-permute-start.15
  177.6 1.4 collective-permute-start.13
  179.0 5.1 %collective-permute-done.11 = f32[8,48,256]{2,1,0:T(8,128)S(1)} collective-permute-done((f32[8,48,256]{2,1,0:T(8,128)S(1)}, f32[8,48,256]{2,1,0:T(8,128)S(1)}, u32[]{:S(2)}, u32[]{:S(2)}) %collective-permute-start.11) | collective-permute-done | bytes 393248 | tf_op jit(solution)/shard_map/ppermute | solution.py:25
  185.3 2.5 collective-permute-start.18
  187.7 1.2 collective-permute-start.14
  189.8 1.5 collective-permute-start.16
  193.3 1.6 collective-permute-start.24
  196.8 4.1 %all-to-all-start.3 = ((f32[4,8,16,256]{3,2,1,0:T(8,128)}), f32[4,8,16,256]{3,2,1,0:T(8,128)S(1)}, u32[]{:S(2)}, u32[]{:S(2)}) async-start(f32[4,8,16,256]{3,2,1,0:T(8,128)} %bitcast.8), calls=%async_computation.3 | async-start | bytes 1048576 | tf_op jit(solution)/shard_map/all_to_all | solution.py:37
  201.3 1.1 add_add_fusion.2
  202.6 5.3 %all-to-all-done.3 = f32[4,8,16,256]{3,2,1,0:T(8,128)S(1)} async-done(((f32[4,8,16,256]{3,2,1,0:T(8,128)}), f32[4,8,16,256]{3,2,1,0:T(8,128)S(1)}, u32[]{:S(2)}, u32[]{:S(2)}) %all-to-all-start.3) | async-done | bytes 524320 | tf_op jit(solution)/shard_map/all_to_all | solution.py:37
  207.9 1.3 collective-permute-start.20
  209.2 1.4 collective-permute-start.21
  210.6 1.8 slice.24
  212.5 1.8 slice.25
  214.2 2.6 collective-permute-start.25
  216.9 2.5 collective-permute-start.29
  219.3 1.5 maximum_select_fusion
  220.8 3.5 %collective-permute-done.23.refs_4_ = f32[4,96,256]{2,1,0:T(8,128)S(1)} collective-permute-done((f32[4,96,256]{2,1,0:T(8,128)}, f32[4,96,256]{2,1,0:T(8,128)S(1)}, u32[]{:S(2)}, u32[]{:S(2)}) %collective-permute-start.23) | collective-permute-done | bytes 393248 | tf_op jit(solution)/shard_map/ppermute | solution.py:23
  225.1 1.2 collective-permute-start.27
  226.3 1.7 collective-permute-start.28
  228.0 2.4 collective-permute-start.30
  230.6 2.7 collective-permute-start.32
  233.3 12.7 %collective-permute-done.31.refs_2_ = f32[4,64,256]{2,1,0:T(8,128)S(1)} collective-permute-done((f32[4,64,256]{2,1,0:T(8,128)S(1)}, f32[4,64,256]{2,1,0:T(8,128)S(1)}, u32[]{:S(2)}, u32[]{:S(2)}) %collective-permute-start.31) | collective-permute-done | bytes 262176 | tf_op jit(solution)/shard_map/ppermute | solution.py:23
  246.0 9.7 %collective-permute-start.36 = (f32[8,96,256]{2,1,0:T(8,128)}, f32[8,96,256]{2,1,0:T(8,128)}, u32[]{:S(2)}, u32[]{:S(2)}) collective-permute-start(f32[8,96,256]{2,1,0:T(8,128)} %add.65), channel_id=1, source_target_pairs={{0,1},{1,0},{2,3},{3,2},{4,5},{5,4},{6,7},{7,6},{8,9},{9,8},{10,11... | collective-permute-start | bytes 2359304 | tf_op jit(solution)/shard_map/ppermute | solution.py:30
  261.0 3.0 %collective-permute-start.39 = (f32[4,96,256]{2,1,0:T(8,128)}, f32[4,96,256]{2,1,0:T(8,128)}, u32[]{:S(2)}, u32[]{:S(2)}) collective-permute-start(f32[4,96,256]{2,1,0:T(8,128)} %slice.23), channel_id=1, source_target_pairs={{0,12},{4,0},{8,4},{12,8},{1,13},{5,1},{9,5},{13,9},{2,14},{6,2},{... | collective-permute-start | bytes 1179656 | tf_op jit(solution)/shard_map/ppermute | solution.py:23
  264.2 10.5 %shard_map.56 = (f32[2,4,256,256]{3,2,1,0:T(8,128)}, f32[2,4,256,256]{3,2,1,0:T(8,128)}) custom-call(s32[2]{0:T(128)S(1)} %pad_add_fusion.index._, f32[2,4,96,256]{3,2,1,0:T(8,128)S(1)} %bitcast.29, f32[2,4,96,256]{3,2,1,0:T(8,128)} %bitcast.12.refs_1_, f32[2,4,96,256]{3,2,1,0:T(8,128)} %bitcast.13.refs_2_, f32[2,4,96,256]{3,2,1,0:T(8,128)} %bitcast.14.refs_3_, ...), custom_call_target="tpu_custom_call" | custom-call | bytes 39600000 | tf_op jit(solution)/shard_map/pallas_call | solution.py:49
  274.7 5.8 %shard_map.57 = f32[2,4,256,256]{3,2,1,0:T(8,128)} custom-call(s32[2]{0:T(128)S(1)} %pad_add_fusion.index._, f32[2,4,256,256]{3,2,1,0:T(8,128)} %get-tuple-element.85.total, f32[2,4,256,256]{3,2,1,0:T(8,128)} %get-tuple-element.86.kept, f32[4,96,256]{2,1,0:T(8,128)} %collective-permute-done.38.refs_0_, f32[4,96,256]{2,1,0:T(8,128)} %collective-permute-done.39.refs_1_, ...), custom_call_target="tpu_custom_call" | custom-call | bytes 14400000 | tf_op jit(solution)/shard_map/pallas_call | solution.py:49
  (88 shorter events, 15.1 us)
Async XLA Ops:
  5.9 78.4 %all-to-all-start = ((f32[4,16,96,256]{3,2,1,0:T(8,128)}), f32[4,16,96,256]{3,2,1,0:T(8,128)}, u32[]{:S(2)}, u32[]{:S(2)}) async-start(f32[4,16,96,256]{3,2,1,0:T(8,128)} %shard_map.46), calls=%async_computation | async-start | bytes 12582912 | tf_op jit(solution)/shard_map/all_to_all | solution.py:35
  15.2 69.1 %collective-permute-start.3 = (f32[4,16,48,256]{3,2,1,0:T(8,128)}, f32[4,16,48,256]{3,2,1,0:T(8,128)S(1)}, u32[]{:S(2)}, u32[]{:S(2)}) collective-permute-start(f32[4,16,48,256]{3,2,1,0:T(8,128)} %shard_map.52), channel_id=1, source_target_pairs={{0,16},{16,0},{32,48},{48,32},{64,80},{80,64},{96,112},{112,96},{1... | collective-permute-start | bytes 9437192 | tf_op jit(solution)/shard_map/ppermute | solution.py:27
  19.5 25.4 %collective-permute-start = (f32[16,4,16,256]{3,2,1,0:T(8,128)}, f32[16,4,16,256]{3,2,1,0:T(8,128)}, u32[]{:S(2)}, u32[]{:S(2)}) collective-permute-start(f32[16,4,16,256]{3,2,1,0:T(8,128)} %shard_map.47), channel_id=1, source_target_pairs={{0,32},{16,48},{32,64},{48,80},{64,96},{80,112},{96,0},{112,16},{1... | collective-permute-start | bytes 3145736 | tf_op jit(solution)/shard_map/ppermute | solution.py:25
  23.7 44.8 %collective-permute-start.1 = (f32[16,4,16,256]{3,2,1,0:T(8,128)}, f32[16,4,16,256]{3,2,1,0:T(8,128)}, u32[]{:S(2)}, u32[]{:S(2)}) collective-permute-start(f32[16,4,16,256]{3,2,1,0:T(8,128)} %shard_map.48), channel_id=1, source_target_pairs={{0,64},{16,80},{32,96},{48,112},{64,0},{80,16},{96,32},{112,48},{1... | collective-permute-start | bytes 3145736 | tf_op jit(solution)/shard_map/ppermute | solution.py:25
  29.2 42.0 %collective-permute-start.2 = (f32[16,4,16,256]{3,2,1,0:T(8,128)}, f32[16,4,16,256]{3,2,1,0:T(8,128)}, u32[]{:S(2)}, u32[]{:S(2)}) collective-permute-start(f32[16,4,16,256]{3,2,1,0:T(8,128)} %shard_map.49), channel_id=1, source_target_pairs={{0,96},{16,112},{32,0},{48,16},{64,32},{80,48},{96,64},{112,80},{1... | collective-permute-start | bytes 3145736 | tf_op jit(solution)/shard_map/ppermute | solution.py:25
  71.2 1.2 copy-start
  86.3 5.6 %copy-start.8 = (f32[8,64,64]{2,1,0:T(8,128)S(1)}, f32[8,64,64]{2,1,0:T(8,128)}, u32[]{:S(2)}) copy-start(f32[8,64,64]{2,1,0:T(8,128)} %constant.51.clone.w_ref) | copy-start | bytes 393220
  86.3 76.6 %all-to-all-start.1 = ((f32[4,2,16,48,256]{4,3,2,1,0:T(8,128)}), f32[4,2,16,48,256]{4,3,2,1,0:T(8,128)}, u32[]{:S(2)}, u32[]{:S(2)}) async-start(f32[4,2,16,48,256]{4,3,2,1,0:T(8,128)} %shard_map.54), calls=%async_computation.1 | async-start | bytes 12582912 | tf_op jit(solution)/shard_map/all_to_all | solution.py:35
  91.9 10.6 %copy-start.14 = (f32[4,32,16,256]{3,2,1,0:T(8,128)S(1)}, f32[4,32,16,256]{3,2,1,0:T(8,128)}, u32[]{:S(2)}) copy-start(f32[4,32,16,256]{3,2,1,0:T(8,128)} %get-tuple-element.60) | copy-start | bytes 6291460
  100.9 19.5 %collective-permute-start.4 = (f32[8,96,256]{2,1,0:T(8,128)}, f32[8,96,256]{2,1,0:T(8,128)S(1)}, u32[]{:S(2)}, u32[]{:S(2)}) collective-permute-start(f32[8,96,256]{2,1,0:T(8,128)} %get-tuple-element.53), channel_id=1, source_target_pairs={{0,32},{16,48},{32,64},{48,80},{64,96},{80,112},{96,0},{112,16},{1... | collective-permute-start | bytes 2359304 | tf_op jit(solution)/shard_map/ppermute | solution.py:25
  102.5 54.0 %collective-permute-start.10 = (f32[4,32,16,256]{3,2,1,0:T(8,128)S(1)}, f32[4,32,16,256]{3,2,1,0:T(8,128)S(1)}, u32[]{:S(2)}, u32[]{:S(2)}) collective-permute-start(f32[4,32,16,256]{3,2,1,0:T(8,128)S(1)} %copy-done.14), channel_id=1, source_target_pairs={{0,16},{16,0},{32,48},{48,32},{64,80},{80,64},{96,112},{112,96},{1... | collective-permute-start | bytes 6291464 | tf_op jit(solution)/shard_map/ppermute | solution.py:27
  103.7 18.0 %collective-permute-start.8 = (f32[8,96,256]{2,1,0:T(8,128)}, f32[8,96,256]{2,1,0:T(8,128)S(1)}, u32[]{:S(2)}, u32[]{:S(2)}) collective-permute-start(f32[8,96,256]{2,1,0:T(8,128)} %get-tuple-element.58), channel_id=1, source_target_pairs={{0,96},{16,112},{32,0},{48,16},{64,32},{80,48},{96,64},{112,80},{1... | collective-permute-start | bytes 2359304 | tf_op jit(solution)/shard_map/ppermute | solution.py:25
  105.2 32.6 %collective-permute-start.6 = (f32[8,96,256]{2,1,0:T(8,128)}, f32[8,96,256]{2,1,0:T(8,128)S(1)}, u32[]{:S(2)}, u32[]{:S(2)}) collective-permute-start(f32[8,96,256]{2,1,0:T(8,128)} %get-tuple-element.54), channel_id=1, source_target_pairs={{0,96},{16,112},{32,0},{48,16},{64,32},{80,48},{96,64},{112,80},{1... | collective-permute-start | bytes 2359304 | tf_op jit(solution)/shard_map/ppermute | solution.py:25
  120.5 18.1 %collective-permute-start.5 = (f32[8,96,256]{2,1,0:T(8,128)S(1)}, f32[8,96,256]{2,1,0:T(8,128)S(1)}, u32[]{:S(2)}, u32[]{:S(2)}) collective-permute-start(f32[8,96,256]{2,1,0:T(8,128)S(1)} %add.52), channel_id=1, source_target_pairs={{0,32},{16,48},{32,64},{48,80},{64,96},{80,112},{96,0},{112,16},{1... | collective-permute-start | bytes 2359304 | tf_op jit(solution)/shard_map/ppermute | solution.py:25
  120.5 34.9 %collective-permute-start.7 = (f32[8,96,256]{2,1,0:T(8,128)S(1)}, f32[8,96,256]{2,1,0:T(8,128)S(1)}, u32[]{:S(2)}, u32[]{:S(2)}) collective-permute-start(f32[8,96,256]{2,1,0:T(8,128)S(1)} %get-tuple-element.56), channel_id=1, source_target_pairs={{0,32},{16,48},{32,64},{48,80},{64,96},{80,112},{96,0},{112,16},{1... | collective-permute-start | bytes 2359304 | tf_op jit(solution)/shard_map/ppermute | solution.py:25
  123.0 32.4 %collective-permute-start.9 = (f32[8,96,256]{2,1,0:T(8,128)S(1)}, f32[8,96,256]{2,1,0:T(8,128)S(1)}, u32[]{:S(2)}, u32[]{:S(2)}) collective-permute-start(f32[8,96,256]{2,1,0:T(8,128)S(1)} %add.56), channel_id=1, source_target_pairs={{0,96},{16,112},{32,0},{48,16},{64,32},{80,48},{96,64},{112,80},{1... | collective-permute-start | bytes 2359304 | tf_op jit(solution)/shard_map/ppermute | solution.py:25
  138.6 17.9 %copy-start.10 = (f32[4,32,16,256]{3,2,1,0:T(8,128)S(1)}, f32[4,32,16,256]{3,2,1,0:T(8,128)}, u32[]{:S(2)}) copy-start(f32[4,32,16,256]{3,2,1,0:T(8,128)} %get-tuple-element.59) | copy-start | bytes 6291460
  158.3 9.5 %copy-start.7 = (f32[8,64,128]{2,1,0:T(8,128)S(1)}, f32[8,64,128]{2,1,0:T(8,128)}, u32[]{:S(2)}) copy-start(f32[8,64,128]{2,1,0:T(8,128)} %constant.52.clone.w_ref) | copy-start | bytes 786436
  162.8 32.9 %all-to-all-start.2 = ((f32[4,32,16,256]{3,2,1,0:T(8,128)}), f32[4,32,16,256]{3,2,1,0:T(8,128)S(1)}, u32[]{:S(2)}, u32[]{:S(2)}) async-start(f32[4,32,16,256]{3,2,1,0:T(8,128)} %add.58), calls=%async_computation.2 | async-start | bytes 4194304 | tf_op jit(solution)/shard_map/all_to_all | solution.py:35
  166.5 17.8 %collective-permute-start.17 = (f32[8,96,256]{2,1,0:T(8,128)}, f32[8,96,256]{2,1,0:T(8,128)S(1)}, u32[]{:S(2)}, u32[]{:S(2)}) collective-permute-start(f32[8,96,256]{2,1,0:T(8,128)} %add_add_fusion), channel_id=1, source_target_pairs={{0,16},{16,0},{32,48},{48,32},{64,80},{80,64},{96,112},{112,96},{1... | collective-permute-start | bytes 2359304 | tf_op jit(solution)/shard_map/ppermute | solution.py:27
  167.8 16.5 %copy-start.9 = (f32[8,96,256]{2,1,0:T(8,128)S(1)}, f32[8,96,256]{2,1,0:T(8,128)}, u32[]{:S(2)}) copy-start(f32[8,96,256]{2,1,0:T(8,128)} %add_add_fusion.1) | copy-start | bytes 2359300
  174.7 9.3 %collective-permute-start.11 = (f32[8,48,256]{2,1,0:T(8,128)S(1)}, f32[8,48,256]{2,1,0:T(8,128)S(1)}, u32[]{:S(2)}, u32[]{:S(2)}) collective-permute-start(f32[8,48,256]{2,1,0:T(8,128)S(1)} %get-tuple-element.66), channel_id=1, source_target_pairs={{0,32},{16,48},{32,64},{48,80},{64,96},{80,112},{96,0},{112,16},{1... | collective-permute-start | bytes 1179656 | tf_op jit(solution)/shard_map/ppermute | solution.py:25
  176.1 12.8 %collective-permute-start.15 = (f32[8,48,256]{2,1,0:T(8,128)S(1)}, f32[8,48,256]{2,1,0:T(8,128)S(1)}, u32[]{:S(2)}, u32[]{:S(2)}) collective-permute-start(f32[8,48,256]{2,1,0:T(8,128)S(1)} %get-tuple-element.71), channel_id=1, source_target_pairs={{0,96},{16,112},{32,0},{48,16},{64,32},{80,48},{96,64},{112,80},{1... | collective-permute-start | bytes 1179656 | tf_op jit(solution)/shard_map/ppermute | solution.py:25
  177.6 14.6 %collective-permute-start.13 = (f32[8,48,256]{2,1,0:T(8,128)S(1)}, f32[8,48,256]{2,1,0:T(8,128)S(1)}, u32[]{:S(2)}, u32[]{:S(2)}) collective-permute-start(f32[8,48,256]{2,1,0:T(8,128)S(1)} %get-tuple-element.67), channel_id=1, source_target_pairs={{0,96},{16,112},{32,0},{48,16},{64,32},{80,48},{96,64},{112,80},{1... | collective-permute-start | bytes 1179656 | tf_op jit(solution)/shard_map/ppermute | solution.py:25
  184.1 9.1 %collective-permute-start.12 = (f32[8,48,256]{2,1,0:T(8,128)S(1)}, f32[8,48,256]{2,1,0:T(8,128)S(1)}, u32[]{:S(2)}, u32[]{:S(2)}) collective-permute-start(f32[8,48,256]{2,1,0:T(8,128)S(1)} %add.59), channel_id=1, source_target_pairs={{0,32},{16,48},{32,64},{48,80},{64,96},{80,112},{96,0},{112,16},{1... | collective-permute-start | bytes 1179656 | tf_op jit(solution)/shard_map/ppermute | solution.py:25
  185.3 17.1 %collective-permute-start.18 = (f32[8,96,256]{2,1,0:T(8,128)}, f32[8,96,256]{2,1,0:T(8,128)}, u32[]{:S(2)}, u32[]{:S(2)}) collective-permute-start(f32[8,96,256]{2,1,0:T(8,128)} %add.65), channel_id=1, source_target_pairs={{0,2},{1,3},{2,0},{3,1},{4,6},{5,7},{6,4},{7,5},{8,10},{9,11},{10,... | collective-permute-start | bytes 2359304 | tf_op jit(solution)/shard_map/ppermute | solution.py:29
  187.7 13.3 %collective-permute-start.14 = (f32[8,48,256]{2,1,0:T(8,128)S(1)}, f32[8,48,256]{2,1,0:T(8,128)S(1)}, u32[]{:S(2)}, u32[]{:S(2)}) collective-permute-start(f32[8,48,256]{2,1,0:T(8,128)S(1)} %get-tuple-element.69), channel_id=1, source_target_pairs={{0,32},{16,48},{32,64},{48,80},{64,96},{80,112},{96,0},{112,16},{1... | collective-permute-start | bytes 1179656 | tf_op jit(solution)/shard_map/ppermute | solution.py:25
  189.8 11.5 %collective-permute-start.16 = (f32[8,48,256]{2,1,0:T(8,128)}, f32[8,48,256]{2,1,0:T(8,128)}, u32[]{:S(2)}, u32[]{:S(2)}) collective-permute-start(f32[8,48,256]{2,1,0:T(8,128)} %add.63), channel_id=1, source_target_pairs={{0,96},{16,112},{32,0},{48,16},{64,32},{80,48},{96,64},{112,80},{1... | collective-permute-start | bytes 1179656 | tf_op jit(solution)/shard_map/ppermute | solution.py:25
  192.2 18.4 %collective-permute-start.22 = (f32[8,96,256]{2,1,0:T(8,128)}, f32[8,96,256]{2,1,0:T(8,128)}, u32[]{:S(2)}, u32[]{:S(2)}) collective-permute-start(f32[8,96,256]{2,1,0:T(8,128)} %add.65), channel_id=1, source_target_pairs={{0,4},{4,8},{8,12},{12,0},{1,5},{5,9},{9,13},{13,1},{2,6},{6,10},{... | collective-permute-start | bytes 2359304 | tf_op jit(solution)/shard_map/ppermute | solution.py:23
  193.3 19.2 %collective-permute-start.24 = (f32[8,96,256]{2,1,0:T(8,128)}, f32[8,96,256]{2,1,0:T(8,128)}, u32[]{:S(2)}, u32[]{:S(2)}) collective-permute-start(f32[8,96,256]{2,1,0:T(8,128)} %add.65), channel_id=1, source_target_pairs={{0,12},{4,0},{8,4},{12,8},{1,13},{5,1},{9,5},{13,9},{2,14},{6,2},{... | collective-permute-start | bytes 2359304 | tf_op jit(solution)/shard_map/ppermute | solution.py:23
  196.8 11.1 %all-to-all-start.3 = ((f32[4,8,16,256]{3,2,1,0:T(8,128)}), f32[4,8,16,256]{3,2,1,0:T(8,128)S(1)}, u32[]{:S(2)}, u32[]{:S(2)}) async-start(f32[4,8,16,256]{3,2,1,0:T(8,128)} %bitcast.8), calls=%async_computation.3 | async-start | bytes 1048576 | tf_op jit(solution)/shard_map/all_to_all | solution.py:37
  202.4 14.5 %collective-permute-start.19 = (f32[8,48,256]{2,1,0:T(8,128)S(1)}, f32[8,48,256]{2,1,0:T(8,128)}, u32[]{:S(2)}, u32[]{:S(2)}) collective-permute-start(f32[8,48,256]{2,1,0:T(8,128)S(1)} %add_add_fusion.2), channel_id=1, source_target_pairs={{0,16},{16,0},{32,48},{48,32},{64,80},{80,64},{96,112},{112,96},{1... | collective-permute-start | bytes 1179656 | tf_op jit(solution)/shard_map/ppermute | solution.py:27
  207.9 17.3 %collective-permute-start.20 = (f32[8,64,256]{2,1,0:T(8,128)S(1)}, f32[8,64,256]{2,1,0:T(8,128)S(1)}, u32[]{:S(2)}, u32[]{:S(2)}) collective-permute-start(f32[8,64,256]{2,1,0:T(8,128)S(1)} %bitcast.31), channel_id=1, source_target_pairs={{0,4},{4,8},{8,12},{12,0},{1,5},{5,9},{9,13},{13,1},{2,6},{6,10},{... | collective-permute-start | bytes 1572872 | tf_op jit(solution)/shard_map/ppermute | solution.py:23
  209.2 15.9 %collective-permute-start.21 = (f32[8,64,256]{2,1,0:T(8,128)S(1)}, f32[8,64,256]{2,1,0:T(8,128)S(1)}, u32[]{:S(2)}, u32[]{:S(2)}) collective-permute-start(f32[8,64,256]{2,1,0:T(8,128)S(1)} %bitcast.32), channel_id=1, source_target_pairs={{0,12},{4,0},{8,4},{12,8},{1,13},{5,1},{9,5},{13,9},{2,14},{6,2},{... | collective-permute-start | bytes 1572872 | tf_op jit(solution)/shard_map/ppermute | solution.py:23
  212.4 11.9 %collective-permute-start.23 = (f32[4,96,256]{2,1,0:T(8,128)}, f32[4,96,256]{2,1,0:T(8,128)S(1)}, u32[]{:S(2)}, u32[]{:S(2)}) collective-permute-start(f32[4,96,256]{2,1,0:T(8,128)} %slice.24), channel_id=1, source_target_pairs={{0,4},{4,8},{8,12},{12,0},{1,5},{5,9},{9,13},{13,1},{2,6},{6,10},{... | collective-permute-start | bytes 1179656 | tf_op jit(solution)/shard_map/ppermute | solution.py:23
  214.2 10.9 %collective-permute-start.25 = (f32[4,96,256]{2,1,0:T(8,128)}, f32[4,96,256]{2,1,0:T(8,128)}, u32[]{:S(2)}, u32[]{:S(2)}) collective-permute-start(f32[4,96,256]{2,1,0:T(8,128)} %slice.25), channel_id=1, source_target_pairs={{0,12},{4,0},{8,4},{12,8},{1,13},{5,1},{9,5},{13,9},{2,14},{6,2},{... | collective-permute-start | bytes 1179656 | tf_op jit(solution)/shard_map/ppermute | solution.py:23
  216.9 13.7 %collective-permute-start.29 = (f32[8,64,256]{2,1,0:T(8,128)S(1)}, f32[8,64,256]{2,1,0:T(8,128)S(1)}, u32[]{:S(2)}, u32[]{:S(2)}) collective-permute-start(f32[8,64,256]{2,1,0:T(8,128)S(1)} %bitcast.33), channel_id=1, source_target_pairs={{0,2},{1,3},{2,0},{3,1},{4,6},{5,7},{6,4},{7,5},{8,10},{9,11},{10,... | collective-permute-start | bytes 1572872 | tf_op jit(solution)/shard_map/ppermute | solution.py:29
  224.3 32.2 %copy-start.1 = (f32[4,96,256]{2,1,0:T(8,128)}, f32[4,96,256]{2,1,0:T(8,128)S(1)}, u32[]{:S(2)}) copy-start(f32[4,96,256]{2,1,0:T(8,128)S(1)} %collective-permute-done.23.refs_4_) | copy-start | bytes 1179652
  225.1 31.4 %collective-permute-start.27 = (f32[8,96,256]{2,1,0:T(8,128)S(1)}, f32[8,96,256]{2,1,0:T(8,128)S(1)}, u32[]{:S(2)}, u32[]{:S(2)}) collective-permute-start(f32[8,96,256]{2,1,0:T(8,128)S(1)} %maximum_select_fusion), channel_id=1, source_target_pairs={{0,4},{4,8},{8,12},{12,0},{1,5},{5,9},{9,13},{13,1},{2,6},{6,10},{... | collective-permute-start | bytes 2359304 | tf_op jit(solution)/shard_map/ppermute | solution.py:23
  226.3 30.7 %collective-permute-start.28 = (f32[8,96,256]{2,1,0:T(8,128)S(1)}, f32[8,96,256]{2,1,0:T(8,128)S(1)}, u32[]{:S(2)}, u32[]{:S(2)}) collective-permute-start(f32[8,96,256]{2,1,0:T(8,128)S(1)} %maximum_select_fusion), channel_id=1, source_target_pairs={{0,12},{4,0},{8,4},{12,8},{1,13},{5,1},{9,5},{13,9},{2,14},{6,2},{... | collective-permute-start | bytes 2359304 | tf_op jit(solution)/shard_map/ppermute | solution.py:23
  228.0 29.1 %collective-permute-start.30 = (f32[8,96,256]{2,1,0:T(8,128)S(1)}, f32[8,96,256]{2,1,0:T(8,128)}, u32[]{:S(2)}, u32[]{:S(2)}) collective-permute-start(f32[8,96,256]{2,1,0:T(8,128)S(1)} %maximum_select_fusion), channel_id=1, source_target_pairs={{0,2},{1,3},{2,0},{3,1},{4,6},{5,7},{6,4},{7,5},{8,10},{9,11},{10,... | collective-permute-start | bytes 2359304 | tf_op jit(solution)/shard_map/ppermute | solution.py:29
  230.5 15.5 %collective-permute-start.31 = (f32[4,64,256]{2,1,0:T(8,128)S(1)}, f32[4,64,256]{2,1,0:T(8,128)S(1)}, u32[]{:S(2)}, u32[]{:S(2)}) collective-permute-start(f32[4,64,256]{2,1,0:T(8,128)S(1)} %slice.20), channel_id=1, source_target_pairs={{0,4},{4,8},{8,12},{12,0},{1,5},{5,9},{9,13},{13,1},{2,6},{6,10},{... | collective-permute-start | bytes 786440 | tf_op jit(solution)/shard_map/ppermute | solution.py:23
  230.6 25.1 %collective-permute-start.32 = (f32[4,64,256]{2,1,0:T(8,128)S(1)}, f32[4,64,256]{2,1,0:T(8,128)S(1)}, u32[]{:S(2)}, u32[]{:S(2)}) collective-permute-start(f32[4,64,256]{2,1,0:T(8,128)S(1)} %slice.21), channel_id=1, source_target_pairs={{0,12},{4,0},{8,4},{12,8},{1,13},{5,1},{9,5},{13,9},{2,14},{6,2},{... | collective-permute-start | bytes 786440 | tf_op jit(solution)/shard_map/ppermute | solution.py:23
  246.0 15.0 %copy-start.3 = (f32[4,64,256]{2,1,0:T(8,128)}, f32[4,64,256]{2,1,0:T(8,128)S(1)}, u32[]{:S(2)}) copy-start(f32[4,64,256]{2,1,0:T(8,128)S(1)} %collective-permute-done.31.refs_2_) | copy-start | bytes 786436
  246.0 12.0 %collective-permute-start.36 = (f32[8,96,256]{2,1,0:T(8,128)}, f32[8,96,256]{2,1,0:T(8,128)}, u32[]{:S(2)}, u32[]{:S(2)}) collective-permute-start(f32[8,96,256]{2,1,0:T(8,128)} %add.65), channel_id=1, source_target_pairs={{0,1},{1,0},{2,3},{3,2},{4,5},{5,4},{6,7},{7,6},{8,9},{9,8},{10,11... | collective-permute-start | bytes 2359304 | tf_op jit(solution)/shard_map/ppermute | solution.py:30
  255.7 0.7 copy-start.5
  256.4 3.5 %collective-permute-start.37 = (f32[8,96,256]{2,1,0:T(8,128)}, f32[8,96,256]{2,1,0:T(8,128)S(1)}, u32[]{:S(2)}, u32[]{:S(2)}) collective-permute-start(f32[8,96,256]{2,1,0:T(8,128)} %collective-permute-done.18), channel_id=1, source_target_pairs={{0,1},{1,0},{2,3},{3,2},{4,5},{5,4},{6,7},{7,6},{8,9},{9,8},{10,11... | collective-permute-start | bytes 2359304 | tf_op jit(solution)/shard_map/ppermute | solution.py:30
  256.5 4.5 %copy-start.11 = (f32[8,96,256]{2,1,0:T(8,128)}, f32[8,96,256]{2,1,0:T(8,128)S(1)}, u32[]{:S(2)}) copy-start(f32[8,96,256]{2,1,0:T(8,128)S(1)} %collective-permute-done.27) | copy-start | bytes 2359300
  256.5 4.5 %collective-permute-start.34 = (f32[8,64,256]{2,1,0:T(8,128)S(1)}, f32[8,64,256]{2,1,0:T(8,128)S(1)}, u32[]{:S(2)}, u32[]{:S(2)}) collective-permute-start(f32[8,64,256]{2,1,0:T(8,128)S(1)} %bitcast.34), channel_id=1, source_target_pairs={{0,1},{1,0},{2,3},{3,2},{4,5},{5,4},{6,7},{7,6},{8,9},{9,8},{10,11... | collective-permute-start | bytes 1572872 | tf_op jit(solution)/shard_map/ppermute | solution.py:30
  257.0 4.0 %copy-start.12 = (f32[8,96,256]{2,1,0:T(8,128)}, f32[8,96,256]{2,1,0:T(8,128)S(1)}, u32[]{:S(2)}) copy-start(f32[8,96,256]{2,1,0:T(8,128)S(1)} %collective-permute-done.28) | copy-start | bytes 2359300
  257.0 7.1 %collective-permute-start.26 = (f32[8,96,256]{2,1,0:T(8,128)S(1)}, f32[8,96,256]{2,1,0:T(8,128)}, u32[]{:S(2)}, u32[]{:S(2)}) collective-permute-start(f32[8,96,256]{2,1,0:T(8,128)S(1)} %maximum_select_fusion), channel_id=1, source_target_pairs={{0,1},{1,0},{2,3},{3,2},{4,5},{5,4},{6,7},{7,6},{8,9},{9,8},{10,11... | collective-permute-start | bytes 2359304 | tf_op jit(solution)/shard_map/ppermute | solution.py:30
  257.1 7.0 %collective-permute-start.33 = (f32[8,96,256]{2,1,0:T(8,128)}, f32[8,96,256]{2,1,0:T(8,128)}, u32[]{:S(2)}, u32[]{:S(2)}) collective-permute-start(f32[8,96,256]{2,1,0:T(8,128)} %collective-permute-done.30), channel_id=1, source_target_pairs={{0,1},{1,0},{2,3},{3,2},{4,5},{5,4},{6,7},{7,6},{8,9},{9,8},{10,11... | collective-permute-start | bytes 2359304 | tf_op jit(solution)/shard_map/ppermute | solution.py:30
  258.0 6.1 %collective-permute-start.35 = (f32[8,64,256]{2,1,0:T(8,128)S(1)}, f32[8,64,256]{2,1,0:T(8,128)}, u32[]{:S(2)}, u32[]{:S(2)}) collective-permute-start(f32[8,64,256]{2,1,0:T(8,128)S(1)} %collective-permute-done.29), channel_id=1, source_target_pairs={{0,1},{1,0},{2,3},{3,2},{4,5},{5,4},{6,7},{7,6},{8,9},{9,8},{10,11... | collective-permute-start | bytes 1572872 | tf_op jit(solution)/shard_map/ppermute | solution.py:30
  259.9 1.1 copy-start.13
  259.9 14.7 %collective-permute-start.38 = (f32[4,96,256]{2,1,0:T(8,128)}, f32[4,96,256]{2,1,0:T(8,128)}, u32[]{:S(2)}, u32[]{:S(2)}) collective-permute-start(f32[4,96,256]{2,1,0:T(8,128)} %slice.22), channel_id=1, source_target_pairs={{0,4},{4,8},{8,12},{12,0},{1,5},{5,9},{9,13},{13,1},{2,6},{6,10},{... | collective-permute-start | bytes 1179656 | tf_op jit(solution)/shard_map/ppermute | solution.py:23
  261.0 13.6 %collective-permute-start.39 = (f32[4,96,256]{2,1,0:T(8,128)}, f32[4,96,256]{2,1,0:T(8,128)}, u32[]{:S(2)}, u32[]{:S(2)}) collective-permute-start(f32[4,96,256]{2,1,0:T(8,128)} %slice.23), channel_id=1, source_target_pairs={{0,12},{4,0},{8,4},{12,8},{1,13},{5,1},{9,5},{13,9},{2,14},{6,2},{... | collective-permute-start | bytes 1179656 | tf_op jit(solution)/shard_map/ppermute | solution.py:23
  264.1 10.5 %copy-start.2 = (f32[4,96,256]{2,1,0:T(8,128)S(1)}, f32[4,96,256]{2,1,0:T(8,128)}, u32[]{:S(2)}) copy-start(f32[4,96,256]{2,1,0:T(8,128)} %copy-done.1) | copy-start | bytes 1179652
  264.1 10.5 %copy-start.4 = (f32[4,64,256]{2,1,0:T(8,128)S(1)}, f32[4,64,256]{2,1,0:T(8,128)}, u32[]{:S(2)}) copy-start(f32[4,64,256]{2,1,0:T(8,128)} %copy-done.3) | copy-start | bytes 786436
  264.1 10.5 %copy-start.6 = (f32[4,64,256]{2,1,0:T(8,128)S(1)}, f32[4,64,256]{2,1,0:T(8,128)}, u32[]{:S(2)}) copy-start(f32[4,64,256]{2,1,0:T(8,128)} %copy-done.5) | copy-start | bytes 786436

commit v5 on v4

--- a/solution.py
+++ b/solution.py
@@ -145,13 +145,14 @@
     w = w_ref[0]
     wh = w.astype(jnp.bfloat16)
     wl = (w - wh.astype(jnp.float32)).astype(jnp.bfloat16)
-    wcat = jnp.concatenate([wh, wh, wl], axis=1)
+    both = jnp.concatenate([wh, wl], axis=0)
     for s in range(rows):
         x = samples(s)
         xh = x.astype(jnp.bfloat16)
         xl = (x - xh.astype(jnp.float32)).astype(jnp.bfloat16)
-        xcat = jnp.concatenate([xh, xl, xh], axis=0)
-        store(s, jnp.dot(wcat, xcat, preferred_element_type=jnp.float32))
+        high = jnp.dot(both, xh, preferred_element_type=jnp.float32)
+        low = jnp.dot(wh, xl, preferred_element_type=jnp.float32)
+        store(s, high[:64] + (high[64:] + low))
 
 
 def dft_owner_kernel(rows, _, w_ref, x_ref, *outs):

time: 282 us -> 281 us (level)
  transfers between devices with their start and end apart: 44 -> 44, of which waited for: 19 -> 19; matrix products, arithmetic and copies ran while one was open for 6% -> 6% of each run, Pallas kernels for 17% -> 18%
where the time goes in v5:
time: 281 us; the launch traced here: 280 us
  waiting for transfers between devices  119 us (42%)
  starting transfers between devices  79.3 us (28%)
  Pallas kernels  62.8 us (22%)
  other arithmetic  11.8 us (4%)
  local copies, waits for them, and re-layouts  7.19 us (3%)
    ppermute x15, waiting for transfers between devices, shift(): return lax.ppermute(x, 'freq', [(i, (i + 2 * by) % 8) for i in range(8)])  86.8 us
    pallas_call x11, Pallas kernels, call(): pl.pallas_call(kernel, grid_spec=pltpu.PrefetchScalarGridSpec(num_scalar_...  60.8 us
    ppermute x15, starting transfers between devices, shift(): return lax.ppermute(x, 'freq', [(i, (i + 2 * by) % 8) for i in range(8)])  20.2 us
    ppermute x12, waiting for transfers between devices, shift(): return lax.ppermute(x, 'row', [(i, (i + by) % 4) for i in range(4)])  17.1 us
    ppermute x12, starting transfers between devices, shift(): return lax.ppermute(x, 'row', [(i, (i + by) % 4) for i in range(4)])  17 us
    all_to_all x3, starting transfers between devices, exchange(): return lax.all_to_all(x, 'row', split_axis=0, concat_axis=0, tiled=True)  15.1 us
    ppermute x6, starting transfers between devices, shift(): return lax.ppermute(x, 'col', [(i, i ^ 1) for i in range(4)])  11.2 us
    ppermute x3, starting transfers between devices, shift(): return lax.ppermute(x, 'col', [(i, i ^ 2) for i in range(4)])  7.31 us
  transfers between devices with their start and end apart: 44, of which 19 were waited for; matrix products, arithmetic and copies ran while one was open for 6% of the time, Pallas kernels for 18%

profile of v5, /device:TPU:1, one launch (start us, length us, event | category | flops | bytes accessed | tf_op | source)
XLA Modules:
  0.0 280.4 jit_solution(8825065569503982428)
XLA Ops:
  0.1 5.8 %shard_map.46 = f32[4,16,96,256]{3,2,1,0:T(8,128)} custom-call(s32[4]{0:T(128)S(1)} %pad_add_fusion.1.index._, f32[16,4,256,256]{3,2,1,0:T(8,128)} %bitcast.41), custom_call_target="tpu_custom_call" | custom-call | bytes 18000000 | tf_op jit(solution)/shard_map/pallas_call | solution.py:49
  5.9 5.9 %all-to-all-start = ((f32[4,16,96,256]{3,2,1,0:T(8,128)}), f32[4,16,96,256]{3,2,1,0:T(8,128)}, u32[]{:S(2)}, u32[]{:S(2)}) async-start(f32[4,16,96,256]{3,2,1,0:T(8,128)} %shard_map.46), calls=%async_computation | async-start | bytes 12582912 | tf_op jit(solution)/shard_map/all_to_all | solution.py:35
  11.7 3.4 %shard_map.52 = f32[4,16,48,256]{3,2,1,0:T(8,128)} custom-call(s32[4]{0:T(128)S(1)} %pad_add_fusion.1.index._, f32[16,4,256,256]{3,2,1,0:T(8,128)} %bitcast.42), custom_call_target="tpu_custom_call" | custom-call | bytes 10800000 | tf_op jit(solution)/shard_map/pallas_call | solution.py:49
  15.2 1.6 collective-permute-start.3
  16.7 2.8 shard_map.47
  19.5 1.4 collective-permute-start
  20.9 2.8 shard_map.48
  23.7 2.7 collective-permute-start.1
  26.4 2.8 shard_map.49
  29.2 1.1 collective-permute-start.2
  30.3 3.4 %shard_map.51.joined_ref = f32[4,2,16,48,256]{4,3,2,1,0:T(8,128)} custom-call(s32[4]{0:T(128)S(1)} %pad_add_fusion.1.index._, f32[16,4,256,256]{3,2,1,0:T(8,128)} %bitcast.46), custom_call_target="tpu_custom_call" | custom-call | bytes 10800000 | tf_op jit(solution)/shard_map/pallas_call | solution.py:49
  33.8 11.2 %collective-permute-done.refs_1_ = f32[16,4,16,256]{3,2,1,0:T(8,128)} collective-permute-done((f32[16,4,16,256]{3,2,1,0:T(8,128)}, f32[16,4,16,256]{3,2,1,0:T(8,128)}, u32[]{:S(2)}, u32[]{:S(2)}) %collective-permute-start) | collective-permute-done | bytes 1048608 | tf_op jit(solution)/shard_map/ppermute | solution.py:25
  44.9 23.6 %collective-permute-done.1.refs_2_ = f32[16,4,16,256]{3,2,1,0:T(8,128)} collective-permute-done((f32[16,4,16,256]{3,2,1,0:T(8,128)}, f32[16,4,16,256]{3,2,1,0:T(8,128)}, u32[]{:S(2)}, u32[]{:S(2)}) %collective-permute-start.1) | collective-permute-done | bytes 1048608 | tf_op jit(solution)/shard_map/ppermute | solution.py:25
  68.5 2.7 collective-permute-done.2.refs_3_
  71.2 1.2 copy-done
  72.4 7.3 %shard_map.50 = (f32[4,32,16,256]{3,2,1,0:T(8,128)}, f32[4,32,16,256]{3,2,1,0:T(8,128)}) custom-call(s32[2]{0:T(128)S(1)} %pad_add_fusion.2._, f32[32,64,64]{2,1,0:T(8,128)S(1)} %copy-done, f32[16,4,256,256]{3,2,1,0:T(8,128)} %bitcast.47, f32[16,4,16,256]{3,2,1,0:T(8,128)} %collective-permute-done.refs_1_, ...), custom_call_target="tpu_custom_call" | custom-call | bytes 25200000 | tf_op jit(solution)/shard_map/pallas_call | solution.py:49
  79.7 4.6 %collective-permute-done.3.far_ref = f32[4,16,48,256]{3,2,1,0:T(8,128)S(1)} collective-permute-done((f32[4,16,48,256]{3,2,1,0:T(8,128)}, f32[4,16,48,256]{3,2,1,0:T(8,128)S(1)}, u32[]{:S(2)}, u32[]{:S(2)}) %collective-permute-start.3) | collective-permute-done | bytes 3145760 | tf_op jit(solution)/shard_map/ppermute | solution.py:27
  84.3 2.0 shard_map.54
  86.3 5.6 %all-to-all-start.1 = ((f32[4,2,16,48,256]{4,3,2,1,0:T(8,128)}), f32[4,2,16,48,256]{4,3,2,1,0:T(8,128)}, u32[]{:S(2)}, u32[]{:S(2)}) async-start(f32[4,2,16,48,256]{4,3,2,1,0:T(8,128)} %shard_map.54), calls=%async_computation.1 | async-start | bytes 12582912 | tf_op jit(solution)/shard_map/all_to_all | solution.py:35
  91.9 9.4 %shard_map.53 = (f32[8,96,256]{2,1,0:T(8,128)S(1)}, f32[8,96,256]{2,1,0:T(8,128)S(1)}, f32[8,96,256]{2,1,0:T(8,128)S(1)}, f32[8,96,256]{2,1,0:T(8,128)S(1)}, f32...) custom-call(s32[4]{0:T(128)S(1)} %pad_add_fusion.1.index._, ...), custom_call_target="tpu_custom_call" | custom-call | bytes 32400000 | tf_op jit(solution)/shard_map/pallas_call | solution.py:49
  101.3 1.6 collective-permute-start.4
  102.9 1.2 collective-permute-start.10
  104.2 1.5 collective-permute-start.8
  105.7 1.4 collective-permute-start.6
  107.1 13.7 %collective-permute-done.4 = f32[8,96,256]{2,1,0:T(8,128)S(1)} collective-permute-done((f32[8,96,256]{2,1,0:T(8,128)}, f32[8,96,256]{2,1,0:T(8,128)S(1)}, u32[]{:S(2)}, u32[]{:S(2)}) %collective-permute-start.4) | collective-permute-done | bytes 786464 | tf_op jit(solution)/shard_map/ppermute | solution.py:25
  121.0 1.2 collective-permute-start.7
  122.2 1.3 add.56
  123.5 2.1 collective-permute-start.9
  125.6 12.6 %collective-permute-done.6 = f32[8,96,256]{2,1,0:T(8,128)S(1)} collective-permute-done((f32[8,96,256]{2,1,0:T(8,128)}, f32[8,96,256]{2,1,0:T(8,128)S(1)}, u32[]{:S(2)}, u32[]{:S(2)}) %collective-permute-start.6) | collective-permute-done | bytes 786464 | tf_op jit(solution)/shard_map/ppermute | solution.py:25
  139.0 1.1 add_add_fusion.1
  140.1 15.8 %collective-permute-done.7 = f32[8,96,256]{2,1,0:T(8,128)S(1)} collective-permute-done((f32[8,96,256]{2,1,0:T(8,128)S(1)}, f32[8,96,256]{2,1,0:T(8,128)S(1)}, u32[]{:S(2)}, u32[]{:S(2)}) %collective-permute-start.7) | collective-permute-done | bytes 786464 | tf_op jit(solution)/shard_map/ppermute | solution.py:25
  157.0 1.8 add.58
  158.8 4.1 %all-to-all-done.1 = f32[4,2,16,48,256]{4,3,2,1,0:T(8,128)} async-done(((f32[4,2,16,48,256]{4,3,2,1,0:T(8,128)}), f32[4,2,16,48,256]{4,3,2,1,0:T(8,128)}, u32[]{:S(2)}, u32[]{:S(2)}) %all-to-all-start.1) | async-done | bytes 6291488 | tf_op jit(solution)/shard_map/all_to_all | solution.py:35
  162.8 3.6 %all-to-all-start.2 = ((f32[4,32,16,256]{3,2,1,0:T(8,128)}), f32[4,32,16,256]{3,2,1,0:T(8,128)S(1)}, u32[]{:S(2)}, u32[]{:S(2)}) async-start(f32[4,32,16,256]{3,2,1,0:T(8,128)} %add.58), calls=%async_computation.2 | async-start | bytes 4194304 | tf_op jit(solution)/shard_map/all_to_all | solution.py:35
  166.5 1.3 collective-permute-start.17
  167.8 6.9 %shard_map.55 = (f32[8,48,256]{2,1,0:T(8,128)S(1)}, f32[8,48,256]{2,1,0:T(8,128)S(1)}, f32[8,48,256]{2,1,0:T(8,128)S(1)}, f32[8,48,256]{2,1,0:T(8,128)S(1)}, f32...) custom-call(s32[4]{0:T(128)S(1)} %pad_add_fusion.1.index._, ...), custom_call_target="tpu_custom_call" | custom-call | bytes 25200000 | tf_op jit(solution)/shard_map/pallas_call | solution.py:49
  174.7 1.4 collective-permute-start.11
  176.0 1.5 collective-permute-start.15
  177.6 1.4 collective-permute-start.13
  179.0 5.1 %collective-permute-done.11 = f32[8,48,256]{2,1,0:T(8,128)S(1)} collective-permute-done((f32[8,48,256]{2,1,0:T(8,128)S(1)}, f32[8,48,256]{2,1,0:T(8,128)S(1)}, u32[]{:S(2)}, u32[]{:S(2)}) %collective-permute-start.11) | collective-permute-done | bytes 393248 | tf_op jit(solution)/shard_map/ppermute | solution.py:25
  185.2 2.4 collective-permute-start.18
  187.6 1.2 collective-permute-start.14
  189.7 1.5 collective-permute-start.16
  193.2 1.6 collective-permute-start.24
  196.7 4.1 %all-to-all-start.3 = ((f32[4,8,16,256]{3,2,1,0:T(8,128)}), f32[4,8,16,256]{3,2,1,0:T(8,128)S(1)}, u32[]{:S(2)}, u32[]{:S(2)}) async-start(f32[4,8,16,256]{3,2,1,0:T(8,128)} %bitcast.8), calls=%async_computation.3 | async-start | bytes 1048576 | tf_op jit(solution)/shard_map/all_to_all | solution.py:37
  201.2 1.1 add_add_fusion.2
  202.6 5.1 %all-to-all-done.3 = f32[4,8,16,256]{3,2,1,0:T(8,128)S(1)} async-done(((f32[4,8,16,256]{3,2,1,0:T(8,128)}), f32[4,8,16,256]{3,2,1,0:T(8,128)S(1)}, u32[]{:S(2)}, u32[]{:S(2)}) %all-to-all-start.3) | async-done | bytes 524320 | tf_op jit(solution)/shard_map/all_to_all | solution.py:37
  207.8 1.3 collective-permute-start.20
  209.2 1.4 collective-permute-start.21
  210.6 1.8 slice.24
  212.4 1.8 slice.25
  214.2 2.6 collective-permute-start.25
  216.8 2.4 collective-permute-start.29
  219.3 1.5 maximum_select_fusion
  220.7 3.5 %collective-permute-done.23.refs_4_ = f32[4,96,256]{2,1,0:T(8,128)S(1)} collective-permute-done((f32[4,96,256]{2,1,0:T(8,128)}, f32[4,96,256]{2,1,0:T(8,128)S(1)}, u32[]{:S(2)}, u32[]{:S(2)}) %collective-permute-start.23) | collective-permute-done | bytes 393248 | tf_op jit(solution)/shard_map/ppermute | solution.py:23
  225.1 1.2 collective-permute-start.27
  226.3 1.7 collective-permute-start.28
  228.0 2.4 collective-permute-start.30
  230.5 2.7 collective-permute-start.32
  233.3 12.7 %collective-permute-done.31.refs_2_ = f32[4,64,256]{2,1,0:T(8,128)S(1)} collective-permute-done((f32[4,64,256]{2,1,0:T(8,128)S(1)}, f32[4,64,256]{2,1,0:T(8,128)S(1)}, u32[]{:S(2)}, u32[]{:S(2)}) %collective-permute-start.31) | collective-permute-done | bytes 262176 | tf_op jit(solution)/shard_map/ppermute | solution.py:23
  246.0 9.7 %collective-permute-start.36 = (f32[8,96,256]{2,1,0:T(8,128)}, f32[8,96,256]{2,1,0:T(8,128)}, u32[]{:S(2)}, u32[]{:S(2)}) collective-permute-start(f32[8,96,256]{2,1,0:T(8,128)} %add.65), channel_id=1, source_target_pairs={{0,1},{1,0},{2,3},{3,2},{4,5},{5,4},{6,7},{7,6},{8,9},{9,8},{10,11... | collective-permute-start | bytes 2359304 | tf_op jit(solution)/shard_map/ppermute | solution.py:30
  261.0 3.0 %collective-permute-start.39 = (f32[4,96,256]{2,1,0:T(8,128)}, f32[4,96,256]{2,1,0:T(8,128)}, u32[]{:S(2)}, u32[]{:S(2)}) collective-permute-start(f32[4,96,256]{2,1,0:T(8,128)} %slice.23), channel_id=1, source_target_pairs={{0,12},{4,0},{8,4},{12,8},{1,13},{5,1},{9,5},{13,9},{2,14},{6,2},{... | collective-permute-start | bytes 1179656 | tf_op jit(solution)/shard_map/ppermute | solution.py:23
  264.1 10.5 %shard_map.56 = (f32[2,4,256,256]{3,2,1,0:T(8,128)}, f32[2,4,256,256]{3,2,1,0:T(8,128)}) custom-call(s32[2]{0:T(128)S(1)} %pad_add_fusion.index._, f32[2,4,96,256]{3,2,1,0:T(8,128)S(1)} %bitcast.29, f32[2,4,96,256]{3,2,1,0:T(8,128)} %bitcast.12.refs_1_, f32[2,4,96,256]{3,2,1,0:T(8,128)} %bitcast.13.refs_2_, f32[2,4,96,256]{3,2,1,0:T(8,128)} %bitcast.14.refs_3_, ...), custom_call_target="tpu_custom_call" | custom-call | bytes 39600000 | tf_op jit(solution)/shard_map/pallas_call | solution.py:49
  274.6 5.8 %shard_map.57 = f32[2,4,256,256]{3,2,1,0:T(8,128)} custom-call(s32[2]{0:T(128)S(1)} %pad_add_fusion.index._, f32[2,4,256,256]{3,2,1,0:T(8,128)} %get-tuple-element.85.total, f32[2,4,256,256]{3,2,1,0:T(8,128)} %get-tuple-element.86.kept, f32[4,96,256]{2,1,0:T(8,128)} %collective-permute-done.38.refs_0_, f32[4,96,256]{2,1,0:T(8,128)} %collective-permute-done.39.refs_1_, ...), custom_call_target="tpu_custom_call" | custom-call | bytes 14400000 | tf_op jit(solution)/shard_map/pallas_call | solution.py:49
  (88 shorter events, 15.2 us)
Async XLA Ops:
  5.9 78.4 %all-to-all-start = ((f32[4,16,96,256]{3,2,1,0:T(8,128)}), f32[4,16,96,256]{3,2,1,0:T(8,128)}, u32[]{:S(2)}, u32[]{:S(2)}) async-start(f32[4,16,96,256]{3,2,1,0:T(8,128)} %shard_map.46), calls=%async_computation | async-start | bytes 12582912 | tf_op jit(solution)/shard_map/all_to_all | solution.py:35
  15.2 69.1 %collective-permute-start.3 = (f32[4,16,48,256]{3,2,1,0:T(8,128)}, f32[4,16,48,256]{3,2,1,0:T(8,128)S(1)}, u32[]{:S(2)}, u32[]{:S(2)}) collective-permute-start(f32[4,16,48,256]{3,2,1,0:T(8,128)} %shard_map.52), channel_id=1, source_target_pairs={{0,16},{16,0},{32,48},{48,32},{64,80},{80,64},{96,112},{112,96},{1... | collective-permute-start | bytes 9437192 | tf_op jit(solution)/shard_map/ppermute | solution.py:27
  19.5 25.4 %collective-permute-start = (f32[16,4,16,256]{3,2,1,0:T(8,128)}, f32[16,4,16,256]{3,2,1,0:T(8,128)}, u32[]{:S(2)}, u32[]{:S(2)}) collective-permute-start(f32[16,4,16,256]{3,2,1,0:T(8,128)} %shard_map.47), channel_id=1, source_target_pairs={{0,32},{16,48},{32,64},{48,80},{64,96},{80,112},{96,0},{112,16},{1... | collective-permute-start | bytes 3145736 | tf_op jit(solution)/shard_map/ppermute | solution.py:25
  23.7 44.8 %collective-permute-start.1 = (f32[16,4,16,256]{3,2,1,0:T(8,128)}, f32[16,4,16,256]{3,2,1,0:T(8,128)}, u32[]{:S(2)}, u32[]{:S(2)}) collective-permute-start(f32[16,4,16,256]{3,2,1,0:T(8,128)} %shard_map.48), channel_id=1, source_target_pairs={{0,64},{16,80},{32,96},{48,112},{64,0},{80,16},{96,32},{112,48},{1... | collective-permute-start | bytes 3145736 | tf_op jit(solution)/shard_map/ppermute | solution.py:25
  29.2 42.0 %collective-permute-start.2 = (f32[16,4,16,256]{3,2,1,0:T(8,128)}, f32[16,4,16,256]{3,2,1,0:T(8,128)}, u32[]{:S(2)}, u32[]{:S(2)}) collective-permute-start(f32[16,4,16,256]{3,2,1,0:T(8,128)} %shard_map.49), channel_id=1, source_target_pairs={{0,96},{16,112},{32,0},{48,16},{64,32},{80,48},{96,64},{112,80},{1... | collective-permute-start | bytes 3145736 | tf_op jit(solution)/shard_map/ppermute | solution.py:25
  71.2 1.2 copy-start
  86.3 5.6 %copy-start.8 = (f32[8,64,64]{2,1,0:T(8,128)S(1)}, f32[8,64,64]{2,1,0:T(8,128)}, u32[]{:S(2)}) copy-start(f32[8,64,64]{2,1,0:T(8,128)} %constant.51.clone.w_ref) | copy-start | bytes 393220
  86.3 76.6 %all-to-all-start.1 = ((f32[4,2,16,48,256]{4,3,2,1,0:T(8,128)}), f32[4,2,16,48,256]{4,3,2,1,0:T(8,128)}, u32[]{:S(2)}, u32[]{:S(2)}) async-start(f32[4,2,16,48,256]{4,3,2,1,0:T(8,128)} %shard_map.54), calls=%async_computation.1 | async-start | bytes 12582912 | tf_op jit(solution)/shard_map/all_to_all | solution.py:35
  91.9 11.1 %copy-start.14 = (f32[4,32,16,256]{3,2,1,0:T(8,128)S(1)}, f32[4,32,16,256]{3,2,1,0:T(8,128)}, u32[]{:S(2)}) copy-start(f32[4,32,16,256]{3,2,1,0:T(8,128)} %get-tuple-element.60) | copy-start | bytes 6291460
  101.3 19.5 %collective-permute-start.4 = (f32[8,96,256]{2,1,0:T(8,128)}, f32[8,96,256]{2,1,0:T(8,128)S(1)}, u32[]{:S(2)}, u32[]{:S(2)}) collective-permute-start(f32[8,96,256]{2,1,0:T(8,128)} %get-tuple-element.53), channel_id=1, source_target_pairs={{0,32},{16,48},{32,64},{48,80},{64,96},{80,112},{96,0},{112,16},{1... | collective-permute-start | bytes 2359304 | tf_op jit(solution)/shard_map/ppermute | solution.py:25
  102.9 54.0 %collective-permute-start.10 = (f32[4,32,16,256]{3,2,1,0:T(8,128)S(1)}, f32[4,32,16,256]{3,2,1,0:T(8,128)S(1)}, u32[]{:S(2)}, u32[]{:S(2)}) collective-permute-start(f32[4,32,16,256]{3,2,1,0:T(8,128)S(1)} %copy-done.14), channel_id=1, source_target_pairs={{0,16},{16,0},{32,48},{48,32},{64,80},{80,64},{96,112},{112,96},{1... | collective-permute-start | bytes 6291464 | tf_op jit(solution)/shard_map/ppermute | solution.py:27
  104.2 18.0 %collective-permute-start.8 = (f32[8,96,256]{2,1,0:T(8,128)}, f32[8,96,256]{2,1,0:T(8,128)S(1)}, u32[]{:S(2)}, u32[]{:S(2)}) collective-permute-start(f32[8,96,256]{2,1,0:T(8,128)} %get-tuple-element.58), channel_id=1, source_target_pairs={{0,96},{16,112},{32,0},{48,16},{64,32},{80,48},{96,64},{112,80},{1... | collective-permute-start | bytes 2359304 | tf_op jit(solution)/shard_map/ppermute | solution.py:25
  105.7 32.6 %collective-permute-start.6 = (f32[8,96,256]{2,1,0:T(8,128)}, f32[8,96,256]{2,1,0:T(8,128)S(1)}, u32[]{:S(2)}, u32[]{:S(2)}) collective-permute-start(f32[8,96,256]{2,1,0:T(8,128)} %get-tuple-element.54), channel_id=1, source_target_pairs={{0,96},{16,112},{32,0},{48,16},{64,32},{80,48},{96,64},{112,80},{1... | collective-permute-start | bytes 2359304 | tf_op jit(solution)/shard_map/ppermute | solution.py:25
  120.9 18.1 %collective-permute-start.5 = (f32[8,96,256]{2,1,0:T(8,128)S(1)}, f32[8,96,256]{2,1,0:T(8,128)S(1)}, u32[]{:S(2)}, u32[]{:S(2)}) collective-permute-start(f32[8,96,256]{2,1,0:T(8,128)S(1)} %add.52), channel_id=1, source_target_pairs={{0,32},{16,48},{32,64},{48,80},{64,96},{80,112},{96,0},{112,16},{1... | collective-permute-start | bytes 2359304 | tf_op jit(solution)/shard_map/ppermute | solution.py:25
  121.0 34.9 %collective-permute-start.7 = (f32[8,96,256]{2,1,0:T(8,128)S(1)}, f32[8,96,256]{2,1,0:T(8,128)S(1)}, u32[]{:S(2)}, u32[]{:S(2)}) collective-permute-start(f32[8,96,256]{2,1,0:T(8,128)S(1)} %get-tuple-element.56), channel_id=1, source_target_pairs={{0,32},{16,48},{32,64},{48,80},{64,96},{80,112},{96,0},{112,16},{1... | collective-permute-start | bytes 2359304 | tf_op jit(solution)/shard_map/ppermute | solution.py:25
  123.5 32.4 %collective-permute-start.9 = (f32[8,96,256]{2,1,0:T(8,128)S(1)}, f32[8,96,256]{2,1,0:T(8,128)S(1)}, u32[]{:S(2)}, u32[]{:S(2)}) collective-permute-start(f32[8,96,256]{2,1,0:T(8,128)S(1)} %add.56), channel_id=1, source_target_pairs={{0,96},{16,112},{32,0},{48,16},{64,32},{80,48},{96,64},{112,80},{1... | collective-permute-start | bytes 2359304 | tf_op jit(solution)/shard_map/ppermute | solution.py:25
  139.0 17.9 %copy-start.10 = (f32[4,32,16,256]{3,2,1,0:T(8,128)S(1)}, f32[4,32,16,256]{3,2,1,0:T(8,128)}, u32[]{:S(2)}) copy-start(f32[4,32,16,256]{3,2,1,0:T(8,128)} %get-tuple-element.59) | copy-start | bytes 6291460
  158.7 9.0 %copy-start.7 = (f32[8,64,128]{2,1,0:T(8,128)S(1)}, f32[8,64,128]{2,1,0:T(8,128)}, u32[]{:S(2)}) copy-start(f32[8,64,128]{2,1,0:T(8,128)} %constant.52.clone.w_ref) | copy-start | bytes 786436
  162.8 32.8 %all-to-all-start.2 = ((f32[4,32,16,256]{3,2,1,0:T(8,128)}), f32[4,32,16,256]{3,2,1,0:T(8,128)S(1)}, u32[]{:S(2)}, u32[]{:S(2)}) async-start(f32[4,32,16,256]{3,2,1,0:T(8,128)} %add.58), calls=%async_computation.2 | async-start | bytes 4194304 | tf_op jit(solution)/shard_map/all_to_all | solution.py:35
  166.5 17.7 %collective-permute-start.17 = (f32[8,96,256]{2,1,0:T(8,128)}, f32[8,96,256]{2,1,0:T(8,128)S(1)}, u32[]{:S(2)}, u32[]{:S(2)}) collective-permute-start(f32[8,96,256]{2,1,0:T(8,128)} %add_add_fusion), channel_id=1, source_target_pairs={{0,16},{16,0},{32,48},{48,32},{64,80},{80,64},{96,112},{112,96},{1... | collective-permute-start | bytes 2359304 | tf_op jit(solution)/shard_map/ppermute | solution.py:27
  167.8 16.4 %copy-start.9 = (f32[8,96,256]{2,1,0:T(8,128)S(1)}, f32[8,96,256]{2,1,0:T(8,128)}, u32[]{:S(2)}) copy-start(f32[8,96,256]{2,1,0:T(8,128)} %add_add_fusion.1) | copy-start | bytes 2359300
  174.7 9.4 %collective-permute-start.11 = (f32[8,48,256]{2,1,0:T(8,128)S(1)}, f32[8,48,256]{2,1,0:T(8,128)S(1)}, u32[]{:S(2)}, u32[]{:S(2)}) collective-permute-start(f32[8,48,256]{2,1,0:T(8,128)S(1)} %get-tuple-element.66), channel_id=1, source_target_pairs={{0,32},{16,48},{32,64},{48,80},{64,96},{80,112},{96,0},{112,16},{1... | collective-permute-start | bytes 1179656 | tf_op jit(solution)/shard_map/ppermute | solution.py:25
  176.0 12.8 %collective-permute-start.15 = (f32[8,48,256]{2,1,0:T(8,128)S(1)}, f32[8,48,256]{2,1,0:T(8,128)S(1)}, u32[]{:S(2)}, u32[]{:S(2)}) collective-permute-start(f32[8,48,256]{2,1,0:T(8,128)S(1)} %get-tuple-element.71), channel_id=1, source_target_pairs={{0,96},{16,112},{32,0},{48,16},{64,32},{80,48},{96,64},{112,80},{1... | collective-permute-start | bytes 1179656 | tf_op jit(solution)/shard_map/ppermute | solution.py:25
  177.6 14.6 %collective-permute-start.13 = (f32[8,48,256]{2,1,0:T(8,128)S(1)}, f32[8,48,256]{2,1,0:T(8,128)S(1)}, u32[]{:S(2)}, u32[]{:S(2)}) collective-permute-start(f32[8,48,256]{2,1,0:T(8,128)S(1)} %get-tuple-element.67), channel_id=1, source_target_pairs={{0,96},{16,112},{32,0},{48,16},{64,32},{80,48},{96,64},{112,80},{1... | collective-permute-start | bytes 1179656 | tf_op jit(solution)/shard_map/ppermute | solution.py:25
  184.1 9.1 %collective-permute-start.12 = (f32[8,48,256]{2,1,0:T(8,128)S(1)}, f32[8,48,256]{2,1,0:T(8,128)S(1)}, u32[]{:S(2)}, u32[]{:S(2)}) collective-permute-start(f32[8,48,256]{2,1,0:T(8,128)S(1)} %add.59), channel_id=1, source_target_pairs={{0,32},{16,48},{32,64},{48,80},{64,96},{80,112},{96,0},{112,16},{1... | collective-permute-start | bytes 1179656 | tf_op jit(solution)/shard_map/ppermute | solution.py:25
  185.2 17.1 %collective-permute-start.18 = (f32[8,96,256]{2,1,0:T(8,128)}, f32[8,96,256]{2,1,0:T(8,128)}, u32[]{:S(2)}, u32[]{:S(2)}) collective-permute-start(f32[8,96,256]{2,1,0:T(8,128)} %add.65), channel_id=1, source_target_pairs={{0,2},{1,3},{2,0},{3,1},{4,6},{5,7},{6,4},{7,5},{8,10},{9,11},{10,... | collective-permute-start | bytes 2359304 | tf_op jit(solution)/shard_map/ppermute | solution.py:29
  187.6 13.4 %collective-permute-start.14 = (f32[8,48,256]{2,1,0:T(8,128)S(1)}, f32[8,48,256]{2,1,0:T(8,128)S(1)}, u32[]{:S(2)}, u32[]{:S(2)}) collective-permute-start(f32[8,48,256]{2,1,0:T(8,128)S(1)} %get-tuple-element.69), channel_id=1, source_target_pairs={{0,32},{16,48},{32,64},{48,80},{64,96},{80,112},{96,0},{112,16},{1... | collective-permute-start | bytes 1179656 | tf_op jit(solution)/shard_map/ppermute | solution.py:25
  189.7 11.5 %collective-permute-start.16 = (f32[8,48,256]{2,1,0:T(8,128)}, f32[8,48,256]{2,1,0:T(8,128)}, u32[]{:S(2)}, u32[]{:S(2)}) collective-permute-start(f32[8,48,256]{2,1,0:T(8,128)} %add.63), channel_id=1, source_target_pairs={{0,96},{16,112},{32,0},{48,16},{64,32},{80,48},{96,64},{112,80},{1... | collective-permute-start | bytes 1179656 | tf_op jit(solution)/shard_map/ppermute | solution.py:25
  192.1 18.4 %collective-permute-start.22 = (f32[8,96,256]{2,1,0:T(8,128)}, f32[8,96,256]{2,1,0:T(8,128)}, u32[]{:S(2)}, u32[]{:S(2)}) collective-permute-start(f32[8,96,256]{2,1,0:T(8,128)} %add.65), channel_id=1, source_target_pairs={{0,4},{4,8},{8,12},{12,0},{1,5},{5,9},{9,13},{13,1},{2,6},{6,10},{... | collective-permute-start | bytes 2359304 | tf_op jit(solution)/shard_map/ppermute | solution.py:23
  193.2 19.2 %collective-permute-start.24 = (f32[8,96,256]{2,1,0:T(8,128)}, f32[8,96,256]{2,1,0:T(8,128)}, u32[]{:S(2)}, u32[]{:S(2)}) collective-permute-start(f32[8,96,256]{2,1,0:T(8,128)} %add.65), channel_id=1, source_target_pairs={{0,12},{4,0},{8,4},{12,8},{1,13},{5,1},{9,5},{13,9},{2,14},{6,2},{... | collective-permute-start | bytes 2359304 | tf_op jit(solution)/shard_map/ppermute | solution.py:23
  196.7 11.1 %all-to-all-start.3 = ((f32[4,8,16,256]{3,2,1,0:T(8,128)}), f32[4,8,16,256]{3,2,1,0:T(8,128)S(1)}, u32[]{:S(2)}, u32[]{:S(2)}) async-start(f32[4,8,16,256]{3,2,1,0:T(8,128)} %bitcast.8), calls=%async_computation.3 | async-start | bytes 1048576 | tf_op jit(solution)/shard_map/all_to_all | solution.py:37
  202.3 14.5 %collective-permute-start.19 = (f32[8,48,256]{2,1,0:T(8,128)S(1)}, f32[8,48,256]{2,1,0:T(8,128)}, u32[]{:S(2)}, u32[]{:S(2)}) collective-permute-start(f32[8,48,256]{2,1,0:T(8,128)S(1)} %add_add_fusion.2), channel_id=1, source_target_pairs={{0,16},{16,0},{32,48},{48,32},{64,80},{80,64},{96,112},{112,96},{1... | collective-permute-start | bytes 1179656 | tf_op jit(solution)/shard_map/ppermute | solution.py:27
  207.8 17.3 %collective-permute-start.20 = (f32[8,64,256]{2,1,0:T(8,128)S(1)}, f32[8,64,256]{2,1,0:T(8,128)S(1)}, u32[]{:S(2)}, u32[]{:S(2)}) collective-permute-start(f32[8,64,256]{2,1,0:T(8,128)S(1)} %bitcast.31), channel_id=1, source_target_pairs={{0,4},{4,8},{8,12},{12,0},{1,5},{5,9},{9,13},{13,1},{2,6},{6,10},{... | collective-permute-start | bytes 1572872 | tf_op jit(solution)/shard_map/ppermute | solution.py:23
  209.2 15.9 %collective-permute-start.21 = (f32[8,64,256]{2,1,0:T(8,128)S(1)}, f32[8,64,256]{2,1,0:T(8,128)S(1)}, u32[]{:S(2)}, u32[]{:S(2)}) collective-permute-start(f32[8,64,256]{2,1,0:T(8,128)S(1)} %bitcast.32), channel_id=1, source_target_pairs={{0,12},{4,0},{8,4},{12,8},{1,13},{5,1},{9,5},{13,9},{2,14},{6,2},{... | collective-permute-start | bytes 1572872 | tf_op jit(solution)/shard_map/ppermute | solution.py:23
  212.3 11.9 %collective-permute-start.23 = (f32[4,96,256]{2,1,0:T(8,128)}, f32[4,96,256]{2,1,0:T(8,128)S(1)}, u32[]{:S(2)}, u32[]{:S(2)}) collective-permute-start(f32[4,96,256]{2,1,0:T(8,128)} %slice.24), channel_id=1, source_target_pairs={{0,4},{4,8},{8,12},{12,0},{1,5},{5,9},{9,13},{13,1},{2,6},{6,10},{... | collective-permute-start | bytes 1179656 | tf_op jit(solution)/shard_map/ppermute | solution.py:23
  214.2 10.9 %collective-permute-start.25 = (f32[4,96,256]{2,1,0:T(8,128)}, f32[4,96,256]{2,1,0:T(8,128)}, u32[]{:S(2)}, u32[]{:S(2)}) collective-permute-start(f32[4,96,256]{2,1,0:T(8,128)} %slice.25), channel_id=1, source_target_pairs={{0,12},{4,0},{8,4},{12,8},{1,13},{5,1},{9,5},{13,9},{2,14},{6,2},{... | collective-permute-start | bytes 1179656 | tf_op jit(solution)/shard_map/ppermute | solution.py:23
  216.8 13.7 %collective-permute-start.29 = (f32[8,64,256]{2,1,0:T(8,128)S(1)}, f32[8,64,256]{2,1,0:T(8,128)S(1)}, u32[]{:S(2)}, u32[]{:S(2)}) collective-permute-start(f32[8,64,256]{2,1,0:T(8,128)S(1)} %bitcast.33), channel_id=1, source_target_pairs={{0,2},{1,3},{2,0},{3,1},{4,6},{5,7},{6,4},{7,5},{8,10},{9,11},{10,... | collective-permute-start | bytes 1572872 | tf_op jit(solution)/shard_map/ppermute | solution.py:29
  224.3 32.2 %copy-start.1 = (f32[4,96,256]{2,1,0:T(8,128)}, f32[4,96,256]{2,1,0:T(8,128)S(1)}, u32[]{:S(2)}) copy-start(f32[4,96,256]{2,1,0:T(8,128)S(1)} %collective-permute-done.23.refs_4_) | copy-start | bytes 1179652
  225.1 31.4 %collective-permute-start.27 = (f32[8,96,256]{2,1,0:T(8,128)S(1)}, f32[8,96,256]{2,1,0:T(8,128)S(1)}, u32[]{:S(2)}, u32[]{:S(2)}) collective-permute-start(f32[8,96,256]{2,1,0:T(8,128)S(1)} %maximum_select_fusion), channel_id=1, source_target_pairs={{0,4},{4,8},{8,12},{12,0},{1,5},{5,9},{9,13},{13,1},{2,6},{6,10},{... | collective-permute-start | bytes 2359304 | tf_op jit(solution)/shard_map/ppermute | solution.py:23
  226.3 30.7 %collective-permute-start.28 = (f32[8,96,256]{2,1,0:T(8,128)S(1)}, f32[8,96,256]{2,1,0:T(8,128)S(1)}, u32[]{:S(2)}, u32[]{:S(2)}) collective-permute-start(f32[8,96,256]{2,1,0:T(8,128)S(1)} %maximum_select_fusion), channel_id=1, source_target_pairs={{0,12},{4,0},{8,4},{12,8},{1,13},{5,1},{9,5},{13,9},{2,14},{6,2},{... | collective-permute-start | bytes 2359304 | tf_op jit(solution)/shard_map/ppermute | solution.py:23
  228.0 29.1 %collective-permute-start.30 = (f32[8,96,256]{2,1,0:T(8,128)S(1)}, f32[8,96,256]{2,1,0:T(8,128)}, u32[]{:S(2)}, u32[]{:S(2)}) collective-permute-start(f32[8,96,256]{2,1,0:T(8,128)S(1)} %maximum_select_fusion), channel_id=1, source_target_pairs={{0,2},{1,3},{2,0},{3,1},{4,6},{5,7},{6,4},{7,5},{8,10},{9,11},{10,... | collective-permute-start | bytes 2359304 | tf_op jit(solution)/shard_map/ppermute | solution.py:29
  230.4 15.5 %collective-permute-start.31 = (f32[4,64,256]{2,1,0:T(8,128)S(1)}, f32[4,64,256]{2,1,0:T(8,128)S(1)}, u32[]{:S(2)}, u32[]{:S(2)}) collective-permute-start(f32[4,64,256]{2,1,0:T(8,128)S(1)} %slice.20), channel_id=1, source_target_pairs={{0,4},{4,8},{8,12},{12,0},{1,5},{5,9},{9,13},{13,1},{2,6},{6,10},{... | collective-permute-start | bytes 786440 | tf_op jit(solution)/shard_map/ppermute | solution.py:23
  230.5 25.1 %collective-permute-start.32 = (f32[4,64,256]{2,1,0:T(8,128)S(1)}, f32[4,64,256]{2,1,0:T(8,128)S(1)}, u32[]{:S(2)}, u32[]{:S(2)}) collective-permute-start(f32[4,64,256]{2,1,0:T(8,128)S(1)} %slice.21), channel_id=1, source_target_pairs={{0,12},{4,0},{8,4},{12,8},{1,13},{5,1},{9,5},{13,9},{2,14},{6,2},{... | collective-permute-start | bytes 786440 | tf_op jit(solution)/shard_map/ppermute | solution.py:23
  246.0 15.0 %copy-start.3 = (f32[4,64,256]{2,1,0:T(8,128)}, f32[4,64,256]{2,1,0:T(8,128)S(1)}, u32[]{:S(2)}) copy-start(f32[4,64,256]{2,1,0:T(8,128)S(1)} %collective-permute-done.31.refs_2_) | copy-start | bytes 786436
  246.0 12.0 %collective-permute-start.36 = (f32[8,96,256]{2,1,0:T(8,128)}, f32[8,96,256]{2,1,0:T(8,128)}, u32[]{:S(2)}, u32[]{:S(2)}) collective-permute-start(f32[8,96,256]{2,1,0:T(8,128)} %add.65), channel_id=1, source_target_pairs={{0,1},{1,0},{2,3},{3,2},{4,5},{5,4},{6,7},{7,6},{8,9},{9,8},{10,11... | collective-permute-start | bytes 2359304 | tf_op jit(solution)/shard_map/ppermute | solution.py:30
  255.7 0.7 copy-start.5
  256.4 3.5 %collective-permute-start.37 = (f32[8,96,256]{2,1,0:T(8,128)}, f32[8,96,256]{2,1,0:T(8,128)S(1)}, u32[]{:S(2)}, u32[]{:S(2)}) collective-permute-start(f32[8,96,256]{2,1,0:T(8,128)} %collective-permute-done.18), channel_id=1, source_target_pairs={{0,1},{1,0},{2,3},{3,2},{4,5},{5,4},{6,7},{7,6},{8,9},{9,8},{10,11... | collective-permute-start | bytes 2359304 | tf_op jit(solution)/shard_map/ppermute | solution.py:30
  256.4 4.5 %copy-start.11 = (f32[8,96,256]{2,1,0:T(8,128)}, f32[8,96,256]{2,1,0:T(8,128)S(1)}, u32[]{:S(2)}) copy-start(f32[8,96,256]{2,1,0:T(8,128)S(1)} %collective-permute-done.27) | copy-start | bytes 2359300
  256.4 4.5 %collective-permute-start.34 = (f32[8,64,256]{2,1,0:T(8,128)S(1)}, f32[8,64,256]{2,1,0:T(8,128)S(1)}, u32[]{:S(2)}, u32[]{:S(2)}) collective-permute-start(f32[8,64,256]{2,1,0:T(8,128)S(1)} %bitcast.34), channel_id=1, source_target_pairs={{0,1},{1,0},{2,3},{3,2},{4,5},{5,4},{6,7},{7,6},{8,9},{9,8},{10,11... | collective-permute-start | bytes 1572872 | tf_op jit(solution)/shard_map/ppermute | solution.py:30
  257.0 4.0 %copy-start.12 = (f32[8,96,256]{2,1,0:T(8,128)}, f32[8,96,256]{2,1,0:T(8,128)S(1)}, u32[]{:S(2)}) copy-start(f32[8,96,256]{2,1,0:T(8,128)S(1)} %collective-permute-done.28) | copy-start | bytes 2359300
  257.0 7.1 %collective-permute-start.26 = (f32[8,96,256]{2,1,0:T(8,128)S(1)}, f32[8,96,256]{2,1,0:T(8,128)}, u32[]{:S(2)}, u32[]{:S(2)}) collective-permute-start(f32[8,96,256]{2,1,0:T(8,128)S(1)} %maximum_select_fusion), channel_id=1, source_target_pairs={{0,1},{1,0},{2,3},{3,2},{4,5},{5,4},{6,7},{7,6},{8,9},{9,8},{10,11... | collective-permute-start | bytes 2359304 | tf_op jit(solution)/shard_map/ppermute | solution.py:30
  257.1 7.0 %collective-permute-start.33 = (f32[8,96,256]{2,1,0:T(8,128)}, f32[8,96,256]{2,1,0:T(8,128)}, u32[]{:S(2)}, u32[]{:S(2)}) collective-permute-start(f32[8,96,256]{2,1,0:T(8,128)} %collective-permute-done.30), channel_id=1, source_target_pairs={{0,1},{1,0},{2,3},{3,2},{4,5},{5,4},{6,7},{7,6},{8,9},{9,8},{10,11... | collective-permute-start | bytes 2359304 | tf_op jit(solution)/shard_map/ppermute | solution.py:30
  257.9 6.1 %collective-permute-start.35 = (f32[8,64,256]{2,1,0:T(8,128)S(1)}, f32[8,64,256]{2,1,0:T(8,128)}, u32[]{:S(2)}, u32[]{:S(2)}) collective-permute-start(f32[8,64,256]{2,1,0:T(8,128)S(1)} %collective-permute-done.29), channel_id=1, source_target_pairs={{0,1},{1,0},{2,3},{3,2},{4,5},{5,4},{6,7},{7,6},{8,9},{9,8},{10,11... | collective-permute-start | bytes 1572872 | tf_op jit(solution)/shard_map/ppermute | solution.py:30
  259.9 1.1 copy-start.13
  259.9 14.7 %collective-permute-start.38 = (f32[4,96,256]{2,1,0:T(8,128)}, f32[4,96,256]{2,1,0:T(8,128)}, u32[]{:S(2)}, u32[]{:S(2)}) collective-permute-start(f32[4,96,256]{2,1,0:T(8,128)} %slice.22), channel_id=1, source_target_pairs={{0,4},{4,8},{8,12},{12,0},{1,5},{5,9},{9,13},{13,1},{2,6},{6,10},{... | collective-permute-start | bytes 1179656 | tf_op jit(solution)/shard_map/ppermute | solution.py:23
  261.0 13.6 %collective-permute-start.39 = (f32[4,96,256]{2,1,0:T(8,128)}, f32[4,96,256]{2,1,0:T(8,128)}, u32[]{:S(2)}, u32[]{:S(2)}) collective-permute-start(f32[4,96,256]{2,1,0:T(8,128)} %slice.23), channel_id=1, source_target_pairs={{0,12},{4,0},{8,4},{12,8},{1,13},{5,1},{9,5},{13,9},{2,14},{6,2},{... | collective-permute-start | bytes 1179656 | tf_op jit(solution)/shard_map/ppermute | solution.py:23
  264.1 10.5 %copy-start.2 = (f32[4,96,256]{2,1,0:T(8,128)S(1)}, f32[4,96,256]{2,1,0:T(8,128)}, u32[]{:S(2)}) copy-start(f32[4,96,256]{2,1,0:T(8,128)} %copy-done.1) | copy-start | bytes 1179652
  264.1 10.5 %copy-start.4 = (f32[4,64,256]{2,1,0:T(8,128)S(1)}, f32[4,64,256]{2,1,0:T(8,128)}, u32[]{:S(2)}) copy-start(f32[4,64,256]{2,1,0:T(8,128)} %copy-done.3) | copy-start | bytes 786436
  264.1 10.5 %copy-start.6 = (f32[4,64,256]{2,1,0:T(8,128)S(1)}, f32[4,64,256]{2,1,0:T(8,128)}, u32[]{:S(2)}) copy-start(f32[4,64,256]{2,1,0:T(8,128)} %copy-done.5) | copy-start | bytes 786436
